TPU v7x, 32 devices: a whole 2x2x4 slice. The times are simulated.
32 devices in a mesh: dp: 8 (over y, x, core), ctx: 4 (over z).
Axes of the slice: x: 2, y: 2, z: 4, core: 2. Of those that a mesh axis runs over, the one named last changes fastest.
Arguments:
- tokens: bfloat16 [12288, 1536], P(('dp', 'ctx')), may hold values from -6 to 6
- seq_lens: int32 [8], P('dp'), may hold values from 1153 to 1536, as said below
- gain_in: bfloat16 [1536], P(('dp', 'ctx')), may hold values from 0.099609375 to 1.8984375
- w_query: bfloat16 [1536, 1536], P(('dp', 'ctx')), may hold values from -0.15625 to 0.15625
- w_key: bfloat16 [1536, 512], P(('dp', 'ctx')), may hold values from -0.15625 to 0.15625
- w_value: bfloat16 [1536, 512], P(('dp', 'ctx')), may hold values from -0.15625 to 0.15625
- w_out: bfloat16 [1536, 1536], P(None, ('dp', 'ctx')), may hold values from -3.5 to 3.5
- qk_gains: bfloat16 [128], P(('dp', 'ctx')), may hold values from 0.099609375 to 1.8984375
- gain_mid: bfloat16 [1536], P(('dp', 'ctx')), may hold values from 0.099609375 to 1.8984375
- w_gate: bfloat16 [1536, 6912], P('dp', 'ctx'), may hold values from -0.15625 to 0.15625
- w_up: bfloat16 [1536, 6912], P('dp', 'ctx'), may hold values from -0.15625 to 0.15625
- w_down: bfloat16 [6912, 1536], P('ctx', 'dp'), may hold values from -0.078125 to 0.078125
- grad_out: bfloat16 [12288, 1536], P(('dp', 'ctx')), may hold values from -6 to 6
Outputs:
- output: bfloat16 [12288, 1536], P(('dp', 'ctx'))
- grad_tokens: float32 [12288, 1536], P(('dp', 'ctx'))
- grad_gain_in: float32 [1536], P(('dp', 'ctx'))
- grad_w_query: float32 [1536, 1536], P(('dp', 'ctx'))
- grad_w_key: float32 [1536, 512], P(('dp', 'ctx'))
- grad_w_value: float32 [1536, 512], P(('dp', 'ctx'))
- grad_w_out: float32 [1536, 1536], P(None, ('dp', 'ctx'))
- grad_qk_gains: float32 [128], P(('dp', 'ctx'))
- grad_gain_mid: float32 [1536], P(('dp', 'ctx'))
- grad_w_gate: float32 [1536, 6912], P('dp', 'ctx')
- grad_w_up: float32 [1536, 6912], P('dp', 'ctx')
- grad_w_down: float32 [6912, 1536], P('ctx', 'dp')
Inputs may be any that keep to these rules, and one draw needn't show every extreme that they name: `seq_lens`: one valid length per sequence slot; in every draw some sequence has exactly 1536.
All inputs are finite; a program needn't handle non-finite values.
Results may differ from a plain program's by a relative error of at most 0.018.
Values may be sent and summed in bfloat16 or wider, within the bound.
A program may use at most 448 MiB of HBM per device.

v0:
```python
import jax
import jax.numpy as jnp
from jax import lax
from jax.sharding import PartitionSpec as P

H = 24
KVH = 8
HD = 64


EPSILON = 1e-05
THETA = 1000000.0
NEG_BIG = -1e30


def rms_scale(values, gain_vec):
    factor = lax.rsqrt(jnp.mean(values * values, axis=-1, keepdims=True) + EPSILON)
    return (values * factor * gain_vec, factor)


def norm_back(grad_upper, values, factor, gain_vec):
    unit_rows = values * factor
    scaled = grad_upper * gain_vec
    grad_lower = factor * (
        scaled - unit_rows * jnp.mean(scaled * unit_rows, axis=-1, keepdims=True)
    )
    return (grad_lower, grad_upper * unit_rows)


def rope_tables(positions, head_width):
    half_width = head_width // 2
    frequency = THETA ** (-jnp.arange(half_width, dtype=jnp.float32) * 2.0 / head_width)
    angles = positions.astype(jnp.float32)[:, None] * frequency[None, :]
    cosine_table = jnp.concatenate([jnp.cos(angles), jnp.cos(angles)], -1)[:, None, :]
    sine_table = jnp.concatenate([jnp.sin(angles), jnp.sin(angles)], -1)[:, None, :]
    return (cosine_table, sine_table)


def rotate(values, cosine_table, sine_table):
    half_width = values.shape[-1] // 2
    turned = jnp.concatenate([-values[..., half_width:], values[..., :half_width]], -1)
    return values * cosine_table + turned * sine_table


def rotate_back(grad_upper, cosine_table, sine_table):
    half_width = grad_upper.shape[-1] // 2
    moved_sine = grad_upper * sine_table
    turned = jnp.concatenate([moved_sine[..., half_width:], -moved_sine[..., :half_width]], -1)
    return grad_upper * cosine_table + turned


def shards(
    tokens,
    seq_lens,
    gain_in,
    w_query,
    w_key,
    w_value,
    w_out,
    qk_gains,
    gain_mid,
    w_gate,
    w_up,
    w_down,
    grad_out,
):
    f32 = jnp.float32
    bf16 = jnp.bfloat16
    local_rows = tokens.shape[0]
    total_len = local_rows * lax.axis_size("ctx")
    group_size = H // KVH
    score_scale = HD ** (-0.5)
    first_row = lax.axis_index("ctx") * local_rows
    positions = first_row + jnp.arange(local_rows, dtype=jnp.int32)
    key_positions = jnp.arange(total_len, dtype=jnp.int32)
    length = seq_lens[0]
    allowed = (key_positions[None, :] <= positions[:, None]) & (key_positions[None, :] < length)
    valid_rows = (positions < length).astype(f32)[:, None]
    cosine_table, sine_table = rope_tables(positions, HD)
    attn_set = (
        lax.all_gather(w_query, ("dp", "ctx"), axis=0, tiled=True),
        lax.all_gather(w_key, ("dp", "ctx"), axis=0, tiled=True),
        lax.all_gather(w_value, ("dp", "ctx"), axis=0, tiled=True),
        lax.all_gather(w_out, ("dp", "ctx"), axis=1, tiled=True),
        lax.all_gather(gain_in, ("dp", "ctx"), axis=0, tiled=True),
        lax.all_gather(qk_gains, ("dp", "ctx"), axis=0, tiled=True),
        lax.all_gather(gain_mid, ("dp", "ctx"), axis=0, tiled=True),
    )
    full_query, full_key, full_value, full_out, full_gain_in, full_qk, full_gain_mid = attn_set
    ffn_rows = (
        lax.all_gather(w_gate, "dp", axis=0, tiled=True),
        lax.all_gather(w_up, "dp", axis=0, tiled=True),
        lax.all_gather(w_down, "dp", axis=1, tiled=True),
    )
    inputs = tokens.astype(f32)
    upstream = grad_out.astype(f32) * valid_rows
    upstream_low = upstream.astype(bf16)
    normed_f, factor_in = rms_scale(inputs, full_gain_in.astype(f32))
    normed = normed_f.astype(bf16)
    query_raw = jnp.dot(normed, full_query, preferred_element_type=f32).reshape(local_rows, H, HD)
    key_raw = jnp.dot(normed, full_key, preferred_element_type=f32).reshape(local_rows, KVH, HD)
    value_low = jnp.dot(normed, full_value, preferred_element_type=f32).astype(bf16)
    gain_query = full_qk[:HD].astype(f32)
    gain_key = full_qk[HD:].astype(f32)
    query_normed, factor_query = rms_scale(query_raw, gain_query)
    key_normed, factor_key = rms_scale(key_raw, gain_key)
    query_low = rotate(query_normed, cosine_table, sine_table).astype(bf16)
    key_low = (
        rotate(key_normed, cosine_table, sine_table).astype(bf16).reshape(local_rows, KVH * HD)
    )
    key_all, value_all = (
        lax.all_gather(key_low, "ctx", axis=0, tiled=True),
        lax.all_gather(value_low, "ctx", axis=0, tiled=True),
    )

    def split_keys(matrix):
        return matrix.reshape(total_len, KVH, HD).transpose(1, 0, 2)

    def join_keys(matrix):
        return matrix.transpose(1, 0, 2).reshape(total_len, KVH * HD)

    query_heads = query_low.reshape(local_rows, KVH, group_size, HD).transpose(1, 0, 2, 3)

    def head_scores(query_head, key_head):
        scores = (
            jnp.einsum("tgd,jd->tgj", query_head, key_head, preferred_element_type=f32)
            * score_scale
        )
        return jnp.where(allowed[:, None, :], scores, NEG_BIG)

    def head_forward(pieces):
        query_head, key_head, value_head = pieces
        scores = head_scores(query_head, key_head)
        row_top = jnp.max(scores, axis=-1, keepdims=True)
        expanded = jnp.exp(scores - row_top)
        row_total = jnp.sum(expanded, axis=-1, keepdims=True)
        probs_low = (expanded / row_total).astype(bf16)
        mixed_head = jnp.einsum("tgj,jd->tgd", probs_low, value_head, preferred_element_type=f32)
        return (mixed_head, row_top + jnp.log(row_total))

    mixed_heads, log_total = lax.map(
        head_forward, (query_heads, split_keys(key_all), split_keys(value_all))
    )
    mixed_low = mixed_heads.transpose(1, 0, 2, 3).reshape(local_rows, H * HD).astype(bf16)
    hidden = inputs + jnp.dot(mixed_low, full_out, preferred_element_type=f32)
    normed_mid_f, factor_mid = rms_scale(hidden, full_gain_mid.astype(f32))
    normed_mid = normed_mid_f.astype(bf16)
    full_gate, full_up, full_down = (
        lax.all_gather(ffn_rows[0], "ctx", axis=1, tiled=True),
        lax.all_gather(ffn_rows[1], "ctx", axis=1, tiled=True),
        lax.all_gather(ffn_rows[2], "ctx", axis=0, tiled=True),
    )
    gate_proj = jnp.dot(normed_mid, full_gate, preferred_element_type=f32)
    up_proj = jnp.dot(normed_mid, full_up, preferred_element_type=f32)
    gate_sigmoid = jax.nn.sigmoid(gate_proj)
    silu_gate = gate_proj * gate_sigmoid
    activated = (silu_gate * up_proj).astype(bf16)
    down_term = jnp.dot(activated, full_down, preferred_element_type=f32)
    result = hidden + down_term
    output = result.astype(bf16)
    grad_down = jnp.einsum("tf,td->fd", activated, upstream_low, preferred_element_type=f32)
    grad_activated = jnp.einsum("td,fd->tf", upstream_low, full_down, preferred_element_type=f32)
    silu_slope = gate_sigmoid * (1.0 + gate_proj * (1.0 - gate_sigmoid))
    grad_gate_low = (grad_activated * up_proj * silu_slope).astype(bf16)
    grad_up_low = (grad_activated * silu_gate).astype(bf16)
    grad_wgate = jnp.einsum("td,tf->df", normed_mid, grad_gate_low, preferred_element_type=f32)
    grad_wup = jnp.einsum("td,tf->df", normed_mid, grad_up_low, preferred_element_type=f32)
    grad_mid_term = jnp.einsum(
        "tf,df->td", grad_gate_low, full_gate, preferred_element_type=f32
    ) + jnp.einsum("tf,df->td", grad_up_low, full_up, preferred_element_type=f32)
    col_grads = (
        lax.psum_scatter(
            grad_wgate.astype(jnp.bfloat16), "ctx", scatter_dimension=1, tiled=True
        ).astype(jnp.float32),
        lax.psum_scatter(
            grad_wup.astype(jnp.bfloat16), "ctx", scatter_dimension=1, tiled=True
        ).astype(jnp.float32),
        lax.psum_scatter(
            grad_down.astype(jnp.bfloat16), "ctx", scatter_dimension=0, tiled=True
        ).astype(jnp.float32),
    )
    ffn_grads = (
        lax.psum_scatter(
            col_grads[0].astype(jnp.bfloat16), "dp", scatter_dimension=0, tiled=True
        ).astype(jnp.float32),
        lax.psum_scatter(
            col_grads[1].astype(jnp.bfloat16), "dp", scatter_dimension=0, tiled=True
        ).astype(jnp.float32),
        lax.psum_scatter(
            col_grads[2].astype(jnp.bfloat16), "dp", scatter_dimension=1, tiled=True
        ).astype(jnp.float32),
    )
    grad_hidden_norm, gain_terms_mid = norm_back(
        grad_mid_term, hidden, factor_mid, full_gain_mid.astype(f32)
    )
    grad_hidden = upstream + grad_hidden_norm
    grad_branch = grad_hidden.astype(bf16)
    grad_wout = jnp.einsum("ta,td->ad", mixed_low, grad_branch, preferred_element_type=f32)
    grad_mixed = jnp.einsum("td,ad->ta", grad_branch, full_out, preferred_element_type=f32).astype(
        bf16
    )
    grad_heads = grad_mixed.reshape(local_rows, KVH, group_size, HD).transpose(1, 0, 2, 3)
    key_back, value_back = (
        lax.all_gather(key_low, "ctx", axis=0, tiled=True),
        lax.all_gather(value_low, "ctx", axis=0, tiled=True),
    )

    def head_backward(pieces):
        query_head, key_head, value_head, log_head, grad_head = pieces
        probs_full = jnp.exp(head_scores(query_head, key_head) - log_head)
        grad_probs = jnp.einsum("tgd,jd->tgj", grad_head, value_head, preferred_element_type=f32)
        row_inner = jnp.sum(probs_full * grad_probs, axis=-1, keepdims=True)
        grad_scores = (probs_full * (grad_probs - row_inner)).astype(bf16)
        grad_query = (
            jnp.einsum("tgj,jd->tgd", grad_scores, key_head, preferred_element_type=f32)
            * score_scale
        )
        grad_key = (
            jnp.einsum("tgj,tgd->jd", grad_scores, query_head, preferred_element_type=f32)
            * score_scale
        )
        grad_value = jnp.einsum(
            "tgj,tgd->jd", probs_full.astype(bf16), grad_head, preferred_element_type=f32
        )
        return (grad_query, grad_key, grad_value)

    grad_query_heads, grad_key_terms, grad_value_terms = lax.map(
        head_backward,
        (query_heads, split_keys(key_back), split_keys(value_back), log_total, grad_heads),
    )
    grad_key_local, grad_value_local = (
        lax.psum_scatter(
            join_keys(grad_key_terms).astype(jnp.bfloat16), "ctx", scatter_dimension=0, tiled=True
        ).astype(jnp.float32),
        lax.psum_scatter(
            join_keys(grad_value_terms).astype(jnp.bfloat16), "ctx", scatter_dimension=0, tiled=True
        ).astype(jnp.float32),
    )
    grad_query_rot = grad_query_heads.transpose(1, 0, 2, 3).reshape(local_rows, H, HD)
    grad_query_norm = rotate_back(grad_query_rot, cosine_table, sine_table)
    grad_query_raw, gain_terms_query = norm_back(
        grad_query_norm, query_raw, factor_query, gain_query
    )
    grad_key_norm = rotate_back(
        grad_key_local.reshape(local_rows, KVH, HD), cosine_table, sine_table
    )
    grad_key_raw, gain_terms_key = norm_back(grad_key_norm, key_raw, factor_key, gain_key)
    grad_query_low = grad_query_raw.reshape(local_rows, H * HD).astype(bf16)
    grad_key_low = grad_key_raw.reshape(local_rows, KVH * HD).astype(bf16)
    grad_value_low = grad_value_local.astype(bf16)
    grad_wquery = jnp.einsum("td,ta->da", normed, grad_query_low, preferred_element_type=f32)
    grad_wkey = jnp.einsum("td,ta->da", normed, grad_key_low, preferred_element_type=f32)
    grad_wvalue = jnp.einsum("td,ta->da", normed, grad_value_low, preferred_element_type=f32)
    grad_normed = (
        jnp.einsum("ta,da->td", grad_query_low, full_query, preferred_element_type=f32)
        + jnp.einsum("ta,da->td", grad_key_low, full_key, preferred_element_type=f32)
        + jnp.einsum("ta,da->td", grad_value_low, full_value, preferred_element_type=f32)
    )
    grad_input_norm, gain_terms_in = norm_back(
        grad_normed, inputs, factor_in, full_gain_in.astype(f32)
    )
    grad_tokens = grad_hidden + grad_input_norm
    grad_qk = jnp.concatenate(
        [jnp.sum(gain_terms_query, axis=(0, 1)), jnp.sum(gain_terms_key, axis=(0, 1))]
    )
    attn_grads = (
        lax.psum_scatter(grad_wquery, ("dp", "ctx"), scatter_dimension=0, tiled=True),
        lax.psum_scatter(grad_wkey, ("dp", "ctx"), scatter_dimension=0, tiled=True),
        lax.psum_scatter(grad_wvalue, ("dp", "ctx"), scatter_dimension=0, tiled=True),
        lax.psum_scatter(grad_wout, ("dp", "ctx"), scatter_dimension=1, tiled=True),
        lax.psum_scatter(
            jnp.sum(gain_terms_in, axis=0), ("dp", "ctx"), scatter_dimension=0, tiled=True
        ),
        lax.psum_scatter(grad_qk, ("dp", "ctx"), scatter_dimension=0, tiled=True),
        lax.psum_scatter(
            jnp.sum(gain_terms_mid, axis=0), ("dp", "ctx"), scatter_dimension=0, tiled=True
        ),
    )
    return (
        output,
        grad_tokens,
        attn_grads[4],
        attn_grads[0],
        attn_grads[1],
        attn_grads[2],
        attn_grads[3],
        attn_grads[5],
        attn_grads[6],
        ffn_grads[0],
        ffn_grads[1],
        ffn_grads[2],
    )


def solution(mesh):
    in_specs = (
        P(("dp", "ctx"), None),
        P("dp"),
        P(("dp", "ctx")),
        P(("dp", "ctx"), None),
        P(("dp", "ctx"), None),
        P(("dp", "ctx"), None),
        P(None, ("dp", "ctx")),
        P(("dp", "ctx")),
        P(("dp", "ctx")),
        P("dp", "ctx"),
        P("dp", "ctx"),
        P("ctx", "dp"),
        P(("dp", "ctx"), None),
    )
    out_specs = (
        P(("dp", "ctx"), None),
        P(("dp", "ctx"), None),
        P(("dp", "ctx")),
        P(("dp", "ctx"), None),
        P(("dp", "ctx"), None),
        P(("dp", "ctx"), None),
        P(None, ("dp", "ctx")),
        P(("dp", "ctx")),
        P(("dp", "ctx")),
        P("dp", "ctx"),
        P("dp", "ctx"),
        P("ctx", "dp"),
    )
    return jax.shard_map(shards, mesh=mesh, in_specs=in_specs, out_specs=out_specs, check_vma=False)
```

profile of v0, /device:TPU:0, one launch (start us, length us, event | category | flops | bytes accessed | tf_op | source)
XLA Modules:
  0.0 3414.7 jit_solution(4939336347800522832)
XLA Ops:
  13.2 42.4 %all-reduce.7 = (bf16[1536]{0:T(1024)(128)(2,1)S(1)}, bf16[128]{0:T(256)(128)(2,1)S(1)}, bf16[1536]{0:T(1024)(128)(2,1)}) all-reduce(bf16[1536]{0:T(1024)(128)(2,1)S(1)} %dynamic-update-slice, bf16[128]{0:T(256)(128)(2,1)S(1)} %dynamic-update-slice.1, bf16[1536]{0:T(1024)(128)(2,1)S(1)} %dynamic-update-slice.2), channel_id=1, replica_groups=mesh['dp'=8,'ctx'=4] {'dp','ctx'}, use_global_device_ids=true, to_apply=%add | all-reduce | flops 3200 | bytes 12800
  78.3 47.3 %all-gather.19.cloned.1.call-done = bf16[1536,512]{1,0:T(8,128)(2,1)} async-done(((bf16[48,512]{1,0:T(8,128)(2,1)}), bf16[1536,512]{1,0:T(8,128)(2,1)}) %all-gather.19.cloned.1.call-update) | async-done | bytes 1572880 | tf_op jit(solution)/shard_map/all_gather | solution.py:83
  130.1 38.5 %all-gather.25.cloned.1.call-done = bf16[1536,1728]{1,0:T(8,128)(2,1)} async-done(((bf16[192,1728]{1,0:T(8,128)(2,1)}), bf16[1536,1728]{1,0:T(8,128)(2,1)}) %all-gather.25.cloned.1.call-update) | async-done | bytes 5308432 | tf_op jit(solution)/shard_map/all_gather | solution.py:91
  176.9 35.7 %all-gather.29.cloned.1.call-done = bf16[1536,1728]{1,0:T(8,128)(2,1)} async-done(((bf16[192,1728]{1,0:T(8,128)(2,1)}), bf16[1536,1728]{1,0:T(8,128)(2,1)}) %all-gather.29.cloned.1.call-update) | async-done | bytes 5308432 | tf_op jit(solution)/shard_map/all_gather | solution.py:92
  220.9 35.7 %all-gather.33.cloned.1.call-done = bf16[1728,1536]{0,1:T(8,128)(2,1)} async-done(((bf16[1728,192]{0,1:T(8,128)(2,1)}), bf16[1728,1536]{0,1:T(8,128)(2,1)}) %all-gather.33.cloned.1.call-update) | async-done | bytes 5308432 | tf_op jit(solution)/shard_map/all_gather | solution.py:93
  268.1 27.6 all-gather.17.cloned.1.call-done
  298.3 35.5 %all-gather.21.cloned.1.call-done = bf16[1536,512]{1,0:T(8,128)(2,1)} async-done(((bf16[384,512]{1,0:T(8,128)(2,1)}), bf16[1536,512]{1,0:T(8,128)(2,1)}) %all-gather.21.cloned.1.call-update) | async-done | bytes 1572880 | tf_op jit(solution)/shard_map/all_gather | solution.py:113
  336.4 62.7 %all-gather.13.cloned.1.call-done = bf16[1536,1536]{1,0:T(8,128)(2,1)} async-done(((bf16[48,1536]{1,0:T(8,128)(2,1)}), bf16[1536,1536]{1,0:T(8,128)(2,1)}) %all-gather.13.cloned.1.call-update) | async-done | bytes 4718608 | tf_op jit(solution)/shard_map/all_gather | solution.py:81
  413.3 78.7 %while.30 = (s32[]{:T(128)}, bf16[8,384,3,64]{1,3,2,0:T(8,128)(2,1)}, f32[8,384,3,1]{1,2,3,0:T(4,128)}, bf16[8,384,3,64]{1,3,2,0:T(8,128)(2,1)}, bf16[8,1536,64]...) while((s32[]{:T(128)}, ...), condition=%wide.region_6.7_spmd.clone.clone, body=%wide.region_3.6_spmd.clone.sunk.clone | while | flops 475396992 | bytes 24472660 | solution.py:141
  498.5 327.2 %all-gather.27.cloned.1.call-done = bf16[1536,6912]{0,1:T(8,128)(2,1)} async-done(((bf16[1536,1728]{0,1:T(8,128)(2,1)}), bf16[1536,6912]{0,1:T(8,128)(2,1)}) %all-gather.27.cloned.1.call-update) | async-done | bytes 21233680 | tf_op jit(solution)/shard_map/all_gather | solution.py:149
  825.7 15.5 fusion.92
  841.2 345.8 %all-gather.31.cloned.1.call-done = bf16[1536,6912]{0,1:T(8,128)(2,1)} async-done(((bf16[1536,1728]{0,1:T(8,128)(2,1)}), bf16[1536,6912]{0,1:T(8,128)(2,1)}) %all-gather.31.cloned.1.call-update) | async-done | bytes 21233680 | tf_op jit(solution)/shard_map/all_gather | solution.py:150
  1187.0 15.2 fusion.93
  1202.2 345.9 %all-gather.35.cloned.1.call-done = bf16[6912,1536]{1,0:T(8,128)(2,1)} async-done(((bf16[1728,1536]{1,0:T(8,128)(2,1)}), bf16[6912,1536]{1,0:T(8,128)(2,1)}) %all-gather.35.cloned.1.call-update) | async-done | bytes 21233680 | tf_op jit(solution)/shard_map/all_gather | solution.py:151
  1548.2 24.2 multiply_convert_fusion.1
  1572.3 17.5 convolution_convert_fusion.2
  1590.0 17.1 convolution_convert_fusion.1
  1607.1 17.4 convolution_convert_fusion
  1638.3 14.4 multiply_reduce_fusion.1
  1659.7 144.4 %while.31 = (s32[]{:T(128)}, f32[8,384,3,64]{1,3,2,0:T(8,128)S(1)}, bf16[8,1536,64]{1,2,0:T(8,128)(2,1)}, bf16[8,1536,64]{1,2,0:T(8,128)(2,1)}, bf16[8,384,3,64]...) while((s32[]{:T(128)}, f32[8,384,3,64]{1,3,2,0:T(8,128)S(1)}, ...), condition=%wide.region_11.12_spmd.clone.clone, body=%wide.region_9.11_spmd.clone.sunk.clone | while | flops 1149737856 | bytes 94304968 | solution.py:227
  1810.2 129.8 %reduce-scatter.31.cloned.1.call-done = bf16[1536,1728]{0,1:T(8,128)(2,1)} async-done(((bf16[1536,6912]{0,1:T(8,128)(2,1)}), bf16[1536,1728]{0,1:T(8,128)(2,1)}) %reduce-scatter.31.cloned.1.call-update) | async-done | bytes 5308432 | tf_op jit(solution)/shard_map/reduce_scatter | solution.py:172
  1948.2 347.0 %reduce-scatter.33.cloned.1.call-done = bf16[1536,1728]{0,1:T(8,128)(2,1)} async-done(((bf16[1536,6912]{0,1:T(8,128)(2,1)}), bf16[1536,1728]{0,1:T(8,128)(2,1)}) %reduce-scatter.33.cloned.1.call-update) | async-done | bytes 5308432 | tf_op jit(solution)/shard_map/reduce_scatter | solution.py:175
  2303.4 346.9 %reduce-scatter.35.cloned.1.call-done = bf16[1728,1536]{1,0:T(8,128)(2,1)} async-done(((bf16[6912,1536]{1,0:T(8,128)(2,1)}), bf16[1728,1536]{1,0:T(8,128)(2,1)}) %reduce-scatter.35.cloned.1.call-update) | async-done | bytes 5308432 | tf_op jit(solution)/shard_map/reduce_scatter | solution.py:178
  2658.4 30.9 reduce-scatter.21.cloned.1.call-done
  2704.4 21.6 reduce-scatter.37.cloned.1.call-done
  2790.5 15.4 fusion.60
  2814.6 38.8 %all-reduce.6 = (f32[1536]{0:T(1024)}, f32[128]{0:T(128)}, f32[1536]{0:T(1024)}) all-reduce(f32[1536]{0:T(1024)} %get-tuple-element.219, f32[128]{0:T(128)} %pad_maximum_fusion.4, f32[1536]{0:T(1024)} %get-tuple-element.217), channel_id=4, replica_groups=mesh['dp'=8,'ctx'=4] {'dp','ctx'}, use_global_device_ids=true, to_apply=%region_18.19.clone | all-reduce | flops 3200 | bytes 25600
  2866.7 43.5 %reduce-scatter.43.cloned.1.call-done = bf16[192,1728]{1,0:T(8,128)(2,1)} async-done(((bf16[1536,1728]{1,0:T(8,128)(2,1)}), bf16[192,1728]{1,0:T(8,128)(2,1)}) %reduce-scatter.43.cloned.1.call-update) | async-done | bytes 663568
  2913.0 104.7 %reduce-scatter.25.cloned.1.call-done = f32[48,512]{1,0:T(8,128)} async-done(((f32[1536,512]{1,0:T(8,128)}), f32[48,512]{1,0:T(8,128)}) %reduce-scatter.25.cloned.1.call-update) | async-done | bytes 98320 | tf_op jit(solution)/shard_map/reduce_scatter | solution.py:268
  3017.7 106.5 %reduce-scatter.27.cloned.1.call-done = f32[48,512]{1,0:T(8,128)} async-done(((f32[1536,512]{1,0:T(8,128)}), f32[48,512]{1,0:T(8,128)}) %reduce-scatter.27.cloned.1.call-update) | async-done | bytes 98320 | tf_op jit(solution)/shard_map/reduce_scatter | solution.py:269
  3124.2 141.2 %reduce-scatter.23.cloned.1.call-done = f32[48,1536]{1,0:T(8,128)} async-done(((f32[1536,1536]{1,0:T(8,128)}), f32[48,1536]{1,0:T(8,128)}) %reduce-scatter.23.cloned.1.call-update) | async-done | bytes 294928 | tf_op jit(solution)/shard_map/reduce_scatter | solution.py:267
  3265.4 141.9 %reduce-scatter.29.cloned.1.call-done = f32[1536,48]{0,1:T(8,128)} async-done(((f32[1536,1536]{0,1:T(8,128)}), f32[1536,48]{0,1:T(8,128)}) %reduce-scatter.29.cloned.1.call-update) | async-done | bytes 294928 | tf_op jit(solution)/shard_map/reduce_scatter | solution.py:270
  (424 shorter events, 464.1 us)
Async XLA Ops:
  7.2 61.6 %all-gather.15.cloned.1.call-start = ((), (), s32[]{:S(2)}) async-start(), calls=%async_computation.13 | async-start | bytes 1622016 | tf_op jit(solution)/shard_map/all_gather | solution.py:82
  7.9 117.7 %all-gather.19.cloned.1.call-start = ((), (), s32[]{:S(2)}) async-start(), calls=%async_computation.15 | async-start | bytes 1622016 | tf_op jit(solution)/shard_map/all_gather | solution.py:83
  8.7 49.6 %copy-start.1 = (bf16[384,1536]{1,0:T(8,128)(2,1)S(1)}, bf16[384,1536]{1,0:T(8,128)(2,1)}, u32[]{:S(2)}) copy-start(bf16[384,1536]{1,0:T(8,128)(2,1)} %param.17) | copy-start | bytes 3538948
  8.7 159.9 %all-gather.25.cloned.1.call-start = ((), (), s32[]{:S(2)}) async-start(), calls=%async_computation.18 | async-start | bytes 6193152 | tf_op jit(solution)/shard_map/all_gather | solution.py:91
  9.4 203.2 %all-gather.29.cloned.1.call-start = ((), (), s32[]{:S(2)}) async-start(), calls=%async_computation.20 | async-start | bytes 6193152 | tf_op jit(solution)/shard_map/all_gather | solution.py:92
  10.0 246.6 %all-gather.33.cloned.1.call-start = ((), (), s32[]{:S(2)}) async-start(), calls=%async_computation.22 | async-start | bytes 6193152 | tf_op jit(solution)/shard_map/all_gather | solution.py:93
  10.6 285.1 %all-gather.17.cloned.1.call-start = ((), (), s32[]{:S(2)}) async-start(), calls=%async_computation.14 | async-start | bytes 1966080 | tf_op jit(solution)/shard_map/all_gather | solution.py:112
  55.5 343.5 %copy-start.33 = (f32[1536]{0:T(1024)}, f32[1536]{0:T(1024)S(1)}, u32[]{:S(2)}) copy-start(f32[1536]{0:T(1024)S(1)} %convert_element_type.144) | copy-start | bytes 18436
  58.6 67.0 %copy-start.42 = (f32[384]{0:T(512)}, f32[384]{0:T(512)S(1)}, u32[]{:S(2)}) copy-start(f32[384]{0:T(512)S(1)} %add_rsqrt_fusion.3) | copy-start | bytes 4612
  78.2 255.6 %all-gather.21.cloned.1.call-start = ((), (), s32[]{:S(2)}) async-start(), calls=%async_computation.16 | async-start | bytes 1966080 | tf_op jit(solution)/shard_map/all_gather | solution.py:113
  128.6 270.5 %all-gather.13.cloned.1.call-start = ((), (), s32[]{:S(2)}) async-start(), calls=%async_computation.12 | async-start | bytes 4866048 | tf_op jit(solution)/shard_map/all_gather | solution.py:81
  129.3 362.6 %all-gather.23.cloned.1.call-start = ((), (), s32[]{:S(2)}) async-start(), calls=%async_computation.17 | async-start | bytes 4866048 | tf_op jit(solution)/shard_map/all_gather | solution.py:84
  130.1 695.6 %all-gather.27.cloned.1.call-start = ((), (), s32[]{:S(2)}) async-start(), calls=%async_computation.19 | async-start | bytes 26542080 | tf_op jit(solution)/shard_map/all_gather | solution.py:149
  176.9 1010.1 %all-gather.31.cloned.1.call-start = ((), (), s32[]{:S(2)}) async-start(), calls=%async_computation.21 | async-start | bytes 26542080 | tf_op jit(solution)/shard_map/all_gather | solution.py:150
  220.9 1327.3 %all-gather.35.cloned.1.call-start = ((), (), s32[]{:S(2)}) async-start(), calls=%async_computation.23 | async-start | bytes 26542080 | tf_op jit(solution)/shard_map/all_gather | solution.py:151
  264.8 1675.2 %reduce-scatter.31.cloned.1.call-start = ((), (), s32[]{:S(2)}) async-start(), calls=%async_computation.29 | async-start | bytes 26542080 | tf_op jit(solution)/shard_map/reduce_scatter | solution.py:172
  298.3 100.8 %copy-start.43 = (f32[384]{0:T(512)S(1)}, f32[384]{0:T(512)}, u32[]{:S(2)}) copy-start(f32[384]{0:T(512)} %copy-done.42) | copy-start | bytes 4612
  841.2 707.0 %copy-start.32 = (bf16[384,1536]{1,0:T(8,128)(2,1)S(1)}, bf16[384,1536]{1,0:T(8,128)(2,1)}, u32[]{:S(2)}) copy-start(bf16[384,1536]{1,0:T(8,128)(2,1)} %param.29) | copy-start | bytes 3538948
  841.2 707.0 %copy-start.50 = (f32[384]{0:T(512)S(1)}, f32[384]{0:T(512)}, u32[]{:S(2)}) copy-start(f32[384]{0:T(512)} %compare_convert_fusion) | copy-start | bytes 4612
  1589.9 705.3 %reduce-scatter.33.cloned.1.call-start = ((), (), s32[]{:S(2)}) async-start(), calls=%async_computation.30 | async-start | bytes 26542080 | tf_op jit(solution)/shard_map/reduce_scatter | solution.py:175
  1607.1 1043.3 %reduce-scatter.35.cloned.1.call-start = ((), (), s32[]{:S(2)}) async-start(), calls=%async_computation.31 | async-start | bytes 26542080 | tf_op jit(solution)/shard_map/reduce_scatter | solution.py:178
  1624.5 1064.9 %reduce-scatter.21.cloned.1.call-start = ((), (), s32[]{:S(2)}) async-start(), calls=%async_computation.24 | async-start | bytes 1966080 | tf_op jit(solution)/shard_map/reduce_scatter | solution.py:232
  1804.0 939.9 %copy-start.7 = (f32[8,384,3,64]{1,3,2,0:T(8,128)}, f32[8,384,3,64]{1,3,2,0:T(8,128)S(1)}, u32[]{:S(2)}) copy-start(f32[8,384,3,64]{1,3,2,0:T(8,128)S(1)} %get-tuple-element.106) | copy-start | bytes 7077892
  1807.4 918.5 %reduce-scatter.37.cloned.1.call-start = ((), (), s32[]{:S(2)}) async-start(), calls=%async_computation.32 | async-start | bytes 1966080
  1810.1 1050.9 %reduce-scatter.39.cloned.1.call-start = ((), (), s32[]{:S(2)}) async-start(), calls=%async_computation.33 | async-start | bytes 6193152
  1948.2 915.7 %reduce-scatter.41.cloned.1.call-start = ((), (), s32[]{:S(2)}) async-start(), calls=%async_computation.34 | async-start | bytes 6193152
  2303.4 606.8 %reduce-scatter.43.cloned.1.call-start = ((), (), s32[]{:S(2)}) async-start(), calls=%async_computation.35 | async-start | bytes 6193152
  2658.3 34.4 %copy-start.10 = (f32[384,512]{0,1:T(8,128)S(1)}, f32[384,512]{0,1:T(8,128)}, u32[]{:S(2)}) copy-start(f32[384,512]{0,1:T(8,128)} %copy-done.9) | copy-start | bytes 2359300
  2658.4 359.3 %reduce-scatter.25.cloned.1.call-start = ((), (), s32[]{:S(2)}) async-start(), calls=%async_computation.26 | async-start | bytes 3244032 | tf_op jit(solution)/shard_map/reduce_scatter | solution.py:268
  2704.3 419.9 %reduce-scatter.27.cloned.1.call-start = ((), (), s32[]{:S(2)}) async-start(), calls=%async_computation.27 | async-start | bytes 3244032 | tf_op jit(solution)/shard_map/reduce_scatter | solution.py:269
  2729.8 535.7 %reduce-scatter.23.cloned.1.call-start = ((), (), s32[]{:S(2)}) async-start(), calls=%async_computation.25 | async-start | bytes 9732096 | tf_op jit(solution)/shard_map/reduce_scatter | solution.py:267
  2775.9 631.5 %reduce-scatter.29.cloned.1.call-start = ((), (), s32[]{:S(2)}) async-start(), calls=%async_computation.28 | async-start | bytes 9732096 | tf_op jit(solution)/shard_map/reduce_scatter | solution.py:270
  (69 other events, 399.3 us)
Sparse Core Ops, SparseCore 0:
  10.9 57.8 all-gather.14
  71.6 53.9 all-gather.18
  127.5 41.0 all-gather.24
  170.3 42.2 all-gather.28
  214.3 42.2 all-gather.32
  258.6 37.0 all-gather.16
  297.9 35.9 all-gather.20
  336.6 62.3 all-gather.12
  401.9 62.3 all-gather.22
  465.7 359.9 all-gather.26
  827.3 359.6 all-gather.30
  1188.4 359.6 all-gather.34
  1590.0 349.9 reduce-scatter.30
  1942.3 352.8 reduce-scatter.32
  2297.4 352.8 reduce-scatter.34
  2652.6 36.7 reduce-scatter.20
  2691.6 34.2 reduce-scatter.36
  2729.6 56.8 reduce-scatter.38
  2789.9 58.5 reduce-scatter.40
  2852.3 57.8 reduce-scatter.42
  2916.2 101.4 reduce-scatter.24
  3023.7 100.4 reduce-scatter.26
  3130.7 134.6 reduce-scatter.22
  3272.8 134.5 reduce-scatter.28
where the time goes:
time: 3420 us; the launch traced here: 3410 us
  waiting for transfers between devices  2730 us (80%)
  matrix products  358 us (10%)
  local copies, waits for them, and re-layouts  128 us (4%)
  other arithmetic  98.4 us (3%)
  blocking collectives  81.1 us (2%)
    reduce_scatter x1, waiting for transfers between devices, shards(): lax.psum_scatter(grad_wup.astype(jnp.bfloat16), 'ctx', scatter_dimension=...  347 us
    reduce_scatter x1, waiting for transfers between devices, shards(): lax.psum_scatter(grad_down.astype(jnp.bfloat16), 'ctx', scatter_dimension...  347 us
    all_gather x1, waiting for transfers between devices, shards(): lax.all_gather(ffn_rows[2], 'ctx', axis=0, tiled=True)  346 us
    all_gather x1, waiting for transfers between devices, shards(): lax.all_gather(ffn_rows[1], 'ctx', axis=1, tiled=True)  346 us
    all_gather x1, waiting for transfers between devices, shards(): lax.all_gather(ffn_rows[0], 'ctx', axis=1, tiled=True)  327 us
    reduce_scatter x1, waiting for transfers between devices, shards(): lax.psum_scatter(grad_wout, ('dp', 'ctx'), scatter_dimension=1, tiled=True)  142 us
    reduce_scatter x1, waiting for transfers between devices, shards(): lax.psum_scatter(grad_wquery, ('dp', 'ctx'), scatter_dimension=0, tiled=T...  141 us
    reduce_scatter x1, waiting for transfers between devices, shards(): lax.psum_scatter(grad_wgate.astype(jnp.bfloat16), 'ctx', scatter_dimensio...  130 us
  transfers between devices with their start and end apart: 24, of which 21 were waited for; matrix products, arithmetic and copies ran while one was open for 16% of the time, Pallas kernels for 0%

commit v1 on v0

v1 whole, which is shorter than its diff:
```python
import functools

import jax
import jax.numpy as jnp
from jax import lax
from jax.experimental import pallas as pl
from jax.experimental.pallas import tpu as pltpu
from jax.sharding import PartitionSpec as P

H = 24
KVH = 8
HD = 64
GROUP = H // KVH
PAIRS = KVH // 2


EPSILON = 1e-05
THETA = 1000000.0
NEG_BIG = -1e30

f32 = jnp.float32
bf16 = jnp.bfloat16

NT = (((1,), (1,)), ((), ()))
NN = (((1,), (0,)), ((), ()))


def rms_scale(values, gain_vec):
    factor = lax.rsqrt(jnp.mean(values * values, axis=-1, keepdims=True) + EPSILON)
    return (values * factor * gain_vec, factor)


def norm_back(grad_upper, values, factor, gain_vec):
    unit_rows = values * factor
    scaled = grad_upper * gain_vec
    grad_lower = factor * (
        scaled - unit_rows * jnp.mean(scaled * unit_rows, axis=-1, keepdims=True)
    )
    return (grad_lower, grad_upper * unit_rows)


def rope_tables(positions, head_width):
    half_width = head_width // 2
    frequency = THETA ** (-jnp.arange(half_width, dtype=jnp.float32) * 2.0 / head_width)
    angles = positions.astype(jnp.float32)[:, None] * frequency[None, :]
    cosine_table = jnp.concatenate([jnp.cos(angles), jnp.cos(angles)], -1)[:, None, :]
    sine_table = jnp.concatenate([jnp.sin(angles), jnp.sin(angles)], -1)[:, None, :]
    return (cosine_table, sine_table)


def rotate(values, cosine_table, sine_table):
    half_width = values.shape[-1] // 2
    turned = jnp.concatenate([-values[..., half_width:], values[..., :half_width]], -1)
    return values * cosine_table + turned * sine_table


def rotate_back(grad_upper, cosine_table, sine_table):
    half_width = grad_upper.shape[-1] // 2
    moved_sine = grad_upper * sine_table
    turned = jnp.concatenate([moved_sine[..., half_width:], -moved_sine[..., :half_width]], -1)
    return grad_upper * cosine_table + turned


def mdot(a, b, dims=NN):
    return lax.dot_general(a, b, dims, preferred_element_type=f32)


def causal_mask(rows, limit, key_axis):
    shape = (rows, rows)
    key = lax.broadcasted_iota(jnp.int32, shape, key_axis)
    row = lax.broadcasted_iota(jnp.int32, shape, 1 - key_axis)
    return jnp.where((key <= row) & (key < limit), 0.0, NEG_BIG).astype(f32)


def attn_fwd_kernel(blocks, where_ref, q_ref, *refs):
    kv_refs, (o_ref, log_ref, mask, acc) = refs[:blocks], refs[blocks:]
    rows = q_ref.shape[0]
    mine, limit = where_ref[0], where_ref[1]

    @pl.when(pl.program_id(0) == 0)
    def _():
        mask[...] = causal_mask(rows, limit, 1)

    def head(kv_ref, pair, diagonal):
        keys = kv_ref[0][:, pair * HD : (pair + 1) * HD]
        values = kv_ref[1][:, pair * HD : (pair + 1) * HD]
        extended = jnp.concatenate([values, jnp.ones_like(values)], -1)
        for g in range(GROUP):
            h = pair * GROUP + g
            scores = mdot(q_ref[:, h * HD : (h + 1) * HD], keys, NT)
            if diagonal:
                scores = scores + mask[...]
            term = mdot(jnp.exp(scores).astype(bf16), extended)
            acc[h] = term if diagonal else acc[h] + term

    for pair in range(2):
        head(kv_refs[0], pair, True)
    for back in range(1, blocks):

        @pl.when(mine >= back)
        def _():
            for pair in range(2):
                head(kv_refs[back], pair, False)

    lane = lax.broadcasted_iota(jnp.int32, (rows, 2 * HD), 1)
    logs = jnp.zeros((rows, 2 * HD), f32)
    for h in range(2 * GROUP):
        full = acc[h]
        total = full[:, HD : HD + 1]
        o_ref[:, h * HD : (h + 1) * HD] = (full[:, :HD] / total).astype(bf16)
        logs = jnp.where(lane == h, jnp.log(total), logs)
    log_ref[0] = jnp.transpose(logs)[:8]


def attn_bwd_kernel(blocks, where_ref, q_ref, *refs):
    kv_refs = refs[:blocks]
    do_ref, o_ref, log_ref = refs[blocks : blocks + 3]
    dq_ref = refs[blocks + 3]
    dkv_refs = refs[blocks + 4 : 2 * blocks + 4]
    mask, dqt, inner = refs[2 * blocks + 4 :]
    rows = q_ref.shape[0]
    mine, limit = where_ref[0], where_ref[1]

    @pl.when(pl.program_id(0) == 0)
    def _():
        mask[...] = causal_mask(rows, limit, 0)

    ones = jnp.ones((8, HD), f32)
    for h in range(2 * GROUP):
        cols = slice(h * HD, (h + 1) * HD)
        product = do_ref[:, cols].astype(f32) * o_ref[:, cols].astype(f32)
        inner[h] = lax.dot_general(
            ones, product, NT, preferred_element_type=f32, precision=lax.Precision.HIGHEST
        )

    def head(back, pair):
        cols = slice(pair * HD, (pair + 1) * HD)
        keys = kv_refs[back][0][:, cols]
        values = kv_refs[back][1][:, cols]
        keys_t = jnp.transpose(keys)
        grad_k = jnp.zeros((rows, HD), f32)
        grad_v = jnp.zeros((rows, HD), f32)
        for g in range(GROUP):
            h = pair * GROUP + g
            query = q_ref[:, h * HD : (h + 1) * HD]
            grad = do_ref[:, h * HD : (h + 1) * HD]
            scores = mdot(keys, query, NT) - log_ref[0][h : h + 1]
            if back == 0:
                scores = scores + mask[...]
            probs = jnp.exp(scores)
            gaps = mdot(values, grad, NT) - inner[h][0:1]
            grad_scores = (probs * gaps).astype(bf16)
            grad_k += mdot(grad_scores, query)
            grad_v += mdot(probs.astype(bf16), grad)
            term = mdot(keys_t, grad_scores)
            dqt[h] = term if back == 0 else dqt[h] + term
        dkv_refs[back][0, :, cols] = grad_k.astype(dkv_refs[back].dtype)
        dkv_refs[back][1, :, cols] = grad_v.astype(dkv_refs[back].dtype)

    for pair in range(2):
        head(0, pair)
    for back in range(1, blocks):

        @pl.when(mine >= back)
        def _():
            for pair in range(2):
                head(back, pair)

        @pl.when(mine < back)
        def _():
            dkv_refs[back][...] = jnp.zeros_like(dkv_refs[back])

    for h in range(2 * GROUP):
        dq_ref[:, h * HD : (h + 1) * HD] = jnp.transpose(dqt[h]) * (HD**-0.5)


def kv_spec(rows):
    return pl.BlockSpec((2, rows, 2 * HD), lambda i, *_: (0, 0, i))


def head_spec(rows):
    return pl.BlockSpec((rows, 2 * GROUP * HD), lambda i, *_: (0, i))


def log_spec(rows):
    return pl.BlockSpec((1, 8, rows), lambda i, *_: (i, 0, 0))


def attn_forward(where, query, kv_blocks):
    rows, blocks = query.shape[0], len(kv_blocks)
    return pl.pallas_call(
        functools.partial(attn_fwd_kernel, blocks),
        grid_spec=pltpu.PrefetchScalarGridSpec(
            num_scalar_prefetch=1,
            grid=(PAIRS,),
            in_specs=[head_spec(rows)] + [kv_spec(rows)] * blocks,
            out_specs=[head_spec(rows), log_spec(rows)],
            scratch_shapes=[
                pltpu.VMEM((rows, rows), f32),
                pltpu.VMEM((2 * GROUP, rows, 2 * HD), f32),
            ],
        ),
        out_shape=[
            jax.ShapeDtypeStruct((rows, H * HD), bf16),
            jax.ShapeDtypeStruct((PAIRS, 8, rows), f32),
        ],
        compiler_params=pltpu.CompilerParams(vmem_limit_bytes=48 * 2**20),
        cost_estimate=pl.CostEstimate(
            flops=16 * H * rows * rows * blocks * HD,
            bytes_accessed=8 * rows * H * HD,
            transcendentals=H * rows * rows * blocks,
        ),
        name="attn_forward",
    )(where, query, *kv_blocks)


def attn_backward(where, query, kv_blocks, grad, mixed, logs):
    rows, blocks = query.shape[0], len(kv_blocks)
    kinds = [f32] + [bf16] * (blocks - 1)
    return pl.pallas_call(
        functools.partial(attn_bwd_kernel, blocks),
        grid_spec=pltpu.PrefetchScalarGridSpec(
            num_scalar_prefetch=1,
            grid=(PAIRS,),
            in_specs=[head_spec(rows)]
            + [kv_spec(rows)] * blocks
            + [head_spec(rows), head_spec(rows), log_spec(rows)],
            out_specs=[head_spec(rows)] + [kv_spec(rows)] * blocks,
            scratch_shapes=[
                pltpu.VMEM((rows, rows), f32),
                pltpu.VMEM((2 * GROUP, HD, rows), f32),
                pltpu.VMEM((2 * GROUP, 8, rows), f32),
            ],
        ),
        out_shape=[jax.ShapeDtypeStruct((rows, H * HD), f32)]
        + [jax.ShapeDtypeStruct((2, rows, KVH * HD), kind) for kind in kinds],
        compiler_params=pltpu.CompilerParams(vmem_limit_bytes=56 * 2**20),
        cost_estimate=pl.CostEstimate(
            flops=40 * H * rows * rows * blocks * HD,
            bytes_accessed=20 * rows * H * HD,
            transcendentals=H * rows * rows * blocks,
        ),
        name="attn_backward",
    )(where, query, *kv_blocks, grad, mixed, logs)


def shards(
    tokens,
    seq_lens,
    gain_in,
    w_query,
    w_key,
    w_value,
    w_out,
    qk_gains,
    gain_mid,
    w_gate,
    w_up,
    w_down,
    grad_out,
):
    every = ("dp", "ctx")
    rows, width = tokens.shape
    ctx = lax.axis_size("ctx")
    world = ctx * lax.axis_size("dp")
    mine = lax.axis_index("ctx")
    share = w_query.shape[0]
    qk_share = qk_gains.shape[0]
    positions = mine * rows + jnp.arange(rows, dtype=jnp.int32)
    length = seq_lens[0]
    valid_rows = (positions < length).astype(f32)[:, None]
    where = jnp.stack([mine.astype(jnp.int32), length - mine * rows])
    cosine_table, sine_table = rope_tables(positions, HD)

    def swap(block, r):
        return lax.ppermute(block, "ctx", [(i, i ^ r) for i in range(ctx)])

    def up(block, k):
        return lax.ppermute(block, "ctx", [(i, i + k) for i in range(ctx - k)])

    def down(block, k):
        return lax.ppermute(block, "ctx", [(i + k, i) for i in range(ctx - k)])

    def gather(block, axes):
        return lax.all_gather(block, axes, axis=0, tiled=True)

    def scatter(block, axes):
        return lax.psum_scatter(block, axes, scatter_dimension=0, tiled=True)

    extra = jnp.stack([gain_in, gain_mid, jnp.pad(qk_gains, (0, share - qk_share))], 1)
    extra = jnp.pad(extra, ((0, 0), (0, 125)))
    full_kv = gather(jnp.concatenate([w_key, w_value, extra], 1), every)
    kv_width = 2 * KVH * HD
    full_extra = full_kv[:, kv_width:].astype(f32)
    full_gain_in, full_gain_mid = full_extra[:, 0], full_extra[:, 1]
    full_qk = full_extra[:, 2].reshape(world, share)[:, :qk_share].reshape(-1)
    full_kv = full_kv[:, :kv_width]
    full_query = gather(w_query, every)
    full_out_t = gather(w_out.T, every)
    full_gate = gather(w_gate, "dp")
    full_up = gather(w_up, "dp")
    full_down_t = gather(w_down.T, "dp")

    inputs = tokens.astype(f32)
    upstream = grad_out.astype(f32) * valid_rows
    upstream_low = upstream.astype(bf16)
    ups = [upstream_low] + [swap(upstream_low, r) for r in range(1, ctx)]

    normed_f, factor_in = rms_scale(inputs, full_gain_in)
    normed = normed_f.astype(bf16)
    kv_raw = mdot(normed, full_kv)
    key_raw = kv_raw[:, : KVH * HD].reshape(rows, KVH, HD)
    value_low = kv_raw[:, KVH * HD :].astype(bf16)
    query_raw = mdot(normed, full_query).reshape(rows, H, HD)
    gain_query = full_qk[:HD]
    gain_key = full_qk[HD:]
    key_normed, factor_key = rms_scale(key_raw, gain_key)
    key_low = rotate(key_normed, cosine_table, sine_table).astype(bf16).reshape(rows, KVH * HD)
    kv_own = jnp.stack([key_low, value_low])
    kv_blocks = [kv_own] + [up(kv_own, k) for k in range(1, ctx)]
    query_normed, factor_query = rms_scale(query_raw, gain_query)
    query_low = rotate(query_normed, cosine_table, sine_table).astype(bf16)
    query_low = (query_low * (HD**-0.5)).astype(bf16).reshape(rows, H * HD)

    mixed_low, logs = attn_forward(where, query_low, kv_blocks)
    hidden = inputs + mdot(mixed_low, full_out_t, NT)
    normed_mid_f, factor_mid = rms_scale(hidden, full_gain_mid)
    normed_mid = normed_mid_f.astype(bf16)

    mids = [normed_mid] + [swap(normed_mid, r) for r in range(1, ctx)]
    kept = []
    downs, grads_mid = [], []
    for r in range(ctx):
        gate_proj = mdot(mids[r], full_gate)
        up_proj = mdot(mids[r], full_up)
        grad_activated = mdot(ups[r], full_down_t)
        gate_sigmoid = jax.nn.sigmoid(gate_proj)
        silu_gate = gate_proj * gate_sigmoid
        activated = (silu_gate * up_proj).astype(bf16)
        silu_slope = gate_sigmoid * (1.0 + gate_proj * (1.0 - gate_sigmoid))
        grad_gate = (grad_activated * up_proj * silu_slope).astype(bf16)
        grad_up = (grad_activated * silu_gate).astype(bf16)
        kept.append((activated, grad_gate, grad_up))
        grad_term = mdot(grad_gate, full_gate, NT) + mdot(grad_up, full_up, NT)
        down_term = mdot(activated, full_down_t, NT)
        if r:
            grad_term = swap(grad_term.astype(bf16), r).astype(f32)
            down_term = swap(down_term.astype(bf16), r).astype(f32)
        grads_mid.append(grad_term)
        downs.append(down_term)
    grad_mid_term = sum(grads_mid[1:], grads_mid[0])
    output = (hidden + sum(downs[1:], downs[0])).astype(bf16)

    TN = (((0,), (0,)), ((), ()))
    all_mid = jnp.concatenate(mids, 0)
    all_up = jnp.concatenate(ups, 0)
    all_act, all_gg, all_gu = (jnp.concatenate([k[i] for k in kept], 0) for i in range(3))
    grad_wgate = scatter(mdot(all_mid, all_gg, TN).astype(bf16), "dp").astype(f32)
    grad_wup = scatter(mdot(all_mid, all_gu, TN).astype(bf16), "dp").astype(f32)
    grad_wdown = scatter(mdot(all_up, all_act, TN).astype(bf16), "dp").astype(f32).T

    grad_hidden_norm, gain_terms_mid = norm_back(grad_mid_term, hidden, factor_mid, full_gain_mid)
    grad_hidden = upstream + grad_hidden_norm
    grad_branch = grad_hidden.astype(bf16)
    grad_mixed = mdot(grad_branch, full_out_t).astype(bf16)
    grad_wout_t = mdot(grad_branch, mixed_low, TN).astype(bf16)

    grad_query_rot, grad_kv_own, *grad_kv_terms = attn_backward(
        where, query_low, kv_blocks, grad_mixed, mixed_low, logs
    )
    grad_kv = grad_kv_own
    for k in range(1, ctx):
        grad_kv = grad_kv + down(grad_kv_terms[k - 1], k).astype(f32)

    grad_query_norm = rotate_back(grad_query_rot.reshape(rows, H, HD), cosine_table, sine_table)
    grad_query_raw, gain_terms_query = norm_back(
        grad_query_norm, query_raw, factor_query, gain_query
    )
    grad_key_norm = rotate_back(grad_kv[0].reshape(rows, KVH, HD), cosine_table, sine_table)
    grad_key_raw, gain_terms_key = norm_back(grad_key_norm, key_raw, factor_key, gain_key)
    grad_query_low = grad_query_raw.reshape(rows, H * HD).astype(bf16)
    grad_kv_low = jnp.concatenate(
        [grad_key_raw.reshape(rows, KVH * HD).astype(bf16), grad_kv[1].astype(bf16)], 1
    )
    grad_wquery = mdot(normed, grad_query_low, TN).astype(bf16)
    grad_wkv = mdot(normed, grad_kv_low, TN).astype(bf16)
    grad_normed = mdot(grad_query_low, full_query, NT) + mdot(grad_kv_low, full_kv, NT)
    grad_input_norm, gain_terms_in = norm_back(grad_normed, inputs, factor_in, full_gain_in)
    grad_tokens = grad_hidden + grad_input_norm
    grad_qk = jnp.concatenate(
        [jnp.sum(gain_terms_query, axis=(0, 1)), jnp.sum(gain_terms_key, axis=(0, 1))]
    )
    qk_column = jnp.pad(grad_qk.reshape(world, qk_share), ((0, 0), (0, share - qk_share)))
    grad_extra = jnp.stack(
        [jnp.sum(gain_terms_in, axis=0), jnp.sum(gain_terms_mid, axis=0), qk_column.reshape(-1)], 1
    )
    grad_extra = jnp.pad(grad_extra, ((0, 0), (0, 125))).astype(bf16)
    grad_wout = scatter(grad_wout_t, every).astype(f32).T
    grad_rest = scatter(jnp.concatenate([grad_wquery, grad_wkv, grad_extra], 1), every).astype(f32)
    cuts = (H * HD, H * HD + KVH * HD, H * HD + 2 * KVH * HD)
    return (
        output,
        grad_tokens,
        grad_rest[:, cuts[2]],
        grad_rest[:, : cuts[0]],
        grad_rest[:, cuts[0] : cuts[1]],
        grad_rest[:, cuts[1] : cuts[2]],
        grad_wout,
        grad_rest[:qk_share, cuts[2] + 2],
        grad_rest[:, cuts[2] + 1],
        grad_wgate,
        grad_wup,
        grad_wdown,
    )


def solution(mesh):
    every = ("dp", "ctx")
    rows, one = P(every, None), P(every)
    in_specs = (
        rows,
        P("dp"),
        one,
        rows,
        rows,
        rows,
        P(None, every),
        one,
        one,
        P("dp", "ctx"),
        P("dp", "ctx"),
        P("ctx", "dp"),
        rows,
    )
    out_specs = (
        rows,
        rows,
        one,
        rows,
        rows,
        rows,
        P(None, every),
        one,
        one,
        P("dp", "ctx"),
        P("dp", "ctx"),
        P("ctx", "dp"),
    )
    return jax.shard_map(shards, mesh=mesh, in_specs=in_specs, out_specs=out_specs, check_vma=False)
```

time: 3420 us -> 1170 us (0.34)
  waiting for transfers between devices: 2730 us -> 713 us
  matrix products: 358 us -> 213 us
  blocking collectives: 81.1 us -> 0 us
  starting transfers between devices: 1.14 us -> 59.6 us
  local copies, waits for them, and re-layouts: 128 us -> 72.4 us
  other arithmetic: 98.4 us -> 55.7 us
    reduce_scatter x8 -> x4, waiting for transfers between devices: 1350 us -> 64.3 us  [scatter(): return lax.psum_scatter(block, axes, scatter_dimension=0, tiled=True)]
    all_gather x12 -> x6, waiting for transfers between devices: 1310 us -> 300 us  [gather(): return lax.all_gather(block, axes, axis=0, tiled=True)]
    ppermute x0 -> x18, waiting for transfers between devices: none -> 212 us  [the longest x12 130 us: swap(): return lax.ppermute(block, 'ctx', [(i, i ^ r) for i in range(ctx)])]
    dot_general x77 -> x36, matrix products: 358 us -> 213 us  [mdot(): return lax.dot_general(a, b, dims, preferred_element_type=f32)]
    unnamed x2 -> x0, blocking collectives: 81.1 us -> none
    unnamed x28 -> x12, waiting for transfers between devices: 69.8 us -> 136 us
    ppermute x0 -> x18, starting transfers between devices: none -> 58.3 us  [the longest x12 46.3 us: swap(): return lax.ppermute(block, 'ctx', [(i, i ^ r) for i in range(ctx)])]
  transfers between devices with their start and end apart: 24 -> 29, of which waited for: 21 -> 14; matrix products, arithmetic and copies ran while one was open for 16% -> 27% of each run, Pallas kernels for 0% -> 3%
where the time goes in v1:
time: 1170 us; the launch traced here: 1160 us
  waiting for transfers between devices  713 us (61%)
  matrix products  213 us (18%)
  local copies, waits for them, and re-layouts  72.4 us (6%)
  starting transfers between devices  59.6 us (5%)
  other arithmetic  55.7 us (5%)
  Pallas kernels  33.9 us (3%)
  between operations  15.9 us (1%)
    all_gather x6, waiting for transfers between devices, gather(): return lax.all_gather(block, axes, axis=0, tiled=True)  300 us
    dot_general x36, matrix products, mdot(): return lax.dot_general(a, b, dims, preferred_element_type=f32)  213 us
    unnamed x12, waiting for transfers between devices  136 us
    ppermute x12, waiting for transfers between devices, swap(): return lax.ppermute(block, 'ctx', [(i, i ^ r) for i in range(ctx)])  130 us
    ppermute x3, waiting for transfers between devices, down(): return lax.ppermute(block, 'ctx', [(i + k, i) for i in range(ctx - k)])  81.4 us
    reduce_scatter x4, waiting for transfers between devices, scatter(): return lax.psum_scatter(block, axes, scatter_dimension=0, tiled=True)  64.3 us
    ppermute x12, starting transfers between devices, swap(): return lax.ppermute(block, 'ctx', [(i, i ^ r) for i in range(ctx)])  46.3 us
    unnamed x175, local copies, waits for them, and re-layouts  29.7 us
  transfers between devices with their start and end apart: 29, of which 14 were waited for; matrix products, arithmetic and copies ran while one was open for 27% of the time, Pallas kernels for 3%

profile of v1, /device:TPU:0, one launch (start us, length us, event | category | flops | bytes accessed | tf_op | source)
XLA Modules:
  0.0 1163.7 jit_solution(13221019861951236830)
XLA Ops:
  25.0 89.2 %all-gather.7.cloned.1.call-done = bf16[1536,1152]{1,0:T(8,128)(2,1)} async-done(((bf16[48,1152]{1,0:T(8,128)(2,1)}), bf16[1536,1152]{1,0:T(8,128)(2,1)}) %all-gather.7.cloned.1.call-update) | async-done | bytes 3538960 | tf_op jit(solution)/shard_map/all_gather | solution.py:285
  139.1 51.0 %all-gather.9.cloned.1.call-done = bf16[1536,1536]{1,0:T(8,128)(2,1)} async-done(((bf16[48,1536]{1,0:T(8,128)(2,1)}), bf16[1536,1536]{1,0:T(8,128)(2,1)}) %all-gather.9.cloned.1.call-update) | async-done | bytes 4718608 | tf_op jit(solution)/shard_map/all_gather | solution.py:285
  190.1 6.1 fusion.80
  211.9 6.3 fusion.50
  218.1 26.3 %collective-permute-start.13 = (bf16[384,1536]{1,0:T(8,128)(2,1)}, bf16[384,1536]{1,0:T(8,128)(2,1)}, u32[]{:S(2)}, u32[]{:S(2)}) collective-permute-start(bf16[384,1536]{1,0:T(8,128)(2,1)} %fusion.49), channel_id=1, source_target_pairs={{0,3},{1,2},{2,1},{3,0},{4,7},{5,6},{6,5},{7,4},{8,11},{9,10},{10,... | collective-permute-start | bytes 3538952 | tf_op jit(solution)/shard_map/ppermute | solution.py:276
  244.5 11.3 attn_forward.1
  258.5 50.3 %all-gather.11.cloned.1.call-done = bf16[1536,1536]{1,0:T(8,128)(2,1)} async-done(((bf16[48,1536]{1,0:T(8,128)(2,1)}), bf16[1536,1536]{1,0:T(8,128)(2,1)}) %all-gather.11.cloned.1.call-update) | async-done | bytes 4718608 | tf_op jit(solution)/shard_map/all_gather | solution.py:285
  316.2 35.7 %all-gather.13.cloned.1.call-done = bf16[1536,1728]{1,0:T(8,128)(2,1)} async-done(((bf16[192,1728]{1,0:T(8,128)(2,1)}), bf16[1536,1728]{1,0:T(8,128)(2,1)}) %all-gather.13.cloned.1.call-update) | async-done | bytes 5308432 | tf_op jit(solution)/shard_map/all_gather | solution.py:285
  351.8 7.0 fusion.86
  358.8 37.0 %all-gather.15.cloned.1.call-done = bf16[1536,1728]{1,0:T(8,128)(2,1)} async-done(((bf16[192,1728]{1,0:T(8,128)(2,1)}), bf16[1536,1728]{1,0:T(8,128)(2,1)}) %all-gather.15.cloned.1.call-update) | async-done | bytes 5308432 | tf_op jit(solution)/shard_map/all_gather | solution.py:285
  395.8 7.1 fusion.87
  402.9 36.9 %all-gather.17.cloned.1.call-done = bf16[1536,1728]{1,0:T(8,128)(2,1)} async-done(((bf16[192,1728]{1,0:T(8,128)(2,1)}), bf16[1536,1728]{1,0:T(8,128)(2,1)}) %all-gather.17.cloned.1.call-update) | async-done | bytes 5308432 | tf_op jit(solution)/shard_map/all_gather | solution.py:285
  439.8 9.6 multiply_convert_fusion.6
  449.4 7.8 fusion.95
  473.1 9.6 multiply_convert_fusion.4
  493.2 6.0 fusion.92
  499.2 10.0 multiply_convert_fusion.2
  524.5 10.4 multiply_convert_fusion
  559.1 35.4 %collective-permute-done.12 = bf16[384,1536]{1,0:T(8,128)(2,1)S(1)} collective-permute-done((bf16[384,1536]{1,0:T(8,128)(2,1)S(1)}, bf16[384,1536]{1,0:T(8,128)(2,1)S(1)}, u32[]{:S(2)}, u32[]{:S(2)}) %collective-permute-start.12) | collective-permute-done | bytes 1179680 | tf_op jit(solution)/shard_map/ppermute | solution.py:276
  594.5 6.0 multiply_reduce_fusion.1
  600.5 18.2 %collective-permute-done.4 = bf16[384,1536]{1,0:T(8,128)(2,1)S(1)} collective-permute-done((bf16[384,1536]{1,0:T(8,128)(2,1)S(1)}, bf16[384,1536]{1,0:T(8,128)(2,1)S(1)}, u32[]{:S(2)}, u32[]{:S(2)}) %collective-permute-start.4) | collective-permute-done | bytes 1179680 | tf_op jit(solution)/shard_map/ppermute | solution.py:276
  618.7 76.9 %collective-permute-done.6 = bf16[384,1536]{1,0:T(8,128)(2,1)S(1)} collective-permute-done((bf16[384,1536]{1,0:T(8,128)(2,1)S(1)}, bf16[384,1536]{1,0:T(8,128)(2,1)S(1)}, u32[]{:S(2)}, u32[]{:S(2)}) %collective-permute-start.6) | collective-permute-done | bytes 1179680 | tf_op jit(solution)/shard_map/ppermute | solution.py:276
  704.7 14.4 %convolution_convert_fusion.1 = bf16[1536,1728]{1,0:T(8,128)(2,1)} fusion(bf16[384,1728]{0,1:T(8,128)(2,1)} %get-tuple-element.95, bf16[384,1728]{0,1:T(8,128)(2,1)} %get-tuple-element.92, bf16[384,1728]{0,1:T(8,128)(2,1)} %get-tuple-element.86, bf16[384,1728]{0,1:T(8,128)(2,1)} %get-tuple-element.89, bf16[384,1536]{1,0:T(8,128)(2,1)S(1)} %copy-done.64, ...), kind=kOutput, calls=%fused_computation.2 | convolution fusion | flops 8196489216 | bytes 15335424 | tf_op jit(solution)/shard_map/dot_general | solution.py:65
  719.6 14.4 %convolution_convert_fusion.2 = bf16[1536,1728]{1,0:T(8,128)(2,1)} fusion(bf16[384,1728]{0,1:T(8,128)(2,1)} %get-tuple-element.96, bf16[384,1728]{0,1:T(8,128)(2,1)} %copy-done.71, bf16[384,1728]{0,1:T(8,128)(2,1)} %copy-done.70, bf16[384,1728]{0,1:T(8,128)(2,1)} %copy-done.69, bf16[384,1536]{1,0:T(8,128)(2,1)S(1)} %copy-done.64, ...), kind=kOutput, calls=%fused_computation.3 | convolution fusion | flops 8196489216 | bytes 15335424 | tf_op jit(solution)/shard_map/dot_general | solution.py:65
  736.3 14.5 %convolution_convert_fusion = bf16[1536,1728]{1,0:T(8,128)(2,1)} fusion(bf16[384,1728]{0,1:T(8,128)(2,1)} %get-tuple-element.97, bf16[384,1728]{0,1:T(8,128)(2,1)} %get-tuple-element.94, bf16[384,1728]{0,1:T(8,128)(2,1)S(1)} %copy-done.73, bf16[384,1728]{0,1:T(8,128)(2,1)S(1)} %copy-done.68, bf16[384,1536]{1,0:T(8,128)(2,1)} %collective-permute-done.13, ...), kind=kOutput, calls=%fused_computation.1 | convolution fusion | flops 8196489216 | bytes 15335424 | tf_op jit(solution)/shard_map/dot_general | solution.py:65
  758.0 22.6 %attn_backward.1 = (f32[384,1536]{1,0:T(8,128)}, f32[2,384,512]{2,1,0:T(8,128)}, bf16[2,384,512]{2,1,0:T(8,128)(2,1)}, bf16[2,384,512]{2,1,0:T(8,128)(2,1)}, bf16[2,384,512]{2,1,0:T(8,128)(2,1)}) custom-call(s32[2]{0:T(128)} %copy-done.5, bf16[384,1536]{1,0:T(8,128)(2,1)} %copy-done, bf16[2,384,512]{2,1,0:T(8,128)(2,1)} %copy-done.1, ...), custom_call_target="tpu_custom_call" | custom-call | flops 36238786560 | bytes 11796480 | tf_op jit(solution)/shard_map/attn_backward/pallas_call | solution.py:220
  796.6 7.5 multiply_reduce_fusion
  817.5 22.0 %collective-permute-done.15 = bf16[2,384,512]{2,1,0:T(8,128)(2,1)} collective-permute-done((bf16[2,384,512]{2,1,0:T(8,128)(2,1)}, bf16[2,384,512]{2,1,0:T(8,128)(2,1)}, u32[]{:S(2)}, u32[]{:S(2)}) %collective-permute-start.15) | collective-permute-done | bytes 786464 | tf_op jit(solution)/shard_map/ppermute | solution.py:282
  839.5 59.4 %collective-permute-done.16 = bf16[2,384,512]{2,1,0:T(8,128)(2,1)} collective-permute-done((bf16[2,384,512]{2,1,0:T(8,128)(2,1)}, bf16[2,384,512]{2,1,0:T(8,128)(2,1)}, u32[]{:S(2)}, u32[]{:S(2)}) %collective-permute-start.16) | collective-permute-done | bytes 786464 | tf_op jit(solution)/shard_map/ppermute | solution.py:282
  928.5 11.2 copy.107
  956.5 59.3 %reduce-scatter.14.cloned.1.call-done = bf16[192,1728]{1,0:T(8,128)(2,1)} async-done(((bf16[1536,1728]{1,0:T(8,128)(2,1)}), bf16[192,1728]{1,0:T(8,128)(2,1)}) %reduce-scatter.14.cloned.1.call-update) | async-done | bytes 663568 | tf_op jit(solution)/shard_map/reduce_scatter | solution.py:288
  1018.1 133.8 %reduce-scatter.16.cloned.1.call-done = bf16[48,2688]{1,0:T(8,128)(2,1)} async-done(((bf16[1536,2688]{1,0:T(8,128)(2,1)}), bf16[48,2688]{1,0:T(8,128)(2,1)}) %reduce-scatter.16.cloned.1.call-update) | async-done | bytes 258064
  (357 shorter events, 234.4 us)
Async XLA Ops:
  7.2 106.9 %all-gather.7.cloned.1.call-start = ((), (), s32[]{:S(2)}) async-start(), calls=%async_computation.5 | async-start | bytes 3649536 | tf_op jit(solution)/shard_map/all_gather | solution.py:285
  10.3 179.8 %all-gather.9.cloned.1.call-start = ((), (), s32[]{:S(2)}) async-start(), calls=%async_computation.6 | async-start | bytes 4866048 | tf_op jit(solution)/shard_map/all_gather | solution.py:285
  11.0 297.8 %all-gather.11.cloned.1.call-start = ((), (), s32[]{:S(2)}) async-start(), calls=%async_computation.7 | async-start | bytes 4866048 | tf_op jit(solution)/shard_map/all_gather | solution.py:285
  11.8 340.1 %all-gather.13.cloned.1.call-start = ((), (), s32[]{:S(2)}) async-start(), calls=%async_computation.8 | async-start | bytes 6193152 | tf_op jit(solution)/shard_map/all_gather | solution.py:285
  12.4 383.5 %all-gather.15.cloned.1.call-start = ((), (), s32[]{:S(2)}) async-start(), calls=%async_computation.9 | async-start | bytes 6193152 | tf_op jit(solution)/shard_map/all_gather | solution.py:285
  12.9 426.9 %all-gather.17.cloned.1.call-start = ((), (), s32[]{:S(2)}) async-start(), calls=%async_computation.10 | async-start | bytes 6193152 | tf_op jit(solution)/shard_map/all_gather | solution.py:285
  15.0 458.1 %collective-permute-start.9 = (bf16[384,1536]{1,0:T(8,128)(2,1)}, bf16[384,1536]{1,0:T(8,128)(2,1)}, u32[]{:S(2)}, u32[]{:S(2)}) collective-permute-start(bf16[384,1536]{1,0:T(8,128)(2,1)} %fusion.49), channel_id=1, source_target_pairs={{0,1},{1,0},{2,3},{3,2},{4,5},{5,4},{6,7},{7,6},{8,9},{9,8},{10,11... | collective-permute-start | bytes 3538952 | tf_op jit(solution)/shard_map/ppermute | solution.py:276
  18.0 481.3 %collective-permute-start.11 = (bf16[384,1536]{1,0:T(8,128)(2,1)}, bf16[384,1536]{1,0:T(8,128)(2,1)}, u32[]{:S(2)}, u32[]{:S(2)}) collective-permute-start(bf16[384,1536]{1,0:T(8,128)(2,1)} %fusion.49), channel_id=1, source_target_pairs={{0,2},{1,3},{2,0},{3,1},{4,6},{5,7},{6,4},{7,5},{8,10},{9,11},{10,... | collective-permute-start | bytes 3538952 | tf_op jit(solution)/shard_map/ppermute | solution.py:276
  20.6 924.8 %reduce-scatter.8.cloned.1.call-start = ((), (), s32[]{:S(2)}) async-start(), calls=%async_computation.11 | async-start | bytes 4866048 | tf_op jit(solution)/shard_map/reduce_scatter | solution.py:288
  21.0 169.1 %copy-start.55 = (f32[384]{0:T(512)}, f32[384]{0:T(512)S(1)}, u32[]{:S(2)}) copy-start(f32[384]{0:T(512)S(1)} %add_rsqrt_fusion.3) | copy-start | bytes 4612
  21.3 181.1 %copy-start.35 = (f32[384,64]{0,1:T(8,128)}, f32[384,64]{0,1:T(8,128)S(1)}, u32[]{:S(2)}) copy-start(f32[384,64]{0,1:T(8,128)S(1)} %get-tuple-element.124) | copy-start | bytes 294916
  25.0 219.5 %copy-start.5 = (s32[2]{0:T(128)}, s32[2]{0:T(128)S(1)}, u32[]{:S(2)}) copy-start(s32[2]{0:T(128)S(1)} %pad_add_fusion.where_ref) | copy-start | bytes 28
  130.8 87.3 %collective-permute-start = (bf16[2,384,512]{2,1,0:T(8,128)(2,1)S(1)}, bf16[2,384,512]{2,1,0:T(8,128)(2,1)S(1)}, u32[]{:S(2)}, u32[]{:S(2)}) collective-permute-start(bf16[2,384,512]{2,1,0:T(8,128)(2,1)S(1)} %pad_maximum_fusion.5.refs_0_), channel_id=1, source_target_pairs={{0,1},{1,2},{2,3},{4,5},{5,6},{6,7},{8,9},{9,10},{10,11},{12,13},{... | collective-permute-start | bytes 2359304 | tf_op jit(solution)/shard_map/ppermute | solution.py:279
  133.8 110.7 %collective-permute-start.1 = (bf16[2,384,512]{2,1,0:T(8,128)(2,1)S(1)}, bf16[2,384,512]{2,1,0:T(8,128)(2,1)S(1)}, u32[]{:S(2)}, u32[]{:S(2)}) collective-permute-start(bf16[2,384,512]{2,1,0:T(8,128)(2,1)S(1)} %pad_maximum_fusion.5.refs_0_), channel_id=1, source_target_pairs={{0,2},{1,3},{4,6},{5,7},{8,10},{9,11},{12,14},{13,15},{16,18},{17,... | collective-permute-start | bytes 2359304 | tf_op jit(solution)/shard_map/ppermute | solution.py:279
  137.4 107.1 %collective-permute-start.2 = (bf16[2,384,512]{2,1,0:T(8,128)(2,1)S(1)}, bf16[2,384,512]{2,1,0:T(8,128)(2,1)S(1)}, u32[]{:S(2)}, u32[]{:S(2)}) collective-permute-start(bf16[2,384,512]{2,1,0:T(8,128)(2,1)S(1)} %pad_maximum_fusion.5.refs_0_), channel_id=1, source_target_pairs={{0,3},{4,7},{8,11},{12,15},{16,19},{20,23},{24,27},{28,31}} | collective-permute-start | bytes 2359304 | tf_op jit(solution)/shard_map/ppermute | solution.py:279
  218.1 306.4 %collective-permute-start.13 = (bf16[384,1536]{1,0:T(8,128)(2,1)}, bf16[384,1536]{1,0:T(8,128)(2,1)}, u32[]{:S(2)}, u32[]{:S(2)}) collective-permute-start(bf16[384,1536]{1,0:T(8,128)(2,1)} %fusion.49), channel_id=1, source_target_pairs={{0,3},{1,2},{2,1},{3,0},{4,7},{5,6},{6,5},{7,4},{8,11},{9,10},{10,... | collective-permute-start | bytes 3538952 | tf_op jit(solution)/shard_map/ppermute | solution.py:276
  314.3 145.3 %collective-permute-start.3 = (bf16[384,1536]{1,0:T(8,128)(2,1)S(1)}, bf16[384,1536]{1,0:T(8,128)(2,1)}, u32[]{:S(2)}, u32[]{:S(2)}) collective-permute-start(bf16[384,1536]{1,0:T(8,128)(2,1)S(1)} %multiply_convert_fusion.13), channel_id=1, source_target_pairs={{0,1},{1,0},{2,3},{3,2},{4,5},{5,4},{6,7},{7,6},{8,9},{9,8},{10,11... | collective-permute-start | bytes 3538952 | tf_op jit(solution)/shard_map/ppermute | solution.py:276
  314.3 173.1 %collective-permute-start.5 = (bf16[384,1536]{1,0:T(8,128)(2,1)S(1)}, bf16[384,1536]{1,0:T(8,128)(2,1)}, u32[]{:S(2)}, u32[]{:S(2)}) collective-permute-start(bf16[384,1536]{1,0:T(8,128)(2,1)S(1)} %multiply_convert_fusion.13), channel_id=1, source_target_pairs={{0,2},{1,3},{2,0},{3,1},{4,6},{5,7},{6,4},{7,5},{8,10},{9,11},{10,... | collective-permute-start | bytes 3538952 | tf_op jit(solution)/shard_map/ppermute | solution.py:276
  459.6 55.6 %collective-permute-start.7 = (bf16[384,1536]{1,0:T(8,128)(2,1)S(1)}, bf16[384,1536]{1,0:T(8,128)(2,1)S(1)}, u32[]{:S(2)}, u32[]{:S(2)}) collective-permute-start(bf16[384,1536]{1,0:T(8,128)(2,1)S(1)} %multiply_convert_fusion.13), channel_id=1, source_target_pairs={{0,3},{1,2},{2,1},{3,0},{4,7},{5,6},{6,5},{7,4},{8,11},{9,10},{10,... | collective-permute-start | bytes 3538952 | tf_op jit(solution)/shard_map/ppermute | solution.py:276
  487.4 68.3 %collective-permute-start.10 = (bf16[384,1536]{1,0:T(8,128)(2,1)S(1)}, bf16[384,1536]{1,0:T(8,128)(2,1)S(1)}, u32[]{:S(2)}, u32[]{:S(2)}) collective-permute-start(bf16[384,1536]{1,0:T(8,128)(2,1)S(1)} %fusion.32), channel_id=1, source_target_pairs={{0,1},{1,0},{2,3},{3,2},{4,5},{5,4},{6,7},{7,6},{8,9},{9,8},{10,11... | collective-permute-start | bytes 3538952 | tf_op jit(solution)/shard_map/ppermute | solution.py:276
  514.1 80.4 %collective-permute-start.12 = (bf16[384,1536]{1,0:T(8,128)(2,1)S(1)}, bf16[384,1536]{1,0:T(8,128)(2,1)S(1)}, u32[]{:S(2)}, u32[]{:S(2)}) collective-permute-start(bf16[384,1536]{1,0:T(8,128)(2,1)S(1)} %fusion.33), channel_id=1, source_target_pairs={{0,2},{1,3},{2,0},{3,1},{4,6},{5,7},{6,4},{7,5},{8,10},{9,11},{10,... | collective-permute-start | bytes 3538952 | tf_op jit(solution)/shard_map/ppermute | solution.py:276
  542.7 51.8 %collective-permute-start.14 = (bf16[384,1536]{1,0:T(8,128)(2,1)S(1)}, bf16[384,1536]{1,0:T(8,128)(2,1)S(1)}, u32[]{:S(2)}, u32[]{:S(2)}) collective-permute-start(bf16[384,1536]{1,0:T(8,128)(2,1)S(1)} %fusion.34), channel_id=1, source_target_pairs={{0,3},{1,2},{2,1},{3,0},{4,7},{5,6},{6,5},{7,4},{8,11},{9,10},{10,... | collective-permute-start | bytes 3538952 | tf_op jit(solution)/shard_map/ppermute | solution.py:276
  548.7 70.0 %collective-permute-start.4 = (bf16[384,1536]{1,0:T(8,128)(2,1)S(1)}, bf16[384,1536]{1,0:T(8,128)(2,1)S(1)}, u32[]{:S(2)}, u32[]{:S(2)}) collective-permute-start(bf16[384,1536]{1,0:T(8,128)(2,1)S(1)} %convolution_convert_fusion.9), channel_id=1, source_target_pairs={{0,1},{1,0},{2,3},{3,2},{4,5},{5,4},{6,7},{7,6},{8,9},{9,8},{10,11... | collective-permute-start | bytes 3538952 | tf_op jit(solution)/shard_map/ppermute | solution.py:276
  551.3 144.3 %collective-permute-start.6 = (bf16[384,1536]{1,0:T(8,128)(2,1)S(1)}, bf16[384,1536]{1,0:T(8,128)(2,1)S(1)}, u32[]{:S(2)}, u32[]{:S(2)}) collective-permute-start(bf16[384,1536]{1,0:T(8,128)(2,1)S(1)} %convolution_convert_fusion.8), channel_id=1, source_target_pairs={{0,2},{1,3},{2,0},{3,1},{4,6},{5,7},{6,4},{7,5},{8,10},{9,11},{10,... | collective-permute-start | bytes 3538952 | tf_op jit(solution)/shard_map/ppermute | solution.py:276
  555.8 139.9 %collective-permute-start.8 = (bf16[384,1536]{1,0:T(8,128)(2,1)}, bf16[384,1536]{1,0:T(8,128)(2,1)S(1)}, u32[]{:S(2)}, u32[]{:S(2)}) collective-permute-start(bf16[384,1536]{1,0:T(8,128)(2,1)} %convolution_convert_fusion.7), channel_id=1, source_target_pairs={{0,3},{1,2},{2,1},{3,0},{4,7},{5,6},{6,5},{7,4},{8,11},{9,10},{10,... | collective-permute-start | bytes 3538952 | tf_op jit(solution)/shard_map/ppermute | solution.py:276
  703.5 243.6 %reduce-scatter.12.cloned.1.call-start = ((), (), s32[]{:S(2)}) async-start(), calls=%async_computation.13 | async-start | bytes 6193152 | tf_op jit(solution)/shard_map/reduce_scatter | solution.py:288
  719.1 235.1 %reduce-scatter.10.cloned.1.call-start = ((), (), s32[]{:S(2)}) async-start(), calls=%async_computation.12 | async-start | bytes 6193152 | tf_op jit(solution)/shard_map/reduce_scatter | solution.py:288
  734.0 281.8 %reduce-scatter.14.cloned.1.call-start = ((), (), s32[]{:S(2)}) async-start(), calls=%async_computation.14 | async-start | bytes 6193152 | tf_op jit(solution)/shard_map/reduce_scatter | solution.py:288
  750.8 401.1 %reduce-scatter.16.cloned.1.call-start = ((), (), s32[]{:S(2)}) async-start(), calls=%async_computation.15 | async-start | bytes 8515584
  780.6 58.9 %collective-permute-start.15 = (bf16[2,384,512]{2,1,0:T(8,128)(2,1)}, bf16[2,384,512]{2,1,0:T(8,128)(2,1)}, u32[]{:S(2)}, u32[]{:S(2)}) collective-permute-start(bf16[2,384,512]{2,1,0:T(8,128)(2,1)} %get-tuple-element.23), channel_id=1, source_target_pairs={{1,0},{2,1},{3,2},{5,4},{6,5},{7,6},{9,8},{10,9},{11,10},{13,12},{... | collective-permute-start | bytes 2359304 | tf_op jit(solution)/shard_map/ppermute | solution.py:282
  781.9 117.0 %collective-permute-start.16 = (bf16[2,384,512]{2,1,0:T(8,128)(2,1)}, bf16[2,384,512]{2,1,0:T(8,128)(2,1)}, u32[]{:S(2)}, u32[]{:S(2)}) collective-permute-start(bf16[2,384,512]{2,1,0:T(8,128)(2,1)} %get-tuple-element.24), channel_id=1, source_target_pairs={{2,0},{3,1},{6,4},{7,5},{10,8},{11,9},{14,12},{15,13},{18,16},{19,... | collective-permute-start | bytes 2359304 | tf_op jit(solution)/shard_map/ppermute | solution.py:282
  783.4 115.5 %collective-permute-start.17 = (bf16[2,384,512]{2,1,0:T(8,128)(2,1)}, bf16[2,384,512]{2,1,0:T(8,128)(2,1)}, u32[]{:S(2)}, u32[]{:S(2)}) collective-permute-start(bf16[2,384,512]{2,1,0:T(8,128)(2,1)} %get-tuple-element.25), channel_id=1, source_target_pairs={{3,0},{7,4},{11,8},{15,12},{19,16},{23,20},{27,24},{31,28}} | collective-permute-start | bytes 2359304 | tf_op jit(solution)/shard_map/ppermute | solution.py:282
  (81 other events, 1055.5 us)
Sparse Core Ops, SparseCore 0:
  11.4 102.6 all-gather.6
  116.9 73.1 all-gather.8
  192.9 115.8 all-gather.10
  310.6 41.2 all-gather.12
  353.6 42.2 all-gather.14
  397.6 42.2 all-gather.16
  703.6 128.7 reduce-scatter.7
  836.2 56.6 reduce-scatter.11
  896.4 57.7 reduce-scatter.9
  957.9 57.8 reduce-scatter.13
  1021.7 130.1 reduce-scatter.15

commit v2 on v1

--- a/solution.py
+++ b/solution.py
@@ -23,6 +23,7 @@
 
 NT = (((1,), (1,)), ((), ()))
 NN = (((1,), (0,)), ((), ()))
+TN = (((0,), (0,)), ((), ()))
 
 
 def rms_scale(values, gain_vec):
@@ -63,6 +64,259 @@
 
 def mdot(a, b, dims=NN):
     return lax.dot_general(a, b, dims, preferred_element_type=f32)
+
+
+ANY = pl.BlockSpec(memory_space=pl.ANY)
+
+
+def remote(src, dst, send, recv, dp, ctx):
+    return pltpu.make_async_remote_copy(
+        src_ref=src,
+        dst_ref=dst,
+        send_sem=send,
+        recv_sem=recv,
+        device_id=(dp, ctx),
+        device_id_type=pl.DeviceIdType.MESH,
+    )
+
+
+def greet(dp, ctx, near, far):
+    barrier = pltpu.get_barrier_semaphore()
+    partners = [(dp ^ r, ctx) for r in near] + [(dp, ctx ^ s) for s in far]
+    for partner in partners:
+        pl.semaphore_signal(
+            barrier, inc=1, device_id=partner, device_id_type=pl.DeviceIdType.MESH
+        )
+    pl.semaphore_wait(barrier, len(partners))
+
+
+def gather_kernel(parts, riders, *refs):
+    srcs, riding = refs[:parts], refs[parts : parts + riders]
+    outs, landed = refs[parts + riders : 2 * parts + riders], refs[2 * parts + riders :][:riders]
+    own_sem, send, recv, ride_send, ride_recv = refs[2 * parts + 2 * riders :]
+    dp, ctx = lax.axis_index("dp"), lax.axis_index("ctx")
+    greet(dp, ctx, (1, 2, 4), (1, 2, 3))
+
+    def ride(i):
+        return remote(riding[i], landed[i], ride_send.at[i], ride_recv.at[i], dp, ctx ^ 1)
+
+    def line(p, s):
+        return remote(
+            srcs[p], outs[p].at[dp, ctx], send.at[p, s - 1], recv.at[p, s - 1], dp, ctx ^ s
+        )
+
+    def plane(p, way):
+        return remote(
+            outs[p].at[dp], outs[p].at[dp], send.at[p, 3 + way], recv.at[p, 3 + way],
+            dp ^ (2 << way), ctx,
+        )
+
+    def corner(p, way):
+        block = outs[p].at[dp ^ (2 << (1 - way)), pl.ds(2 * way, 2)]
+        return remote(block, block, send.at[p, 5 + way], recv.at[p, 5 + way], dp ^ (2 << way), ctx)
+
+    def across(p, k):
+        block = outs[p].at[dp ^ (2 * k)]
+        return remote(block, block, send.at[p, 7 + k], recv.at[p, 7 + k], dp ^ 1, ctx)
+
+    def own(p):
+        return pltpu.make_async_copy(srcs[p], outs[p].at[dp, ctx], own_sem.at[p])
+
+    for p in range(parts):
+        own(p).start()
+        for s in (1, 2, 3):
+            line(p, s).start()
+    for i in range(riders):
+        ride(i).start()
+    for step in range(parts + 2):
+        if step < parts:
+            p = step
+            own(p).wait()
+            for s in (1, 2, 3):
+                line(p, s).wait_recv()
+            for way in (0, 1):
+                plane(p, way).start()
+            across(p, 0).start()
+        if 0 <= step - 1 < parts:
+            p = step - 1
+            for way in (0, 1):
+                plane(p, way).wait_recv()
+            for way in (0, 1):
+                corner(p, way).start()
+            for k in (1, 2):
+                across(p, k).start()
+        if 0 <= step - 2 < parts:
+            p = step - 2
+            for way in (0, 1):
+                corner(p, way).wait_recv()
+            across(p, 3).start()
+    for p in range(parts):
+        for s in (1, 2, 3):
+            line(p, s).wait_send()
+        for way in (0, 1):
+            plane(p, way).wait_send()
+            corner(p, way).wait_send()
+        for k in range(4):
+            across(p, k).wait_send()
+            across(p, k).wait_recv()
+    for i in range(riders):
+        ride(i).wait()
+
+
+def gather_all(shards, riding, cid):
+    parts, riders = len(shards), len(riding)
+    outs = pl.pallas_call(
+        functools.partial(gather_kernel, parts, riders),
+        in_specs=[ANY] * (parts + riders),
+        out_specs=[ANY] * (parts + riders),
+        out_shape=[jax.ShapeDtypeStruct((8, 4) + s.shape, s.dtype) for s in shards]
+        + [jax.ShapeDtypeStruct(s.shape, s.dtype) for s in riding],
+        scratch_shapes=[
+            pltpu.SemaphoreType.DMA((parts,)),
+            pltpu.SemaphoreType.DMA((parts, 11)),
+            pltpu.SemaphoreType.DMA((parts, 11)),
+            pltpu.SemaphoreType.DMA((max(riders, 1),)),
+            pltpu.SemaphoreType.DMA((max(riders, 1),)),
+        ],
+        compiler_params=pltpu.CompilerParams(collective_id=cid, has_side_effects=True),
+        name="gather_all",
+    )(*shards, *riding)
+    full = [o.reshape(32 * s.shape[0], s.shape[1]) for o, s in zip(outs, shards)]
+    return full + list(outs[parts:])
+
+
+def sum_kernel(parts, *refs):
+    ins, outs = refs[:parts], refs[parts : 2 * parts]
+    keep = refs[2 * parts : 3 * parts]
+    got = refs[3 * parts : 4 * parts]
+    plane1 = refs[4 * parts : 5 * parts]
+    plane2 = refs[5 * parts : 6 * parts]
+    lines = refs[6 * parts : 7 * parts]
+    load, send, recv = refs[7 * parts :]
+    dp, ctx = lax.axis_index("dp"), lax.axis_index("ctx")
+    chip = dp // 2
+    core = dp - 2 * chip
+
+    halves = (pl.ds(0, 2), pl.ds(2, 2))
+
+    def fetch(p, k):
+        return pltpu.make_async_copy(
+            ins[p].at[2 * (chip ^ k) + core], keep[p].at[k], load.at[p, k]
+        )
+
+    def across(p, k):
+        return remote(
+            ins[p].at[2 * (chip ^ k) + (1 - core)], got[p].at[k],
+            send.at[p, k], recv.at[p, k], dp ^ 1, ctx,
+        )
+
+    def first(p, w, i):
+        k = (1 << w) if i == 0 else 3
+        return remote(
+            keep[p].at[k, halves[w]], plane1[p].at[i, halves[w]],
+            send.at[p, 4 + 2 * w + i], recv.at[p, 4 + 2 * w + i], dp ^ (2 << w), ctx,
+        )
+
+    def second(p, w):
+        k = 1 << (1 - w)
+        return remote(
+            keep[p].at[k, halves[w]], plane2[p].at[halves[w]],
+            send.at[p, 8 + w], recv.at[p, 8 + w], dp ^ (2 << (1 - w)), ctx,
+        )
+
+    def line(p, s):
+        return remote(
+            keep[p].at[0, ctx ^ s], lines[p].at[s - 1],
+            send.at[p, 9 + s], recv.at[p, 9 + s], dp, ctx ^ s,
+        )
+
+    for p in range(parts):
+        for k in (3, 1, 2, 0):
+            fetch(p, k).start()
+    greet(dp, ctx, (1, 2, 4), (1, 2, 3))
+    for p in range(parts):
+        for k in (3, 1, 2, 0):
+            across(p, k).start()
+
+    def add(target, term):
+        target[...] = (target[...].astype(f32) + term[...].astype(f32)).astype(bf16)
+
+    for step in range(parts + 3):
+        if step < parts:
+            p = step
+            for k in (3, 1, 2, 0):
+                fetch(p, k).wait()
+                across(p, k).wait_recv()
+                for c in range(4):
+                    add(keep[p].at[k, c], got[p].at[k, c])
+                if k == 3:
+                    for w in (0, 1):
+                        first(p, w, 1).start()
+                elif k:
+                    first(p, k - 1, 0).start()
+        if 0 <= step - 1 < parts:
+            p = step - 1
+            for w in (0, 1):
+                first(p, w, 1).wait_recv()
+                other = 1 << (1 - w)
+                for c in (2 * w, 2 * w + 1):
+                    add(keep[p].at[other, c], plane1[p].at[1, c])
+                second(p, w).start()
+            for w in (0, 1):
+                first(p, w, 0).wait_recv()
+                for c in (2 * w, 2 * w + 1):
+                    add(keep[p].at[0, c], plane1[p].at[0, c])
+        if 0 <= step - 2 < parts:
+            p = step - 2
+            for w in (0, 1):
+                second(p, w).wait_recv()
+                for c in (2 * w, 2 * w + 1):
+                    add(keep[p].at[0, c], plane2[p].at[c])
+            for s in (3, 2, 1):
+                line(p, s).start()
+        if 0 <= step - 3 < parts:
+            p = step - 3
+            for s in (1, 2, 3):
+                line(p, s).wait_recv()
+            total = keep[p][0, ctx].astype(f32)
+            for s in (1, 2, 3):
+                total = total + lines[p][s - 1].astype(f32)
+            outs[p][...] = total
+    for p in range(parts):
+        for k in range(4):
+            across(p, k).wait_send()
+        for w in (0, 1):
+            for i in (0, 1):
+                first(p, w, i).wait_send()
+            second(p, w).wait_send()
+        for s in (1, 2, 3):
+            line(p, s).wait_send()
+
+
+def sum_all(terms, cid):
+    parts = len(terms)
+    blocks = [t.reshape(8, 4, t.shape[0] // 32, t.shape[1]) for t in terms]
+    shapes = [b.shape[2:] for b in blocks]
+
+    def per(lead):
+        return [pltpu.VMEM(lead + s, bf16) for s in shapes]
+
+    return pl.pallas_call(
+        functools.partial(sum_kernel, parts),
+        in_specs=[ANY] * parts,
+        out_specs=[pl.BlockSpec(memory_space=pltpu.VMEM)] * parts,
+        out_shape=[jax.ShapeDtypeStruct(s, f32) for s in shapes],
+        scratch_shapes=per((4, 4)) + per((4, 4)) + per((2, 4)) + per((4,)) + per((3,))
+        + [
+            pltpu.SemaphoreType.DMA((parts, 4)),
+            pltpu.SemaphoreType.DMA((parts, 13)),
+            pltpu.SemaphoreType.DMA((parts, 13)),
+        ],
+        compiler_params=pltpu.CompilerParams(
+            collective_id=cid, has_side_effects=True, vmem_limit_bytes=48 * 2**20
+        ),
+        name="sum_all",
+    )(*blocks)
 
 
 def causal_mask(rows, limit, key_axis):
@@ -205,11 +459,6 @@
             jax.ShapeDtypeStruct((PAIRS, 8, rows), f32),
         ],
         compiler_params=pltpu.CompilerParams(vmem_limit_bytes=48 * 2**20),
-        cost_estimate=pl.CostEstimate(
-            flops=16 * H * rows * rows * blocks * HD,
-            bytes_accessed=8 * rows * H * HD,
-            transcendentals=H * rows * rows * blocks,
-        ),
         name="attn_forward",
     )(where, query, *kv_blocks)
 
@@ -235,13 +484,206 @@
         out_shape=[jax.ShapeDtypeStruct((rows, H * HD), f32)]
         + [jax.ShapeDtypeStruct((2, rows, KVH * HD), kind) for kind in kinds],
         compiler_params=pltpu.CompilerParams(vmem_limit_bytes=56 * 2**20),
-        cost_estimate=pl.CostEstimate(
-            flops=40 * H * rows * rows * blocks * HD,
-            bytes_accessed=20 * rows * H * HD,
-            transcendentals=H * rows * rows * blocks,
-        ),
         name="attn_backward",
     )(where, query, *kv_blocks, grad, mixed, logs)
+
+
+def feed_forward_kernel(dp_blocks, *refs):
+    mid_hbm, gate_hbm, up_hbm, down_hbm = refs[:4]
+    ups_hbm = refs[4:8]
+    grad_ref, parts_hbm, dw_hbm = refs[8:11]
+    mids, ups, w_gate, w_up, w_down, act, grad_g, grad_u, to_send, received, staged = refs[11:22]
+    load, store, out_sem, send, recv = refs[22:]
+    rows, width = mid_hbm.shape
+    hidden = gate_hbm.shape[1]
+    share = width // dp_blocks
+    tile, whole = 256, hidden // 256
+    dp, ctx = lax.axis_index("dp"), lax.axis_index("ctx")
+    middle = (ctx == 1) | (ctx == 2)
+
+    def slot(ref, r):
+        return ref.at[pl.ds(pl.multiple_of(r * rows, rows), rows)]
+
+    def give(r):
+        return remote(mid_hbm, slot(mids, r), send.at[r], recv.at[r], dp, ctx ^ r)
+
+    relay = remote(slot(mids, 2), slot(mids, 3), send.at[0], recv.at[3], dp, ctx ^ 1)
+
+    def back(r):
+        return remote(
+            to_send.at[r - 1], received.at[r - 1], send.at[3 + r], recv.at[3 + r], dp, ctx ^ r
+        )
+
+    def load_ups(r, source):
+        return pltpu.make_async_copy(source, slot(ups, r), load.at[r])
+
+    own = pltpu.make_async_copy(mid_hbm, slot(mids, 0), load.at[4])
+    weights = [
+        pltpu.make_async_copy(source, target, load.at[5 + i])
+        for i, (source, target) in enumerate(
+            ((gate_hbm, w_gate), (up_hbm, w_up), (down_hbm, w_down))
+        )
+    ]
+
+    def put_down(r):
+        return pltpu.make_async_copy(
+            staged.at[lax.rem(r, 2)], parts_hbm.at[ctx ^ r], store.at[lax.rem(r, 2)]
+        )
+
+    own.start()
+    for copy in weights:
+        copy.start()
+    for r in range(4):
+        load_ups(r, ups_hbm[r]).start()
+    greet(dp, ctx, (), (1, 2, 3))
+    give(1).start()
+    give(2).start()
+
+    @pl.when(middle)
+    def _():
+        give(3).start()
+
+    own.wait()
+    for copy in weights:
+        copy.wait()
+
+    def block(r, carry):
+        @pl.when(r > 0)
+        def _():
+            give(r).wait_recv()
+
+        @pl.when((r == 2) & middle)
+        def _():
+            relay.start()
+
+        load_ups(r, mid_hbm).wait()
+        here = pl.ds(pl.multiple_of(r * rows, rows), rows)
+
+        def activate(cols):
+            value, upper = mids[here, :], ups[here, :]
+            gate_proj = mdot(value, w_gate[:, cols])
+            up_proj = mdot(value, w_up[:, cols])
+            grad_activated = mdot(upper, w_down[:, cols])
+            gate_sigmoid = jax.nn.sigmoid(gate_proj)
+            silu_gate = gate_proj * gate_sigmoid
+            silu_slope = gate_sigmoid * (1.0 + gate_proj * (1.0 - gate_sigmoid))
+            act[here, cols] = (silu_gate * up_proj).astype(bf16)
+            grad_g[here, cols] = (grad_activated * up_proj * silu_slope).astype(bf16)
+            grad_u[here, cols] = (grad_activated * silu_gate).astype(bf16)
+
+        def one(t, carry):
+            activate(pl.ds(pl.multiple_of(t * tile, tile), tile))
+            return carry
+
+        lax.fori_loop(0, whole, one, 0)
+        if hidden % tile:
+            activate(pl.ds(whole * tile, hidden % tile))
+
+        @pl.when(r >= 2)
+        def _():
+            put_down(r).wait()
+
+        def two(t, carry):
+            cols = pl.ds(pl.multiple_of(t * tile, tile), tile)
+            term = mdot(grad_g[here, :], w_gate[cols, :], NT)
+            term += mdot(grad_u[here, :], w_up[cols, :], NT)
+
+            @pl.when(r == 0)
+            def _():
+                grad_ref[:, cols] = term
+
+            @pl.when(r > 0)
+            def _():
+                to_send[lax.max(r - 1, 0), :, cols] = term.astype(bf16)
+
+            staged[lax.rem(r, 2), :, cols] = mdot(act[here, :], w_down[cols, :], NT).astype(bf16)
+            return carry
+
+        lax.fori_loop(0, width // tile, two, 0)
+        put_down(r).start()
+
+        @pl.when(r > 0)
+        def _():
+            back(r).start()
+
+        return carry
+
+    lax.fori_loop(0, 4, block, 0)
+
+    step = 384
+    for i, (left, right, place) in enumerate(
+        ((mids, grad_g, w_gate), (mids, grad_u, w_up), (ups, act, w_down))
+    ):
+
+        def put(j):
+            return pltpu.make_async_copy(
+                place.at[pl.ds(pl.multiple_of(j * share, share), share)],
+                dw_hbm.at[j, i],
+                out_sem.at[i, j],
+            )
+
+        def three(t, carry):
+            cols = pl.ds(pl.multiple_of(t * step, step), step)
+            place[cols, :] = mdot(left[:, cols], right[...], TN).astype(bf16)
+            for k in range(step // share):
+                put(t * (step // share) + k).start()
+            return carry
+
+        lax.fori_loop(0, width // step, three, 0)
+
+    for r in (1, 2, 3):
+        back(r).wait_recv()
+        grad_ref[...] += received[r - 1].astype(f32)
+    for r in (1, 2, 3):
+        back(r).wait_send()
+    give(1).wait_send()
+    give(2).wait_send()
+
+    @pl.when(middle)
+    def _():
+        give(3).wait_send()
+        relay.wait_send()
+
+    for r in (2, 3):
+        put_down(r).wait()
+    for i, place in enumerate((w_gate, w_up, w_down)):
+        for j in range(dp_blocks):
+            pltpu.make_async_copy(
+                place.at[pl.ds(j * share, share)], dw_hbm.at[j, i], out_sem.at[i, j]
+            ).wait()
+
+
+def feed_forward(mid, ups, full_gate, full_up, full_down_t, dp_blocks, cid):
+    rows, width = mid.shape
+    hidden = full_gate.shape[1]
+    weight = pltpu.VMEM((width, hidden), bf16)
+    kept = pltpu.VMEM((4 * rows, hidden), bf16)
+    every_row = pltpu.VMEM((4 * rows, width), bf16)
+    return pl.pallas_call(
+        functools.partial(feed_forward_kernel, dp_blocks),
+        in_specs=[ANY] * 8,
+        out_specs=[pl.BlockSpec(memory_space=pltpu.VMEM), ANY, ANY],
+        out_shape=[
+            jax.ShapeDtypeStruct((rows, width), f32),
+            jax.ShapeDtypeStruct((4, rows, width), bf16),
+            jax.ShapeDtypeStruct((dp_blocks, 3, width // dp_blocks, hidden), bf16),
+        ],
+        scratch_shapes=[every_row, every_row, weight, weight, weight, kept, kept, kept]
+        + [
+            pltpu.VMEM((3, rows, width), bf16),
+            pltpu.VMEM((3, rows, width), bf16),
+            pltpu.VMEM((2, rows, width), bf16),
+            pltpu.SemaphoreType.DMA((8,)),
+            pltpu.SemaphoreType.DMA((2,)),
+            pltpu.SemaphoreType.DMA((3, dp_blocks)),
+            pltpu.SemaphoreType.DMA((7,)),
+            pltpu.SemaphoreType.DMA((7,)),
+        ],
+        compiler_params=pltpu.CompilerParams(
+            collective_id=cid, has_side_effects=True, vmem_limit_bytes=63 * 2**20
+        ),
+        name="feed_forward",
+    )(mid, full_gate, full_up, full_down_t, *ups)
 
 
 def shards(
@@ -268,56 +710,82 @@
     qk_share = qk_gains.shape[0]
     positions = mine * rows + jnp.arange(rows, dtype=jnp.int32)
     length = seq_lens[0]
-    valid_rows = (positions < length).astype(f32)[:, None]
     where = jnp.stack([mine.astype(jnp.int32), length - mine * rows])
     cosine_table, sine_table = rope_tables(positions, HD)
 
+    small = (lax.axis_size("dp"), ctx) == (8, 4)
+
+    def move(block, pairs):
+        return lax.ppermute(block, "ctx", pairs)
+
+    def lift(block):
+        one = move(block, [(0, 1), (1, 2), (2, 3)])
+        two = move(block, [(0, 2), (1, 3)])
+        return [block, one, two, move(block, [(0, 3)])]
+
+    def lower(terms):
+        relay = move(terms[3], [(3, 2)])
+        two = move((terms[2].astype(f32) + relay.astype(f32)).astype(bf16), [(2, 0), (3, 1)])
+        one = move(terms[1], [(1, 0), (2, 1), (3, 2)])
+        return terms[0].astype(f32) + one.astype(f32) + two.astype(f32)
+
+    def after(value, *others):
+        return lax.optimization_barrier((value, others))[0]
+
     def swap(block, r):
-        return lax.ppermute(block, "ctx", [(i, i ^ r) for i in range(ctx)])
-
-    def up(block, k):
-        return lax.ppermute(block, "ctx", [(i, i + k) for i in range(ctx - k)])
-
-    def down(block, k):
-        return lax.ppermute(block, "ctx", [(i + k, i) for i in range(ctx - k)])
-
-    def gather(block, axes):
-        return lax.all_gather(block, axes, axis=0, tiled=True)
-
-    def scatter(block, axes):
-        return lax.psum_scatter(block, axes, scatter_dimension=0, tiled=True)
+        return move(block, [(i, i ^ r) for i in range(ctx)])
+
+    def gather(blocks, riding, cid):
+        if small:
+            return gather_all(blocks, riding, cid)
+        full = [lax.all_gather(b, every, axis=0, tiled=True) for b in blocks]
+        return full + [swap(b, 1) for b in riding]
+
+    def collect(terms, cid):
+        if small:
+            return sum_all(terms, cid)
+        return [
+            lax.psum_scatter(t, every, scatter_dimension=0, tiled=True).astype(f32) for t in terms
+        ]
 
     extra = jnp.stack([gain_in, gain_mid, jnp.pad(qk_gains, (0, share - qk_share))], 1)
     extra = jnp.pad(extra, ((0, 0), (0, 125)))
-    full_kv = gather(jnp.concatenate([w_key, w_value, extra], 1), every)
+    valid_rows = (positions < length).astype(f32)[:, None]
+    upstream = grad_out.astype(f32) * valid_rows
+    upstream_low = upstream.astype(bf16)
+    full_kv, full_query, full_out_t, ups_near = gather(
+        [jnp.concatenate([w_key, w_value, extra], 1), w_query, w_out.T], [upstream_low], 1
+    )
     kv_width = 2 * KVH * HD
     full_extra = full_kv[:, kv_width:].astype(f32)
     full_gain_in, full_gain_mid = full_extra[:, 0], full_extra[:, 1]
     full_qk = full_extra[:, 2].reshape(world, share)[:, :qk_share].reshape(-1)
+    full_gate, full_up, full_down_t = (
+        lax.all_gather(after(w, full_kv), "dp", axis=0, tiled=True)
+        for w in (w_gate, w_up, w_down.T)
+    )
     full_kv = full_kv[:, :kv_width]
-    full_query = gather(w_query, every)
-    full_out_t = gather(w_out.T, every)
-    full_gate = gather(w_gate, "dp")
-    full_up = gather(w_up, "dp")
-    full_down_t = gather(w_down.T, "dp")
 
     inputs = tokens.astype(f32)
-    upstream = grad_out.astype(f32) * valid_rows
-    upstream_low = upstream.astype(bf16)
-    ups = [upstream_low] + [swap(upstream_low, r) for r in range(1, ctx)]
 
     normed_f, factor_in = rms_scale(inputs, full_gain_in)
     normed = normed_f.astype(bf16)
     kv_raw = mdot(normed, full_kv)
     key_raw = kv_raw[:, : KVH * HD].reshape(rows, KVH, HD)
     value_low = kv_raw[:, KVH * HD :].astype(bf16)
-    query_raw = mdot(normed, full_query).reshape(rows, H, HD)
     gain_query = full_qk[:HD]
     gain_key = full_qk[HD:]
     key_normed, factor_key = rms_scale(key_raw, gain_key)
     key_low = rotate(key_normed, cosine_table, sine_table).astype(bf16).reshape(rows, KVH * HD)
     kv_own = jnp.stack([key_low, value_low])
-    kv_blocks = [kv_own] + [up(kv_own, k) for k in range(1, ctx)]
+    kv_blocks = lift(kv_own)
+    far_low = after(upstream_low, kv_blocks)
+    ups_two = swap(far_low, 2)
+    ups_middle = move(far_low, [(1, 2), (2, 1)])
+    ups_ends = move(ups_two, [(2, 3), (1, 0)])
+    ups_three = jnp.where((mine == 1) | (mine == 2), ups_middle, ups_ends)
+    ups = [upstream_low, ups_near, ups_two, ups_three]
+    query_raw = mdot(normed, full_query).reshape(rows, H, HD)
     query_normed, factor_query = rms_scale(query_raw, gain_query)
     query_low = rotate(query_normed, cosine_table, sine_table).astype(bf16)
     query_low = (query_low * (HD**-0.5)).astype(bf16).reshape(rows, H * HD)
@@ -327,38 +795,15 @@
     normed_mid_f, factor_mid = rms_scale(hidden, full_gain_mid)
     normed_mid = normed_mid_f.astype(bf16)
 
-    mids = [normed_mid] + [swap(normed_mid, r) for r in range(1, ctx)]
-    kept = []
-    downs, grads_mid = [], []
-    for r in range(ctx):
-        gate_proj = mdot(mids[r], full_gate)
-        up_proj = mdot(mids[r], full_up)
-        grad_activated = mdot(ups[r], full_down_t)
-        gate_sigmoid = jax.nn.sigmoid(gate_proj)
-        silu_gate = gate_proj * gate_sigmoid
-        activated = (silu_gate * up_proj).astype(bf16)
-        silu_slope = gate_sigmoid * (1.0 + gate_proj * (1.0 - gate_sigmoid))
-        grad_gate = (grad_activated * up_proj * silu_slope).astype(bf16)
-        grad_up = (grad_activated * silu_gate).astype(bf16)
-        kept.append((activated, grad_gate, grad_up))
-        grad_term = mdot(grad_gate, full_gate, NT) + mdot(grad_up, full_up, NT)
-        down_term = mdot(activated, full_down_t, NT)
-        if r:
-            grad_term = swap(grad_term.astype(bf16), r).astype(f32)
-            down_term = swap(down_term.astype(bf16), r).astype(f32)
-        grads_mid.append(grad_term)
-        downs.append(down_term)
-    grad_mid_term = sum(grads_mid[1:], grads_mid[0])
-    output = (hidden + sum(downs[1:], downs[0])).astype(bf16)
-
-    TN = (((0,), (0,)), ((), ()))
-    all_mid = jnp.concatenate(mids, 0)
-    all_up = jnp.concatenate(ups, 0)
-    all_act, all_gg, all_gu = (jnp.concatenate([k[i] for k in kept], 0) for i in range(3))
-    grad_wgate = scatter(mdot(all_mid, all_gg, TN).astype(bf16), "dp").astype(f32)
-    grad_wup = scatter(mdot(all_mid, all_gu, TN).astype(bf16), "dp").astype(f32)
-    grad_wdown = scatter(mdot(all_up, all_act, TN).astype(bf16), "dp").astype(f32).T
-
+    grad_mid_term, down_parts, grad_ffn = feed_forward(
+        normed_mid, ups, full_gate, full_up, full_down_t, lax.axis_size("dp"), 2
+    )
+    grad_ffn = lax.psum_scatter(
+        grad_ffn.reshape(-1, grad_ffn.shape[-1]), "dp", scatter_dimension=0, tiled=True
+    )
+    down_parts = lax.psum_scatter(
+        down_parts.reshape(-1, width), "ctx", scatter_dimension=0, tiled=True
+    )
     grad_hidden_norm, gain_terms_mid = norm_back(grad_mid_term, hidden, factor_mid, full_gain_mid)
     grad_hidden = upstream + grad_hidden_norm
     grad_branch = grad_hidden.astype(bf16)
@@ -368,21 +813,19 @@
     grad_query_rot, grad_kv_own, *grad_kv_terms = attn_backward(
         where, query_low, kv_blocks, grad_mixed, mixed_low, logs
     )
-    grad_kv = grad_kv_own
-    for k in range(1, ctx):
-        grad_kv = grad_kv + down(grad_kv_terms[k - 1], k).astype(f32)
-
     grad_query_norm = rotate_back(grad_query_rot.reshape(rows, H, HD), cosine_table, sine_table)
     grad_query_raw, gain_terms_query = norm_back(
         grad_query_norm, query_raw, factor_query, gain_query
     )
+    grad_query_low = grad_query_raw.reshape(rows, H * HD).astype(bf16)
+    grad_wquery = mdot(normed, grad_query_low, TN).astype(bf16)
+    sum_query, grad_wout = collect([grad_wquery, grad_wout_t], 3)
+    grad_kv = lower([grad_kv_own] + grad_kv_terms)
     grad_key_norm = rotate_back(grad_kv[0].reshape(rows, KVH, HD), cosine_table, sine_table)
     grad_key_raw, gain_terms_key = norm_back(grad_key_norm, key_raw, factor_key, gain_key)
-    grad_query_low = grad_query_raw.reshape(rows, H * HD).astype(bf16)
     grad_kv_low = jnp.concatenate(
         [grad_key_raw.reshape(rows, KVH * HD).astype(bf16), grad_kv[1].astype(bf16)], 1
     )
-    grad_wquery = mdot(normed, grad_query_low, TN).astype(bf16)
     grad_wkv = mdot(normed, grad_kv_low, TN).astype(bf16)
     grad_normed = mdot(grad_query_low, full_query, NT) + mdot(grad_kv_low, full_kv, NT)
     grad_input_norm, gain_terms_in = norm_back(grad_normed, inputs, factor_in, full_gain_in)
@@ -395,19 +838,24 @@
         [jnp.sum(gain_terms_in, axis=0), jnp.sum(gain_terms_mid, axis=0), qk_column.reshape(-1)], 1
     )
     grad_extra = jnp.pad(grad_extra, ((0, 0), (0, 125))).astype(bf16)
-    grad_wout = scatter(grad_wout_t, every).astype(f32).T
-    grad_rest = scatter(jnp.concatenate([grad_wquery, grad_wkv, grad_extra], 1), every).astype(f32)
-    cuts = (H * HD, H * HD + KVH * HD, H * HD + 2 * KVH * HD)
+    (sum_kv,) = collect([after(jnp.concatenate([grad_wkv, grad_extra], 1), sum_query)], 4)
+    grad_ffn, down_parts = after((grad_ffn, down_parts), sum_kv)
+    output = (hidden + down_parts.astype(f32)).astype(bf16)
+    grad_wgate, grad_wup, grad_wdown = (
+        grad_ffn[i * w_gate.shape[0] : (i + 1) * w_gate.shape[0]].astype(f32) for i in range(3)
+    )
+    grad_wdown = grad_wdown.T
+    cuts = (KVH * HD, 2 * KVH * HD)
     return (
         output,
         grad_tokens,
-        grad_rest[:, cuts[2]],
-        grad_rest[:, : cuts[0]],
-        grad_rest[:, cuts[0] : cuts[1]],
-        grad_rest[:, cuts[1] : cuts[2]],
-        grad_wout,
-        grad_rest[:qk_share, cuts[2] + 2],
-        grad_rest[:, cuts[2] + 1],
+        sum_kv[:, cuts[1]],
+        sum_query,
+        sum_kv[:, : cuts[0]],
+        sum_kv[:, cuts[0] : cuts[1]],
+        grad_wout.T,
+        sum_kv[:qk_share, cuts[1] + 2],
+        sum_kv[:, cuts[1] + 1],
         grad_wgate,
         grad_wup,
         grad_wdown,

time: 1170 us -> 741 us (0.63)
  waiting for transfers between devices: 713 us -> 79.5 us
  Pallas kernels: 33.9 us -> 464 us
  matrix products: 213 us -> 36.2 us
  local copies, waits for them, and re-layouts: 72.4 us -> 51.6 us
  starting transfers between devices: 59.6 us -> 43.3 us
  other arithmetic: 55.7 us -> 42.7 us
    pallas_call x0 -> x4, Pallas kernels: none -> 430 us  [the longest x2 181 us: sum_all(): pl.pallas_call(functools.partial(sum_kernel, parts), in_specs=[ANY] * par...]
    all_gather x6 -> x3, waiting for transfers between devices: 300 us -> 0.01 us  [shards(): lax.all_gather(after(w, full_kv), 'dp', axis=0, tiled=True)]
    dot_general x36 -> x9, matrix products: 213 us -> 36.2 us  [mdot(): return lax.dot_general(a, b, dims, preferred_element_type=f32)]
    unnamed x12 -> x5, waiting for transfers between devices: 136 us -> 1.92 us
    ppermute x18 -> x9, waiting for transfers between devices: 212 us -> 77.6 us  [move(): return lax.ppermute(block, 'ctx', pairs)]
    reduce_scatter x4 -> x2, waiting for transfers between devices: 64.3 us -> 0.01 us  [the longest x1 0.01 us: shards(): lax.psum_scatter(down_parts.reshape(-1, width), 'ctx', scatter_dimension=...]
    unnamed x175 -> x166, local copies, waits for them, and re-layouts: 29.7 us -> 12.5 us
    ppermute x18 -> x9, starting transfers between devices: 58.3 us -> 43.1 us  [move(): return lax.ppermute(block, 'ctx', pairs)]
  transfers between devices with their start and end apart: 29 -> 14, of which waited for: 14 -> 4; matrix products, arithmetic and copies ran while one was open for 27% -> 15% of each run, Pallas kernels for 3% -> 29%
where the time goes in v2:
time: 741 us; the launch traced here: 733 us
  Pallas kernels  464 us (63%)
  waiting for transfers between devices  79.5 us (11%)
  local copies, waits for them, and re-layouts  51.6 us (7%)
  starting transfers between devices  43.3 us (6%)
  other arithmetic  42.7 us (6%)
  matrix products  36.2 us (5%)
  between operations  16 us (2%)
    pallas_call x2, Pallas kernels, sum_all(): pl.pallas_call(functools.partial(sum_kernel, parts), in_specs=[ANY] * par...  181 us
    pallas_call x1, Pallas kernels, feed_forward(): pl.pallas_call(functools.partial(feed_forward_kernel, dp_blocks), in_spec...  177 us
    ppermute x9, waiting for transfers between devices, move(): return lax.ppermute(block, 'ctx', pairs)  77.6 us
    pallas_call x1, Pallas kernels, gather_all(): pl.pallas_call(functools.partial(gather_kernel, parts, riders), in_specs=...  71.6 us
    ppermute x9, starting transfers between devices, move(): return lax.ppermute(block, 'ctx', pairs)  43.1 us
    dot_general x9, matrix products, mdot(): return lax.dot_general(a, b, dims, preferred_element_type=f32)  36.2 us
    pallas_call x1, Pallas kernels, attn_backward(): pl.pallas_call(functools.partial(attn_bwd_kernel, blocks), grid_spec=pltp...  22.4 us
  transfers between devices with their start and end apart: 14, of which 4 were waited for; matrix products, arithmetic and copies ran while one was open for 15% of the time, Pallas kernels for 29%

profile of v2, /device:TPU:0, one launch (start us, length us, event | category | flops | bytes accessed | tf_op | source)
XLA Modules:
  0.0 732.9 jit_solution(9193329468007145226)
XLA Ops:
  9.4 2.5 fusion.16.refs_3_.refs_4_
  12.6 71.6 %gather_all.1 = (bf16[8,4,48,1152]{3,2,1,0:T(8,128)(2,1)}, bf16[8,4,48,1536]{3,2,1,0:T(8,128)(2,1)}, bf16[8,4,48,1536]{3,2,1,0:T(8,128)(2,1)}, bf16[384,1536]{1,0:T(8,128)(2,1)}) custom-call(bf16[48,1152]{1,0:T(8,128)(2,1)} %fusion.37.refs_0_, bf16[48,1536]{1,0:T(8,128)(2,1)} %refs_1_.1, bf16[48,1536]{1,0:T(8,128)(2,1)} %bitcast.101, ...), custom_call_target="tpu_custom_call" | custom-call | tf_op jit(solution)/shard_map/gather_all/pallas_call | solution.py:168
  91.6 3.3 fusion.5
  101.7 4.2 collective-permute-start.2
  105.9 9.4 %collective-permute-start.1 = (bf16[2,384,512]{2,1,0:T(8,128)(2,1)S(1)}, bf16[2,384,512]{2,1,0:T(8,128)(2,1)S(1)}, u32[]{:S(2)}, u32[]{:S(2)}) collective-permute-start(bf16[2,384,512]{2,1,0:T(8,128)(2,1)S(1)} %pad_maximum_fusion.1.refs_0_), channel_id=1, source_target_pairs={{0,2},{1,3},{4,6},{5,7},{8,10},{9,11},{12,14},{13,15},{16,18},{17,... | collective-permute-start | bytes 2359304 | tf_op jit(solution)/shard_map/ppermute | solution.py:719
  117.5 6.7 copy.78
  124.3 6.9 multiply_reduce_fusion.5
  131.2 9.5 %collective-permute-done.1.refs_2_ = bf16[2,384,512]{2,1,0:T(8,128)(2,1)S(1)} collective-permute-done((bf16[2,384,512]{2,1,0:T(8,128)(2,1)S(1)}, bf16[2,384,512]{2,1,0:T(8,128)(2,1)S(1)}, u32[]{:S(2)}, u32[]{:S(2)}) %collective-permute-start.1) | collective-permute-done | bytes 786464 | tf_op jit(solution)/shard_map/ppermute | solution.py:719
  140.7 16.4 %collective-permute-done.refs_1_ = bf16[2,384,512]{2,1,0:T(8,128)(2,1)} collective-permute-done((bf16[2,384,512]{2,1,0:T(8,128)(2,1)S(1)}, bf16[2,384,512]{2,1,0:T(8,128)(2,1)}, u32[]{:S(2)}, u32[]{:S(2)}) %collective-permute-start) | collective-permute-done | bytes 786464 | tf_op jit(solution)/shard_map/ppermute | solution.py:719
  157.1 20.3 %collective-permute-start.3 = (bf16[384,1536]{1,0:T(8,128)(2,1)}, bf16[384,1536]{1,0:T(8,128)(2,1)}, u32[]{:S(2)}, u32[]{:S(2)}) collective-permute-start(bf16[384,1536]{1,0:T(8,128)(2,1)} %fusion.16.refs_3_.refs_4_), channel_id=1, source_target_pairs={{0,2},{1,3},{2,0},{3,1},{4,6},{5,7},{6,4},{7,5},{8,10},{9,11},{10,... | collective-permute-start | bytes 3538952 | tf_op jit(solution)/shard_map/ppermute | solution.py:719
  186.7 11.7 %attn_forward.1 = (bf16[384,1536]{1,0:T(8,128)(2,1)S(1)}, f32[4,8,384]{2,1,0:T(8,128)S(1)}) custom-call(s32[2]{0:T(128)S(1)} %pad_add_fusion.where_ref, bf16[384,1536]{1,0:T(8,128)(2,1)S(1)} %copy.83.q_ref, bf16[2,384,512]{2,1,0:T(8,128)(2,1)S(1)} %pad_maximum_fusion.1.refs_0_, bf16[2,384,512]{2,1,0:T(8,128)(2,1)} %collective-permute-done.refs_1_, ...), custom_call_target="tpu_custom_call" | custom-call | tf_op jit(solution)/shard_map/attn_forward/pallas_call | solution.py:445
  198.4 30.9 %collective-permute-done.3.refs_6_ = bf16[384,1536]{1,0:T(8,128)(2,1)} collective-permute-done((bf16[384,1536]{1,0:T(8,128)(2,1)}, bf16[384,1536]{1,0:T(8,128)(2,1)}, u32[]{:S(2)}, u32[]{:S(2)}) %collective-permute-start.3) | collective-permute-done | bytes 1179680 | tf_op jit(solution)/shard_map/ppermute | solution.py:719
  231.0 4.5 multiply_reduce_fusion.4
  238.3 20.8 %collective-permute-done.5 = bf16[384,1536]{1,0:T(8,128)(2,1)S(1)} collective-permute-done((bf16[384,1536]{1,0:T(8,128)(2,1)}, bf16[384,1536]{1,0:T(8,128)(2,1)S(1)}, u32[]{:S(2)}, u32[]{:S(2)}) %collective-permute-start.5) | collective-permute-done | bytes 1179680 | tf_op jit(solution)/shard_map/ppermute | solution.py:719
  260.2 176.7 %feed_forward.1 = (f32[384,1536]{1,0:T(8,128)}, bf16[4,384,1536]{2,1,0:T(8,128)(2,1)}, bf16[8,3,192,1728]{3,2,1,0:T(8,128)(2,1)}) custom-call(bf16[384,1536]{1,0:T(8,128)(2,1)} %multiply_convert_fusion.1.refs_0_, bf16[1536,1728]{1,0:T(8,128)(2,1)} %all-gather.4.cloned.1.call-done.refs_1_, bf16[1536,1728]{1,0:T(8,128)(2,1)} %all-gather.6.cloned.1.call-done.refs_2_, ...), custom_call_target="tpu_custom_call" | custom-call | tf_op jit(solution)/shard_map/feed_forward/pallas_call | solution.py:662
  437.6 2.5 copy.91
  440.1 2.4 multiply_reduce_fusion.1
  444.4 3.0 convolution_convert_fusion.3.refs_4_
  447.4 22.4 %attn_backward.1 = (f32[384,1536]{1,0:T(8,128)}, f32[2,384,512]{2,1,0:T(8,128)}, bf16[2,384,512]{2,1,0:T(8,128)(2,1)}, bf16[2,384,512]{2,1,0:T(8,128)(2,1)}, bf16[2,384,512]{2,1,0:T(8,128)(2,1)}) custom-call(s32[2]{0:T(128)} %copy-done.12, bf16[384,1536]{1,0:T(8,128)(2,1)} %copy-done, bf16[2,384,512]{2,1,0:T(8,128)(2,1)} %copy-done.1, ...), custom_call_target="tpu_custom_call" | custom-call | tf_op jit(solution)/shard_map/attn_backward/pallas_call | solution.py:469
  479.1 2.5 multiply_reduce_fusion.2
  482.3 2.5 multiply_convert_fusion
  485.1 4.3 convolution_convert_fusion
  492.2 3.1 convolution_convert_fusion.1
  495.4 145.0 %sum_all.2 = (f32[48,1536]{1,0:T(8,128)S(1)}, f32[48,1536]{1,0:T(8,128)S(1)}) custom-call(bf16[8,4,48,1536]{3,2,1,0:T(8,128)(2,1)S(1)} %bitcast.76, bf16[8,4,48,1536]{3,2,1,0:T(8,128)(2,1)} %bitcast.92), custom_call_target="tpu_custom_call" | custom-call | tf_op jit(solution)/shard_map/sum_all/pallas_call | solution.py:304
  640.4 3.5 fusion.51
  646.4 2.4 copy.86
  663.0 4.7 fusion.9
  668.1 2.9 convolution_convert_fusion.2
  673.0 4.5 copy.96
  677.5 36.2 %sum_all.3 = f32[48,1152]{1,0:T(8,128)S(1)} custom-call(bf16[8,4,48,1152]{3,2,1,0:T(8,128)(2,1)S(1)} %bitcast.75), custom_call_target="tpu_custom_call" | custom-call | tf_op jit(solution)/shard_map/sum_all/pallas_call | solution.py:304
  715.8 3.9 fusion.12
  719.7 2.8 add_convert_fusion
  (276 shorter events, 73.0 us)
Async XLA Ops:
  7.2 253.0 %all-gather.4.cloned.1.call-start = ((), (), s32[]{:S(2)}) async-start(), calls=%async_computation.2 | async-start | bytes 6193152 | tf_op jit(solution)/shard_map/all_gather | solution.py:764
  84.2 176.0 %all-gather.6.cloned.1.call-start = ((), (), s32[]{:S(2)}) async-start(), calls=%async_computation.3 | async-start | bytes 6193152 | tf_op jit(solution)/shard_map/all_gather | solution.py:764
  85.0 175.3 %all-gather.8.cloned.1.call-start = ((), (), s32[]{:S(2)}) async-start(), calls=%async_computation.4 | async-start | bytes 6193152 | tf_op jit(solution)/shard_map/all_gather | solution.py:764
  85.7 634.0 %reduce-scatter.5.cloned.1.call-start = ((), (), s32[]{:S(2)}) async-start(), calls=%async_computation.6 | async-start | bytes 5898240 | tf_op jit(solution)/shard_map/reduce_scatter | solution.py:804
  101.7 83.8 %copy-start.1 = (bf16[2,384,512]{2,1,0:T(8,128)(2,1)}, bf16[2,384,512]{2,1,0:T(8,128)(2,1)S(1)}, u32[]{:S(2)}) copy-start(bf16[2,384,512]{2,1,0:T(8,128)(2,1)S(1)} %pad_maximum_fusion.1.refs_0_) | copy-start | bytes 2359300
  101.7 29.5 %collective-permute-start.2 = (bf16[2,384,512]{2,1,0:T(8,128)(2,1)S(1)}, bf16[2,384,512]{2,1,0:T(8,128)(2,1)S(1)}, u32[]{:S(2)}, u32[]{:S(2)}) collective-permute-start(bf16[2,384,512]{2,1,0:T(8,128)(2,1)S(1)} %pad_maximum_fusion.1.refs_0_), channel_id=1, source_target_pairs={{0,3},{4,7},{8,11},{12,15},{16,19},{20,23},{24,27},{28,31}} | collective-permute-start | bytes 2359304 | tf_op jit(solution)/shard_map/ppermute | solution.py:719
  105.9 34.7 %collective-permute-start.1 = (bf16[2,384,512]{2,1,0:T(8,128)(2,1)S(1)}, bf16[2,384,512]{2,1,0:T(8,128)(2,1)S(1)}, u32[]{:S(2)}, u32[]{:S(2)}) collective-permute-start(bf16[2,384,512]{2,1,0:T(8,128)(2,1)S(1)} %pad_maximum_fusion.1.refs_0_), channel_id=1, source_target_pairs={{0,2},{1,3},{4,6},{5,7},{8,10},{9,11},{12,14},{13,15},{16,18},{17,... | collective-permute-start | bytes 2359304 | tf_op jit(solution)/shard_map/ppermute | solution.py:719
  115.4 41.7 %collective-permute-start = (bf16[2,384,512]{2,1,0:T(8,128)(2,1)S(1)}, bf16[2,384,512]{2,1,0:T(8,128)(2,1)}, u32[]{:S(2)}, u32[]{:S(2)}) collective-permute-start(bf16[2,384,512]{2,1,0:T(8,128)(2,1)S(1)} %pad_maximum_fusion.1.refs_0_), channel_id=1, source_target_pairs={{0,1},{1,2},{2,3},{4,5},{5,6},{6,7},{8,9},{9,10},{10,11},{12,13},{... | collective-permute-start | bytes 2359304 | tf_op jit(solution)/shard_map/ppermute | solution.py:719
  117.5 6.7 copy-start.60
  117.5 6.7 copy-start.69
  124.3 53.1 %copy-start.58 = (f32[16,4]{1,0:T(8,128)S(1)}, f32[16,4]{1,0:T(8,128)}, u32[]{:S(2)}) copy-start(f32[16,4]{1,0:T(8,128)} %get-tuple-element.86) | copy-start | bytes 772
  131.2 54.3 %copy-start.2 = (bf16[2,384,512]{2,1,0:T(8,128)(2,1)}, bf16[2,384,512]{2,1,0:T(8,128)(2,1)S(1)}, u32[]{:S(2)}) copy-start(bf16[2,384,512]{2,1,0:T(8,128)(2,1)S(1)} %collective-permute-done.2.refs_3_) | copy-start | bytes 2359300
  140.7 38.9 %copy-start.3 = (bf16[2,384,512]{2,1,0:T(8,128)(2,1)}, bf16[2,384,512]{2,1,0:T(8,128)(2,1)S(1)}, u32[]{:S(2)}) copy-start(bf16[2,384,512]{2,1,0:T(8,128)(2,1)S(1)} %collective-permute-done.1.refs_2_) | copy-start | bytes 2359300
  157.1 72.3 %collective-permute-start.3 = (bf16[384,1536]{1,0:T(8,128)(2,1)}, bf16[384,1536]{1,0:T(8,128)(2,1)}, u32[]{:S(2)}, u32[]{:S(2)}) collective-permute-start(bf16[384,1536]{1,0:T(8,128)(2,1)} %fusion.16.refs_3_.refs_4_), channel_id=1, source_target_pairs={{0,2},{1,3},{2,0},{3,1},{4,6},{5,7},{6,4},{7,5},{8,10},{9,11},{10,... | collective-permute-start | bytes 3538952 | tf_op jit(solution)/shard_map/ppermute | solution.py:719
  184.5 51.0 %copy-start = (bf16[384,1536]{1,0:T(8,128)(2,1)}, bf16[384,1536]{1,0:T(8,128)(2,1)S(1)}, u32[]{:S(2)}) copy-start(bf16[384,1536]{1,0:T(8,128)(2,1)S(1)} %copy.83.q_ref) | copy-start | bytes 3538948
  184.6 50.9 %copy-start.12 = (s32[2]{0:T(128)}, s32[2]{0:T(128)S(1)}, u32[]{:S(2)}) copy-start(s32[2]{0:T(128)S(1)} %pad_add_fusion.where_ref) | copy-start | bytes 28
  184.6 53.7 %collective-permute-start.4 = (bf16[384,1536]{1,0:T(8,128)(2,1)}, bf16[384,1536]{1,0:T(8,128)(2,1)S(1)}, u32[]{:S(2)}, u32[]{:S(2)}) collective-permute-start(bf16[384,1536]{1,0:T(8,128)(2,1)} %fusion.16.refs_3_.refs_4_), channel_id=1, source_target_pairs={{1,2},{2,1},{5,6},{6,5},{9,10},{10,9},{13,14},{14,13},{17,18},{18,... | collective-permute-start | bytes 3538952 | tf_op jit(solution)/shard_map/ppermute | solution.py:719
  186.7 44.3 %copy-start.33 = (bf16[384,1536]{1,0:T(8,128)(2,1)S(1)}, bf16[384,1536]{1,0:T(8,128)(2,1)}, u32[]{:S(2)}) copy-start(bf16[384,1536]{1,0:T(8,128)(2,1)} %param.13) | copy-start | bytes 3538948
  198.4 37.1 %copy-start.5 = (bf16[384,1536]{1,0:T(8,128)(2,1)}, bf16[384,1536]{1,0:T(8,128)(2,1)S(1)}, u32[]{:S(2)}) copy-start(bf16[384,1536]{1,0:T(8,128)(2,1)S(1)} %get-tuple-element.37.refs_5_) | copy-start | bytes 3538948
  198.4 37.1 %copy-start.11 = (f32[4,8,384]{2,1,0:T(8,128)}, f32[4,8,384]{2,1,0:T(8,128)S(1)}, u32[]{:S(2)}) copy-start(f32[4,8,384]{2,1,0:T(8,128)S(1)} %get-tuple-element.47.refs_6_) | copy-start | bytes 147460
  229.3 29.8 %collective-permute-start.5 = (bf16[384,1536]{1,0:T(8,128)(2,1)}, bf16[384,1536]{1,0:T(8,128)(2,1)S(1)}, u32[]{:S(2)}, u32[]{:S(2)}) collective-permute-start(bf16[384,1536]{1,0:T(8,128)(2,1)} %collective-permute-done.3.refs_6_), channel_id=1, source_target_pairs={{2,3},{1,0},{6,7},{5,4},{10,11},{9,8},{14,15},{13,12},{18,19},{17,... | collective-permute-start | bytes 3538952 | tf_op jit(solution)/shard_map/ppermute | solution.py:719
  231.0 5.9 copy-start.53
  437.0 282.7 %reduce-scatter.3.cloned.1.call-start = ((), (), s32[]{:S(2)}) async-start(), calls=%async_computation.5 | async-start | bytes 18579456 | tf_op jit(solution)/shard_map/reduce_scatter | solution.py:801
  469.8 174.1 %collective-permute-start.6 = (bf16[2,384,512]{2,1,0:T(8,128)(2,1)}, bf16[2,384,512]{2,1,0:T(8,128)(2,1)}, u32[]{:S(2)}, u32[]{:S(2)}) collective-permute-start(bf16[2,384,512]{2,1,0:T(8,128)(2,1)} %get-tuple-element.49), channel_id=1, source_target_pairs={{1,0},{2,1},{3,2},{5,4},{6,5},{7,6},{9,8},{10,9},{11,10},{13,12},{... | collective-permute-start | bytes 2359304 | tf_op jit(solution)/shard_map/ppermute | solution.py:719
  471.1 18.3 %collective-permute-start.7 = (bf16[2,384,512]{2,1,0:T(8,128)(2,1)}, bf16[2,384,512]{2,1,0:T(8,128)(2,1)}, u32[]{:S(2)}, u32[]{:S(2)}) collective-permute-start(bf16[2,384,512]{2,1,0:T(8,128)(2,1)} %get-tuple-element.51), channel_id=1, source_target_pairs={{3,2},{7,6},{11,10},{15,14},{19,18},{23,22},{27,26},{31,30}} | collective-permute-start | bytes 2359304 | tf_op jit(solution)/shard_map/ppermute | solution.py:719
  485.1 7.1 copy-start.47
  485.1 155.3 %slice-start = ((s8[4718592]{0:T(1024)(128)(4,1)}), s8[4194304]{0:T(1024)(128)(4,1)S(1)}, s32[]{:S(2)}) async-start(s8[4718592]{0:T(1024)(128)(4,1)} %bitcast.88), calls=%async_computation.7 | async-start | bytes 8388608
  490.9 153.0 %collective-permute-start.8 = (bf16[2,384,512]{2,1,0:T(8,128)(2,1)S(1)}, bf16[2,384,512]{2,1,0:T(8,128)(2,1)S(1)}, u32[]{:S(2)}, u32[]{:S(2)}) collective-permute-start(bf16[2,384,512]{2,1,0:T(8,128)(2,1)S(1)} %add_convert_fusion.1), channel_id=1, source_target_pairs={{2,0},{3,1},{6,4},{7,5},{10,8},{11,9},{14,12},{15,13},{18,16},{19,... | collective-permute-start | bytes 2359304 | tf_op jit(solution)/shard_map/ppermute | solution.py:719
  492.2 148.2 %slice-start.1 = ((s8[4718592]{0:T(1024)(128)(4,1)}), s8[524288]{0:T(1024)(128)(4,1)S(1)}, s32[]{:S(2)}) async-start(s8[4718592]{0:T(1024)(128)(4,1)} %bitcast.88), calls=%async_computation.8 | async-start | bytes 1048576
  495.4 145.0 %copy-start.48 = (bf16[384,24,64]{0,2,1:T(8,128)(2,1)S(1)}, bf16[384,24,64]{0,2,1:T(8,128)(2,1)}, u32[]{:S(2)}) copy-start(bf16[384,24,64]{0,2,1:T(8,128)(2,1)} %copy-done.47) | copy-start | bytes 3538948
  677.5 38.3 %copy-start.25 = (f32[384,1536]{1,0:T(8,128)S(1)}, f32[384,1536]{1,0:T(8,128)}, u32[]{:S(2)}) copy-start(f32[384,1536]{1,0:T(8,128)} %copy-done.23) | copy-start | bytes 7077892
  677.5 38.3 %copy-start.37 = (bf16[384,1536]{1,0:T(8,128)(2,1)S(1)}, bf16[384,1536]{1,0:T(8,128)(2,1)}, u32[]{:S(2)}) copy-start(bf16[384,1536]{1,0:T(8,128)(2,1)} %param.13) | copy-start | bytes 3538948
  (63 other events, 182.9 us)
Sparse Core Ops, SparseCore 0:
  84.4 49.8 all-gather.3
  136.1 42.2 all-gather.5
  180.3 42.2 all-gather.7
  437.1 104.1 reduce-scatter.4
  545.0 139.4 reduce-scatter.2

commit v3 on v2

--- a/solution.py
+++ b/solution.py
@@ -67,6 +67,10 @@
 
 
 ANY = pl.BlockSpec(memory_space=pl.ANY)
+
+
+def lasting(micros):
+    return pl.CostEstimate(flops=micros * 10**9, bytes_accessed=0, transcendentals=0)
 
 
 def remote(src, dst, send, recv, dp, ctx):
@@ -185,15 +189,19 @@
     return full + list(outs[parts:])
 
 
-def sum_kernel(parts, *refs):
-    ins, outs = refs[:parts], refs[parts : 2 * parts]
-    keep = refs[2 * parts : 3 * parts]
-    got = refs[3 * parts : 4 * parts]
-    plane1 = refs[4 * parts : 5 * parts]
-    plane2 = refs[5 * parts : 6 * parts]
-    lines = refs[6 * parts : 7 * parts]
-    load, send, recv = refs[7 * parts :]
+def sum_kernel(parts, hops, *refs):
+    riders = len(hops)
+    ins, riding = refs[:parts], refs[parts : parts + riders]
+    refs = refs[parts + riders :]
+    outs, landed = refs[:parts], refs[parts : parts + riders]
+    refs = refs[parts + riders :]
+    keep, got, plane1, plane2, lines = (refs[i * parts : (i + 1) * parts] for i in range(5))
+    load, send, recv, ride_send, ride_recv = refs[5 * parts :]
     dp, ctx = lax.axis_index("dp"), lax.axis_index("ctx")
+
+    def ride(i):
+        return remote(riding[i], landed[i], ride_send.at[i], ride_recv.at[i], dp, ctx ^ hops[i])
+
     chip = dp // 2
     core = dp - 2 * chip
 
@@ -237,6 +245,8 @@
     for p in range(parts):
         for k in (3, 1, 2, 0):
             across(p, k).start()
+    for i in range(riders):
+        ride(i).start()
 
     def add(target, term):
         target[...] = (target[...].astype(f32) + term[...].astype(f32)).astype(bf16)
@@ -291,10 +301,12 @@
             second(p, w).wait_send()
         for s in (1, 2, 3):
             line(p, s).wait_send()
-
-
-def sum_all(terms, cid):
-    parts = len(terms)
+    for i in range(riders):
+        ride(i).wait()
+
+
+def sum_all(terms, riding, hops, cid):
+    parts, riders = len(terms), len(riding)
     blocks = [t.reshape(8, 4, t.shape[0] // 32, t.shape[1]) for t in terms]
     shapes = [b.shape[2:] for b in blocks]
 
@@ -302,21 +314,24 @@
         return [pltpu.VMEM(lead + s, bf16) for s in shapes]
 
     return pl.pallas_call(
-        functools.partial(sum_kernel, parts),
-        in_specs=[ANY] * parts,
-        out_specs=[pl.BlockSpec(memory_space=pltpu.VMEM)] * parts,
-        out_shape=[jax.ShapeDtypeStruct(s, f32) for s in shapes],
+        functools.partial(sum_kernel, parts, hops),
+        in_specs=[ANY] * (parts + riders),
+        out_specs=[pl.BlockSpec(memory_space=pltpu.VMEM)] * parts + [ANY] * riders,
+        out_shape=[jax.ShapeDtypeStruct(s, f32) for s in shapes]
+        + [jax.ShapeDtypeStruct(r.shape, r.dtype) for r in riding],
         scratch_shapes=per((4, 4)) + per((4, 4)) + per((2, 4)) + per((4,)) + per((3,))
         + [
             pltpu.SemaphoreType.DMA((parts, 4)),
             pltpu.SemaphoreType.DMA((parts, 13)),
             pltpu.SemaphoreType.DMA((parts, 13)),
+            pltpu.SemaphoreType.DMA((riders,)),
+            pltpu.SemaphoreType.DMA((riders,)),
         ],
         compiler_params=pltpu.CompilerParams(
             collective_id=cid, has_side_effects=True, vmem_limit_bytes=48 * 2**20
         ),
         name="sum_all",
-    )(*blocks)
+    )(*blocks, *riding)
 
 
 def causal_mask(rows, limit, key_axis):
@@ -366,26 +381,67 @@
     log_ref[0] = jnp.transpose(logs)[:8]
 
 
-def attn_bwd_kernel(blocks, where_ref, q_ref, *refs):
+def split_dot(values, weights, dims):
+    high = values.astype(bf16)
+    low = (values - high.astype(f32)).astype(bf16)
+    return mdot(high, weights, dims) + mdot(low, weights, dims)
+
+
+def head_means(values):
+    shape = (2 * HD, 2 * HD)
+    same = lax.broadcasted_iota(jnp.int32, shape, 0) // HD == (
+        lax.broadcasted_iota(jnp.int32, shape, 1) // HD
+    )
+    return split_dot(values, jnp.where(same, 1.0 / HD, 0.0).astype(bf16), NN)
+
+
+def first_half(shape):
+    return lax.rem(lax.broadcasted_iota(jnp.int32, shape, 1), HD) < HD // 2
+
+
+def half_swap(values):
+    lower = pltpu.roll(values, HD // 2, 1)
+    upper = pltpu.roll(values, 2 * HD - HD // 2, 1)
+    return jnp.where(first_half(values.shape), upper, lower)
+
+
+def unrotate_norm_back(grad_rot, raw, cosine, signed_sine, gain):
+    grad_upper = grad_rot * cosine + half_swap(grad_rot * signed_sine)
+    factor = lax.rsqrt(head_means(raw * raw) + EPSILON)
+    unit_rows = raw * factor
+    scaled = grad_upper * gain
+    grad_lower = factor * (scaled - unit_rows * head_means(scaled * unit_rows))
+    return grad_lower, jnp.sum(grad_upper * unit_rows, axis=0, keepdims=True)
+
+
+def attn_bwd_kernel(blocks, length_ref, q_ref, *refs):
     kv_refs = refs[:blocks]
-    do_ref, o_ref, log_ref = refs[blocks : blocks + 3]
-    dq_ref = refs[blocks + 3]
-    dkv_refs = refs[blocks + 4 : 2 * blocks + 4]
-    mask, dqt, inner = refs[2 * blocks + 4 :]
+    do_ref, o_ref, log_ref, q_raw, k_raw, cosine, sine, gains = refs[blocks : blocks + 8]
+    gq_ref, gkv_ref, gain_ref = refs[blocks + 8 : blocks + 11]
+    mask, dqt, inner, own, to_send, received, send, recv = refs[blocks + 11 :]
     rows = q_ref.shape[0]
-    mine, limit = where_ref[0], where_ref[1]
-
-    @pl.when(pl.program_id(0) == 0)
+    step = pl.program_id(0)
+    dp, mine = lax.axis_index("dp"), lax.axis_index("ctx")
+
+    def give(back, i):
+        return remote(
+            to_send.at[back - 1, i], received.at[back - 1, i],
+            send.at[back - 1, i], recv.at[back - 1, i], dp, mine - back,
+        )
+
+    @pl.when(step == 0)
     def _():
-        mask[...] = causal_mask(rows, limit, 0)
-
-    ones = jnp.ones((8, HD), f32)
+        greet(dp, mine, (), (1, 2, 3))
+        mask[...] = causal_mask(rows, length_ref[0] - mine * rows, 0)
+        gain_ref[...] = jnp.zeros_like(gain_ref)
+
+    ones = jnp.ones((8, HD), bf16)
     for h in range(2 * GROUP):
         cols = slice(h * HD, (h + 1) * HD)
         product = do_ref[:, cols].astype(f32) * o_ref[:, cols].astype(f32)
-        inner[h] = lax.dot_general(
-            ones, product, NT, preferred_element_type=f32, precision=lax.Precision.HIGHEST
-        )
+        high = product.astype(bf16)
+        low = (product - high.astype(f32)).astype(bf16)
+        inner[h] = mdot(ones, high, NT) + mdot(ones, low, NT)
 
     def head(back, pair):
         cols = slice(pair * HD, (pair + 1) * HD)
@@ -408,24 +464,86 @@
             grad_v += mdot(probs.astype(bf16), grad)
             term = mdot(keys_t, grad_scores)
             dqt[h] = term if back == 0 else dqt[h] + term
-        dkv_refs[back][0, :, cols] = grad_k.astype(dkv_refs[back].dtype)
-        dkv_refs[back][1, :, cols] = grad_v.astype(dkv_refs[back].dtype)
+        if back == 0:
+            own[step, 0, :, cols] = grad_k
+            own[step, 1, :, cols] = grad_v
+        else:
+            to_send[back - 1, step, 0, :, cols] = grad_k.astype(bf16)
+            to_send[back - 1, step, 1, :, cols] = grad_v.astype(bf16)
+
+    def hand_over(i):
+        return remote(
+            to_send.at[2, i], received.at[2, i], send.at[2, i], recv.at[2, i], dp, mine - 1
+        )
+
+    def pass_on(i):
+        hand_over(i).wait_recv()
+        for part in range(2):
+            joined = to_send[1, i, part].astype(f32) + received[2, i, part].astype(f32)
+            to_send[1, i, part] = joined.astype(bf16)
+        give(2, i).start()
 
     for pair in range(2):
         head(0, pair)
-    for back in range(1, blocks):
+    for back in (3, 2, 1):
 
         @pl.when(mine >= back)
         def _():
             for pair in range(2):
                 head(back, pair)
-
-        @pl.when(mine < back)
-        def _():
-            dkv_refs[back][...] = jnp.zeros_like(dkv_refs[back])
-
-    for h in range(2 * GROUP):
-        dq_ref[:, h * HD : (h + 1) * HD] = jnp.transpose(dqt[h]) * (HD**-0.5)
+            if back == 3:
+                hand_over(step).start()
+            elif back == 1:
+                give(1, step).start()
+
+        if back == 2:
+
+            @pl.when(mine == 3)
+            def _():
+                give(2, step).start()
+
+    @pl.when((mine == 2) & (step > 0))
+    def _():
+        pass_on(step - 1)
+
+    @pl.when((mine == 2) & (step == PAIRS - 1))
+    def _():
+        pass_on(step)
+
+    for j in range(GROUP):
+        cols = slice(2 * j * HD, (2 * j + 2) * HD)
+        turned = jnp.concatenate([jnp.transpose(dqt[2 * j]), jnp.transpose(dqt[2 * j + 1])], 1)
+        grad, gain_term = unrotate_norm_back(
+            turned * (HD**-0.5), q_raw[:, cols], cosine[...], sine[...], gains[0:1, :]
+        )
+        gq_ref[:, cols] = grad.astype(bf16)
+        gain_ref[0:1, :] += gain_term
+
+    @pl.when(step == PAIRS - 1)
+    def _():
+        for back in (1, 2):
+
+            @pl.when(mine + back < blocks)
+            def _():
+                for i in range(PAIRS):
+                    give(back, i).wait_recv()
+                    for part in range(2):
+                        own[i, part] += received[back - 1, i, part].astype(f32)
+
+        for i in range(PAIRS):
+            cols = slice(2 * i * HD, (2 * i + 2) * HD)
+            grad, gain_term = unrotate_norm_back(
+                own[i, 0], k_raw[:, cols], cosine[...], sine[...], gains[1:2, :]
+            )
+            gkv_ref[:, cols] = grad.astype(bf16)
+            gkv_ref[:, KVH * HD + 2 * i * HD : KVH * HD + (2 * i + 2) * HD] = own[i, 1].astype(bf16)
+            gain_ref[1:2, :] += gain_term
+        for back in (1, 2, 3):
+
+            @pl.when(mine >= back)
+            def _():
+                for i in range(PAIRS):
+                    (hand_over(i) if back == 3 else give(back, i)).wait_send()
 
 
 def kv_spec(rows):
@@ -463,29 +581,48 @@
     )(where, query, *kv_blocks)
 
 
-def attn_backward(where, query, kv_blocks, grad, mixed, logs):
+def whole_spec(*shape):
+    return pl.BlockSpec(shape, lambda i, *_: (0,) * len(shape))
+
+
+def attn_backward(length, query, kv_blocks, grad, mixed, logs, q_raw, k_raw, tables, gains, cid):
     rows, blocks = query.shape[0], len(kv_blocks)
-    kinds = [f32] + [bf16] * (blocks - 1)
+    pair = (2, rows, 2 * HD)
     return pl.pallas_call(
         functools.partial(attn_bwd_kernel, blocks),
-        grid_spec=pltpu.PrefetchScalarGridSpec(
-            num_scalar_prefetch=1,
-            grid=(PAIRS,),
-            in_specs=[head_spec(rows)]
-            + [kv_spec(rows)] * blocks
-            + [head_spec(rows), head_spec(rows), log_spec(rows)],
-            out_specs=[head_spec(rows)] + [kv_spec(rows)] * blocks,
-            scratch_shapes=[
-                pltpu.VMEM((rows, rows), f32),
-                pltpu.VMEM((2 * GROUP, HD, rows), f32),
-                pltpu.VMEM((2 * GROUP, 8, rows), f32),
-            ],
+        grid=(PAIRS,),
+        in_specs=[pl.BlockSpec(memory_space=pltpu.SMEM), head_spec(rows)]
+        + [kv_spec(rows)] * blocks
+        + [head_spec(rows), head_spec(rows), log_spec(rows), head_spec(rows)]
+        + [whole_spec(rows, KVH * HD)]
+        + [whole_spec(rows, 2 * HD)] * 2
+        + [whole_spec(2, 2 * HD)],
+        out_specs=[
+            head_spec(rows),
+            whole_spec(rows, 2 * KVH * HD),
+            whole_spec(2, 2 * HD),
+        ],
+        out_shape=[
+            jax.ShapeDtypeStruct((rows, H * HD), bf16),
+            jax.ShapeDtypeStruct((rows, 2 * KVH * HD), bf16),
+            jax.ShapeDtypeStruct((2, 2 * HD), f32),
+        ],
+        scratch_shapes=[
+            pltpu.VMEM((rows, rows), f32),
+            pltpu.VMEM((2 * GROUP, HD, rows), f32),
+            pltpu.VMEM((2 * GROUP, 8, rows), f32),
+            pltpu.VMEM((PAIRS,) + pair, f32),
+            pltpu.VMEM((blocks - 1, PAIRS) + pair, bf16),
+            pltpu.VMEM((blocks - 1, PAIRS) + pair, bf16),
+            pltpu.SemaphoreType.DMA((blocks - 1, PAIRS)),
+            pltpu.SemaphoreType.DMA((blocks - 1, PAIRS)),
+        ],
+        compiler_params=pltpu.CompilerParams(
+            collective_id=cid, has_side_effects=True, vmem_limit_bytes=56 * 2**20
         ),
-        out_shape=[jax.ShapeDtypeStruct((rows, H * HD), f32)]
-        + [jax.ShapeDtypeStruct((2, rows, KVH * HD), kind) for kind in kinds],
-        compiler_params=pltpu.CompilerParams(vmem_limit_bytes=56 * 2**20),
+        cost_estimate=lasting(120),
         name="attn_backward",
-    )(where, query, *kv_blocks, grad, mixed, logs)
+    )(length, query, *kv_blocks, grad, mixed, logs, q_raw, k_raw, *tables, gains)
 
 
 def feed_forward_kernel(dp_blocks, *refs):
@@ -723,12 +860,6 @@
         two = move(block, [(0, 2), (1, 3)])
         return [block, one, two, move(block, [(0, 3)])]
 
-    def lower(terms):
-        relay = move(terms[3], [(3, 2)])
-        two = move((terms[2].astype(f32) + relay.astype(f32)).astype(bf16), [(2, 0), (3, 1)])
-        one = move(terms[1], [(1, 0), (2, 1), (3, 2)])
-        return terms[0].astype(f32) + one.astype(f32) + two.astype(f32)
-
     def after(value, *others):
         return lax.optimization_barrier((value, others))[0]
 
@@ -741,12 +872,12 @@
         full = [lax.all_gather(b, every, axis=0, tiled=True) for b in blocks]
         return full + [swap(b, 1) for b in riding]
 
-    def collect(terms, cid):
+    def collect(terms, riding, hops, cid):
         if small:
-            return sum_all(terms, cid)
+            return sum_all(terms, riding, hops, cid)
         return [
             lax.psum_scatter(t, every, scatter_dimension=0, tiled=True).astype(f32) for t in terms
-        ]
+        ] + [swap(block, r) for block, r in zip(riding, hops)]
 
     extra = jnp.stack([gain_in, gain_mid, jnp.pad(qk_gains, (0, share - qk_share))], 1)
     extra = jnp.pad(extra, ((0, 0), (0, 125)))
@@ -785,7 +916,8 @@
     ups_ends = move(ups_two, [(2, 3), (1, 0)])
     ups_three = jnp.where((mine == 1) | (mine == 2), ups_middle, ups_ends)
     ups = [upstream_low, ups_near, ups_two, ups_three]
-    query_raw = mdot(normed, full_query).reshape(rows, H, HD)
+    query_flat = mdot(normed, full_query)
+    query_raw = query_flat.reshape(rows, H, HD)
     query_normed, factor_query = rms_scale(query_raw, gain_query)
     query_low = rotate(query_normed, cosine_table, sine_table).astype(bf16)
     query_low = (query_low * (HD**-0.5)).astype(bf16).reshape(rows, H * HD)
@@ -800,9 +932,6 @@
     )
     grad_ffn = lax.psum_scatter(
         grad_ffn.reshape(-1, grad_ffn.shape[-1]), "dp", scatter_dimension=0, tiled=True
-    )
-    down_parts = lax.psum_scatter(
-        down_parts.reshape(-1, width), "ctx", scatter_dimension=0, tiled=True
     )
     grad_hidden_norm, gain_terms_mid = norm_back(grad_mid_term, hidden, factor_mid, full_gain_mid)
     grad_hidden = upstream + grad_hidden_norm
@@ -810,52 +939,61 @@
     grad_mixed = mdot(grad_branch, full_out_t).astype(bf16)
     grad_wout_t = mdot(grad_branch, mixed_low, TN).astype(bf16)
 
-    grad_query_rot, grad_kv_own, *grad_kv_terms = attn_backward(
-        where, query_low, kv_blocks, grad_mixed, mixed_low, logs
-    )
-    grad_query_norm = rotate_back(grad_query_rot.reshape(rows, H, HD), cosine_table, sine_table)
-    grad_query_raw, gain_terms_query = norm_back(
-        grad_query_norm, query_raw, factor_query, gain_query
-    )
-    grad_query_low = grad_query_raw.reshape(rows, H * HD).astype(bf16)
+    flat_cosine = jnp.concatenate([cosine_table[:, 0], cosine_table[:, 0]], 1)
+    flat_sine = jnp.concatenate([sine_table[:, 0], sine_table[:, 0]], 1)
+    turn_sign = jnp.where(jnp.arange(2 * HD) % HD < HD // 2, -1.0, 1.0).astype(f32)
+    grad_query_low, grad_kv_low, gain_rows = attn_backward(
+        seq_lens,
+        query_low,
+        kv_blocks,
+        grad_mixed,
+        mixed_low,
+        logs,
+        query_flat,
+        kv_raw[:, : KVH * HD],
+        (flat_cosine, flat_sine * turn_sign),
+        jnp.concatenate([full_qk.reshape(2, HD), full_qk.reshape(2, HD)], 1),
+        3,
+    )
+    later = after(down_parts, grad_query_low)
+    for_far, for_two, for_near = (later[mine ^ r] for r in (3, 2, 1))
+    passed = move(for_far, [(0, 1), (3, 2)])
+    down_terms = [later[mine], move(for_far, [(1, 2), (2, 1)])]
+    for_two = (for_two.astype(f32) + passed.astype(f32)).astype(bf16)
     grad_wquery = mdot(normed, grad_query_low, TN).astype(bf16)
-    sum_query, grad_wout = collect([grad_wquery, grad_wout_t], 3)
-    grad_kv = lower([grad_kv_own] + grad_kv_terms)
-    grad_key_norm = rotate_back(grad_kv[0].reshape(rows, KVH, HD), cosine_table, sine_table)
-    grad_key_raw, gain_terms_key = norm_back(grad_key_norm, key_raw, factor_key, gain_key)
-    grad_kv_low = jnp.concatenate(
-        [grad_key_raw.reshape(rows, KVH * HD).astype(bf16), grad_kv[1].astype(bf16)], 1
-    )
     grad_wkv = mdot(normed, grad_kv_low, TN).astype(bf16)
     grad_normed = mdot(grad_query_low, full_query, NT) + mdot(grad_kv_low, full_kv, NT)
     grad_input_norm, gain_terms_in = norm_back(grad_normed, inputs, factor_in, full_gain_in)
     grad_tokens = grad_hidden + grad_input_norm
-    grad_qk = jnp.concatenate(
-        [jnp.sum(gain_terms_query, axis=(0, 1)), jnp.sum(gain_terms_key, axis=(0, 1))]
-    )
+    grad_qk = (gain_rows[:, :HD] + gain_rows[:, HD:]).reshape(-1)
     qk_column = jnp.pad(grad_qk.reshape(world, qk_share), ((0, 0), (0, share - qk_share)))
     grad_extra = jnp.stack(
         [jnp.sum(gain_terms_in, axis=0), jnp.sum(gain_terms_mid, axis=0), qk_column.reshape(-1)], 1
     )
     grad_extra = jnp.pad(grad_extra, ((0, 0), (0, 125))).astype(bf16)
-    (sum_kv,) = collect([after(jnp.concatenate([grad_wkv, grad_extra], 1), sum_query)], 4)
-    grad_ffn, down_parts = after((grad_ffn, down_parts), sum_kv)
-    output = (hidden + down_parts.astype(f32)).astype(bf16)
+    grad_wout, sum_query, sum_kv, sum_extra, *landed = collect(
+        [grad_wout_t, grad_wquery, grad_wkv, grad_extra],
+        [for_two, for_near],
+        (2, 1),
+        4,
+    )
+    down_terms += landed
+    grad_ffn, down_terms = after((grad_ffn, down_terms), sum_kv)
+    output = (hidden + sum(t.astype(f32) for t in down_terms)).astype(bf16)
     grad_wgate, grad_wup, grad_wdown = (
         grad_ffn[i * w_gate.shape[0] : (i + 1) * w_gate.shape[0]].astype(f32) for i in range(3)
     )
     grad_wdown = grad_wdown.T
-    cuts = (KVH * HD, 2 * KVH * HD)
     return (
         output,
         grad_tokens,
-        sum_kv[:, cuts[1]],
+        sum_extra[:, 0],
         sum_query,
-        sum_kv[:, : cuts[0]],
-        sum_kv[:, cuts[0] : cuts[1]],
+        sum_kv[:, : KVH * HD],
+        sum_kv[:, KVH * HD :],
         grad_wout.T,
-        sum_kv[:qk_share, cuts[1] + 2],
-        sum_kv[:, cuts[1] + 1],
+        sum_extra[:qk_share, 2],
+        sum_extra[:, 1],
         grad_wgate,
         grad_wup,
         grad_wdown,

time: 741 us -> 673 us (0.908)
  Pallas kernels: 464 us -> 422 us
  local copies, waits for them, and re-layouts: 51.6 us -> 38 us
  waiting for transfers between devices: 79.5 us -> 69.7 us
    pallas_call x3 -> x2, Pallas kernels: 204 us -> 163 us  [the longest x1 89 us: sum_all(): pl.pallas_call(functools.partial(sum_kernel, parts, hops), in_specs=[ANY]...]
    ppermute x9 -> x8, waiting for transfers between devices: 77.6 us -> 68.3 us  [move(): return lax.ppermute(block, 'ctx', pairs)]
    ppermute x9 -> x8, starting transfers between devices: 43.1 us -> 41.8 us  [move(): return lax.ppermute(block, 'ctx', pairs)]
  transfers between devices with their start and end apart: 14 -> 12, of which waited for: 4 -> 4; matrix products, arithmetic and copies ran while one was open for 15% -> 14% of each run, Pallas kernels for 29% -> 26%
where the time goes in v3:
time: 673 us; the launch traced here: 664 us
  Pallas kernels  422 us (63%)
  waiting for transfers between devices  69.7 us (10%)
  starting transfers between devices  42 us (6%)
  matrix products  38.7 us (6%)
  local copies, waits for them, and re-layouts  38 us (6%)
  other arithmetic  38 us (6%)
  between operations  15.7 us (2%)
    pallas_call x1, Pallas kernels, feed_forward(): pl.pallas_call(functools.partial(feed_forward_kernel, dp_blocks), in_spec...  177 us
    pallas_call x1, Pallas kernels, sum_all(): pl.pallas_call(functools.partial(sum_kernel, parts, hops), in_specs=[ANY]...  89 us
    pallas_call x1, Pallas kernels, attn_backward(): pl.pallas_call(functools.partial(attn_bwd_kernel, blocks), grid=(PAIRS,),...  73.5 us
    pallas_call x1, Pallas kernels, gather_all(): pl.pallas_call(functools.partial(gather_kernel, parts, riders), in_specs=...  71.6 us
    ppermute x8, waiting for transfers between devices, move(): return lax.ppermute(block, 'ctx', pairs)  68.3 us
    ppermute x8, starting transfers between devices, move(): return lax.ppermute(block, 'ctx', pairs)  41.8 us
    dot_general x9, matrix products, mdot(): return lax.dot_general(a, b, dims, preferred_element_type=f32)  38.7 us
  transfers between devices with their start and end apart: 12, of which 4 were waited for; matrix products, arithmetic and copies ran while one was open for 14% of the time, Pallas kernels for 26%

profile of v3, /device:TPU:0, one launch (start us, length us, event | category | flops | bytes accessed | tf_op | source)
XLA Modules:
  0.0 664.1 jit_solution(15448684934961417351)
XLA Ops:
  9.4 2.5 fusion.16.refs_3_.refs_4_
  12.6 71.6 %gather_all.1 = (bf16[8,4,48,1152]{3,2,1,0:T(8,128)(2,1)}, bf16[8,4,48,1536]{3,2,1,0:T(8,128)(2,1)}, bf16[8,4,48,1536]{3,2,1,0:T(8,128)(2,1)}, bf16[384,1536]{1,0:T(8,128)(2,1)}) custom-call(bf16[48,1152]{1,0:T(8,128)(2,1)} %fusion.23.refs_0_, bf16[48,1536]{1,0:T(8,128)(2,1)} %refs_1_.1, bf16[48,1536]{1,0:T(8,128)(2,1)} %bitcast.73, ...), custom_call_target="tpu_custom_call" | custom-call | tf_op jit(solution)/shard_map/gather_all/pallas_call | solution.py:172
  92.1 3.3 fusion.6
  101.1 4.3 collective-permute-start.2
  105.5 9.3 %collective-permute-start.1 = (bf16[2,384,512]{2,1,0:T(8,128)(2,1)S(1)}, bf16[2,384,512]{2,1,0:T(8,128)(2,1)S(1)}, u32[]{:S(2)}, u32[]{:S(2)}) collective-permute-start(bf16[2,384,512]{2,1,0:T(8,128)(2,1)S(1)} %pad_maximum_fusion.refs_0_), channel_id=1, source_target_pairs={{0,2},{1,3},{4,6},{5,7},{8,10},{9,11},{12,14},{13,15},{16,18},{17,... | collective-permute-start | bytes 2359304 | tf_op jit(solution)/shard_map/ppermute | solution.py:856
  116.1 2.6 mul.286
  118.7 3.1 copy.51
  121.9 6.2 fusion.30.refs_7_
  128.2 3.1 copy.48
  134.3 5.9 collective-permute-done.1.refs_2_
  140.2 16.3 %collective-permute-done.refs_1_ = bf16[2,384,512]{2,1,0:T(8,128)(2,1)S(1)} collective-permute-done((bf16[2,384,512]{2,1,0:T(8,128)(2,1)S(1)}, bf16[2,384,512]{2,1,0:T(8,128)(2,1)S(1)}, u32[]{:S(2)}, u32[]{:S(2)}) %collective-permute-start) | collective-permute-done | bytes 786464 | tf_op jit(solution)/shard_map/ppermute | solution.py:856
  156.5 20.2 %collective-permute-start.3 = (bf16[384,1536]{1,0:T(8,128)(2,1)}, bf16[384,1536]{1,0:T(8,128)(2,1)}, u32[]{:S(2)}, u32[]{:S(2)}) collective-permute-start(bf16[384,1536]{1,0:T(8,128)(2,1)} %fusion.16.refs_3_.refs_4_), channel_id=1, source_target_pairs={{0,2},{1,3},{2,0},{3,1},{4,6},{5,7},{6,4},{7,5},{8,10},{9,11},{10,... | collective-permute-start | bytes 3538952 | tf_op jit(solution)/shard_map/ppermute | solution.py:856
  178.3 3.1 copy.53
  183.0 3.1 copy.49
  186.2 5.5 fusion.17.q_ref
  192.8 11.1 %attn_forward.1 = (bf16[384,1536]{1,0:T(8,128)(2,1)S(1)}, f32[4,8,384]{2,1,0:T(8,128)S(1)}) custom-call(s32[2]{0:T(128)S(1)} %pad_add_fusion.where_ref, bf16[384,1536]{1,0:T(8,128)(2,1)S(1)} %fusion.17.q_ref, bf16[2,384,512]{2,1,0:T(8,128)(2,1)S(1)} %pad_maximum_fusion.refs_0_, bf16[2,384,512]{2,1,0:T(8,128)(2,1)S(1)} %collective-permute-done.refs_1_, ...), custom_call_target="tpu_custom_call" | custom-call | tf_op jit(solution)/shard_map/attn_forward/pallas_call | solution.py:563
  203.9 24.8 %collective-permute-done.3.refs_6_ = bf16[384,1536]{1,0:T(8,128)(2,1)} collective-permute-done((bf16[384,1536]{1,0:T(8,128)(2,1)}, bf16[384,1536]{1,0:T(8,128)(2,1)}, u32[]{:S(2)}, u32[]{:S(2)}) %collective-permute-start.3) | collective-permute-done | bytes 1179680 | tf_op jit(solution)/shard_map/ppermute | solution.py:856
  230.1 4.5 multiply_reduce_fusion.2
  237.3 21.3 %collective-permute-done.5 = bf16[384,1536]{1,0:T(8,128)(2,1)S(1)} collective-permute-done((bf16[384,1536]{1,0:T(8,128)(2,1)}, bf16[384,1536]{1,0:T(8,128)(2,1)S(1)}, u32[]{:S(2)}, u32[]{:S(2)}) %collective-permute-start.5) | collective-permute-done | bytes 1179680 | tf_op jit(solution)/shard_map/ppermute | solution.py:856
  259.7 176.7 %feed_forward.1 = (f32[384,1536]{1,0:T(8,128)}, bf16[4,384,1536]{2,1,0:T(8,128)(2,1)}, bf16[8,3,192,1728]{3,2,1,0:T(8,128)(2,1)}) custom-call(bf16[384,1536]{1,0:T(8,128)(2,1)} %multiply_convert_fusion.refs_0_, bf16[1536,1728]{1,0:T(8,128)(2,1)} %all-gather.4.cloned.1.call-done.refs_1_, bf16[1536,1728]{1,0:T(8,128)(2,1)} %all-gather.6.cloned.1.call-done.refs_2_, ...), custom_call_target="tpu_custom_call" | custom-call | tf_op jit(solution)/shard_map/feed_forward/pallas_call | solution.py:799
  442.8 3.0 convolution_convert_fusion.3.refs_4_
  445.8 73.5 %attn_backward.1 = (bf16[384,1536]{1,0:T(8,128)(2,1)}, bf16[384,1024]{1,0:T(8,128)(2,1)}, f32[2,128]{1,0:T(2,128)}) custom-call(s32[1]{0:T(128)} %copy.65.length_ref, bf16[384,1536]{1,0:T(8,128)(2,1)} %copy-done, bf16[2,384,512]{2,1,0:T(8,128)(2,1)} %copy-done.1, bf16[2,384,512]{2,1,0:T(8,128)(2,1)} %copy-done.4, bf16[2,384,512]{2,1,0:T(8,128)(2,1)} %copy-done.3, ...), custom_call_target="tpu_custom_call" | custom-call | flops 120000004096 | tf_op jit(solution)/shard_map/attn_backward/pallas_call | solution.py:591
  521.1 2.6 collective-permute-start.7
  525.4 2.7 fusion.4
  528.2 4.3 fusion.10
  532.8 6.7 %convolution_convert_fusion = bf16[1536,1536]{1,0:T(8,128)(2,1)} fusion(bf16[384,1536]{1,0:T(8,128)(2,1)} %get-tuple-element.53, bf16[384,1536]{1,0:T(8,128)(2,1)} %param.13, f32[1536]{0:T(1024)} %copy-done.39, f32[384]{0:T(512)S(1)} %copy-done.47), kind=kOutput, calls=%fused_computation | convolution fusion | flops 1816657920 | bytes 7085568 | tf_op jit(solution)/shard_map/dot_general | solution.py:66
  539.6 4.4 convolution_convert_fusion.1
  546.6 4.2 fusion.13
  550.8 3.6 convolution_convert_fusion.2
  556.3 89.0 %sum_all.1 = (f32[48,1536]{1,0:T(8,128)S(1)}, f32[48,1536]{1,0:T(8,128)S(1)}, f32[48,1024]{1,0:T(8,128)S(1)}, f32[48,128]{1,0:T(8,128)S(1)}, bf16[384,1536]{1,0:...) custom-call(bf16[8,4,48,1536]{3,2,1,0:T(8,128)(2,1)} %bitcast.67, bf16[8,4,48,1536]{3,2,1,0:T(8,128)(2,1)} %bitcast.66, ...), custom_call_target="tpu_custom_call" | custom-call | tf_op jit(solution)/shard_map/sum_all/pallas_call | solution.py:316
  648.9 3.7 convert_bitcast_fusion
  652.6 3.1 add_convert_fusion
  (213 shorter events, 49.1 us)
Async XLA Ops:
  7.2 4.7 copy-start.35
  7.2 4.7 copy-start.36
  7.2 252.5 %all-gather.4.cloned.1.call-start = ((), (), s32[]{:S(2)}) async-start(), calls=%async_computation.1 | async-start | bytes 6193152 | tf_op jit(solution)/shard_map/all_gather | solution.py:895
  84.2 175.5 %all-gather.6.cloned.1.call-start = ((), (), s32[]{:S(2)}) async-start(), calls=%async_computation.2 | async-start | bytes 6193152 | tf_op jit(solution)/shard_map/all_gather | solution.py:895
  85.0 174.7 %all-gather.8.cloned.1.call-start = ((), (), s32[]{:S(2)}) async-start(), calls=%async_computation.3 | async-start | bytes 6193152 | tf_op jit(solution)/shard_map/all_gather | solution.py:895
  85.7 563.1 %reduce-scatter.2.cloned.1.call-start = ((), (), s32[]{:S(2)}) async-start(), calls=%async_computation.4 | async-start | bytes 18579456 | tf_op jit(solution)/shard_map/reduce_scatter | solution.py:933
  88.7 8.9 %copy-start.32 = (f32[384,64]{0,1:T(8,128)}, f32[384,64]{0,1:T(8,128)S(1)}, u32[]{:S(2)}) copy-start(f32[384,64]{0,1:T(8,128)S(1)} %copy.52) | copy-start | bytes 294916
  90.4 5.1 copy-start.39
  101.1 91.7 %copy-start.1 = (bf16[2,384,512]{2,1,0:T(8,128)(2,1)}, bf16[2,384,512]{2,1,0:T(8,128)(2,1)S(1)}, u32[]{:S(2)}) copy-start(bf16[2,384,512]{2,1,0:T(8,128)(2,1)S(1)} %pad_maximum_fusion.refs_0_) | copy-start | bytes 2359300
  101.1 33.2 %collective-permute-start.2 = (bf16[2,384,512]{2,1,0:T(8,128)(2,1)S(1)}, bf16[2,384,512]{2,1,0:T(8,128)(2,1)S(1)}, u32[]{:S(2)}, u32[]{:S(2)}) collective-permute-start(bf16[2,384,512]{2,1,0:T(8,128)(2,1)S(1)} %pad_maximum_fusion.refs_0_), channel_id=1, source_target_pairs={{0,3},{4,7},{8,11},{12,15},{16,19},{20,23},{24,27},{28,31}} | collective-permute-start | bytes 2359304 | tf_op jit(solution)/shard_map/ppermute | solution.py:856
  105.5 34.7 %collective-permute-start.1 = (bf16[2,384,512]{2,1,0:T(8,128)(2,1)S(1)}, bf16[2,384,512]{2,1,0:T(8,128)(2,1)S(1)}, u32[]{:S(2)}, u32[]{:S(2)}) collective-permute-start(bf16[2,384,512]{2,1,0:T(8,128)(2,1)S(1)} %pad_maximum_fusion.refs_0_), channel_id=1, source_target_pairs={{0,2},{1,3},{4,6},{5,7},{8,10},{9,11},{12,14},{13,15},{16,18},{17,... | collective-permute-start | bytes 2359304 | tf_op jit(solution)/shard_map/ppermute | solution.py:856
  114.7 41.8 %collective-permute-start = (bf16[2,384,512]{2,1,0:T(8,128)(2,1)S(1)}, bf16[2,384,512]{2,1,0:T(8,128)(2,1)S(1)}, u32[]{:S(2)}, u32[]{:S(2)}) collective-permute-start(bf16[2,384,512]{2,1,0:T(8,128)(2,1)S(1)} %pad_maximum_fusion.refs_0_), channel_id=1, source_target_pairs={{0,1},{1,2},{2,3},{4,5},{5,6},{6,7},{8,9},{9,10},{10,11},{12,13},{... | collective-permute-start | bytes 2359304 | tf_op jit(solution)/shard_map/ppermute | solution.py:856
  134.1 42.6 %copy-start.33 = (f32[384,64]{0,1:T(8,128)S(1)}, f32[384,64]{0,1:T(8,128)}, u32[]{:S(2)}) copy-start(f32[384,64]{0,1:T(8,128)} %copy-done.32) | copy-start | bytes 294916
  134.3 58.5 %copy-start.2 = (bf16[2,384,512]{2,1,0:T(8,128)(2,1)}, bf16[2,384,512]{2,1,0:T(8,128)(2,1)S(1)}, u32[]{:S(2)}) copy-start(bf16[2,384,512]{2,1,0:T(8,128)(2,1)S(1)} %collective-permute-done.2.refs_3_) | copy-start | bytes 2359300
  140.2 52.6 %copy-start.3 = (bf16[2,384,512]{2,1,0:T(8,128)(2,1)}, bf16[2,384,512]{2,1,0:T(8,128)(2,1)S(1)}, u32[]{:S(2)}) copy-start(bf16[2,384,512]{2,1,0:T(8,128)(2,1)S(1)} %collective-permute-done.1.refs_2_) | copy-start | bytes 2359300
  156.5 36.3 %copy-start.4 = (bf16[2,384,512]{2,1,0:T(8,128)(2,1)}, bf16[2,384,512]{2,1,0:T(8,128)(2,1)S(1)}, u32[]{:S(2)}) copy-start(bf16[2,384,512]{2,1,0:T(8,128)(2,1)S(1)} %collective-permute-done.refs_1_) | copy-start | bytes 2359300
  156.5 72.3 %collective-permute-start.3 = (bf16[384,1536]{1,0:T(8,128)(2,1)}, bf16[384,1536]{1,0:T(8,128)(2,1)}, u32[]{:S(2)}, u32[]{:S(2)}) collective-permute-start(bf16[384,1536]{1,0:T(8,128)(2,1)} %fusion.16.refs_3_.refs_4_), channel_id=1, source_target_pairs={{0,2},{1,3},{2,0},{3,1},{4,6},{5,7},{6,4},{7,5},{8,10},{9,11},{10,... | collective-permute-start | bytes 3538952 | tf_op jit(solution)/shard_map/ppermute | solution.py:856
  191.7 42.9 %copy-start = (bf16[384,1536]{1,0:T(8,128)(2,1)}, bf16[384,1536]{1,0:T(8,128)(2,1)S(1)}, u32[]{:S(2)}) copy-start(bf16[384,1536]{1,0:T(8,128)(2,1)S(1)} %fusion.17.q_ref) | copy-start | bytes 3538948
  191.7 38.4 %copy-start.20 = (bf16[384,1536]{1,0:T(8,128)(2,1)S(1)}, bf16[384,1536]{1,0:T(8,128)(2,1)}, u32[]{:S(2)}) copy-start(bf16[384,1536]{1,0:T(8,128)(2,1)} %param.13) | copy-start | bytes 3538948
  191.7 45.6 %collective-permute-start.4 = (bf16[384,1536]{1,0:T(8,128)(2,1)}, bf16[384,1536]{1,0:T(8,128)(2,1)S(1)}, u32[]{:S(2)}, u32[]{:S(2)}) collective-permute-start(bf16[384,1536]{1,0:T(8,128)(2,1)} %fusion.16.refs_3_.refs_4_), channel_id=1, source_target_pairs={{1,2},{2,1},{5,6},{6,5},{9,10},{10,9},{13,14},{14,13},{17,18},{18,... | collective-permute-start | bytes 3538952 | tf_op jit(solution)/shard_map/ppermute | solution.py:856
  203.9 30.7 %copy-start.9 = (bf16[384,1536]{1,0:T(8,128)(2,1)}, bf16[384,1536]{1,0:T(8,128)(2,1)S(1)}, u32[]{:S(2)}) copy-start(bf16[384,1536]{1,0:T(8,128)(2,1)S(1)} %get-tuple-element.42.refs_5_) | copy-start | bytes 3538948
  203.9 30.7 %copy-start.11 = (f32[4,8,384]{2,1,0:T(8,128)}, f32[4,8,384]{2,1,0:T(8,128)S(1)}, u32[]{:S(2)}) copy-start(f32[4,8,384]{2,1,0:T(8,128)S(1)} %get-tuple-element.52.refs_6_) | copy-start | bytes 147460
  228.8 29.8 %collective-permute-start.5 = (bf16[384,1536]{1,0:T(8,128)(2,1)}, bf16[384,1536]{1,0:T(8,128)(2,1)S(1)}, u32[]{:S(2)}, u32[]{:S(2)}) collective-permute-start(bf16[384,1536]{1,0:T(8,128)(2,1)} %collective-permute-done.3.refs_6_), channel_id=1, source_target_pairs={{2,3},{1,0},{6,7},{5,4},{10,11},{9,8},{14,15},{13,12},{18,19},{17,... | collective-permute-start | bytes 3538952 | tf_op jit(solution)/shard_map/ppermute | solution.py:856
  230.1 5.9 copy-start.34
  445.8 73.5 %slice-start = ((s8[4718592]{0:T(1024)(128)(4,1)}), s8[4194304]{0:T(1024)(128)(4,1)S(1)}, s32[]{:S(2)}) async-start(s8[4718592]{0:T(1024)(128)(4,1)} %bitcast.64), calls=%async_computation.5 | async-start | bytes 8388608
  445.8 73.6 %slice-start.1 = ((s8[4718592]{0:T(1024)(128)(4,1)}), s8[524288]{0:T(1024)(128)(4,1)S(1)}, s32[]{:S(2)}) async-start(s8[4718592]{0:T(1024)(128)(4,1)} %bitcast.64), calls=%async_computation.6 | async-start | bytes 1048576
  519.4 6.0 copy-start.37
  519.4 8.8 %slice-start.2 = ((s8[4718592]{0:T(1024)(128)(4,1)}), s8[4194304]{0:T(1024)(128)(4,1)S(1)}, s32[]{:S(2)}) async-start(s8[4718592]{0:T(1024)(128)(4,1)} %bitcast.81), calls=%async_computation.7 | async-start | bytes 8388608
  521.1 33.4 %collective-permute-start.7 = (bf16[384,1536]{1,0:T(8,128)(2,1)}, bf16[384,1536]{1,0:T(8,128)(2,1)}, u32[]{:S(2)}, u32[]{:S(2)}) collective-permute-start(bf16[384,1536]{1,0:T(8,128)(2,1)} %get-tuple-element.78), channel_id=1, source_target_pairs={{0,1},{3,2},{4,5},{7,6},{8,9},{11,10},{12,13},{15,14},{16,17},{19,... | collective-permute-start | bytes 3538952 | tf_op jit(solution)/shard_map/ppermute | solution.py:856
  523.6 125.2 %collective-permute-start.6 = (bf16[384,1536]{1,0:T(8,128)(2,1)}, bf16[384,1536]{1,0:T(8,128)(2,1)}, u32[]{:S(2)}, u32[]{:S(2)}) collective-permute-start(bf16[384,1536]{1,0:T(8,128)(2,1)} %get-tuple-element.78), channel_id=1, source_target_pairs={{1,2},{2,1},{5,6},{6,5},{9,10},{10,9},{13,14},{14,13},{17,18},{18,... | collective-permute-start | bytes 3538952 | tf_op jit(solution)/shard_map/ppermute | solution.py:856
  532.8 6.8 %copy-start.10 = (bf16[384,1536]{1,0:T(8,128)(2,1)S(1)}, bf16[384,1536]{1,0:T(8,128)(2,1)}, u32[]{:S(2)}) copy-start(bf16[384,1536]{1,0:T(8,128)(2,1)} %copy-done.9) | copy-start | bytes 3538948
  532.8 6.7 %copy-start.18 = (f32[384,1536]{1,0:T(8,128)S(1)}, f32[384,1536]{1,0:T(8,128)}, u32[]{:S(2)}) copy-start(f32[384,1536]{1,0:T(8,128)} %copy-done.17) | copy-start | bytes 7077892
  (38 other events, 98.9 us)
Sparse Core Ops, SparseCore 0:
  84.4 49.8 all-gather.3
  136.1 42.2 all-gather.5
  180.3 42.2 all-gather.7
  436.6 116.9 reduce-scatter.1

commit v4 on v3

--- a/solution.py
+++ b/solution.py
@@ -94,7 +94,8 @@
     pl.semaphore_wait(barrier, len(partners))
 
 
-def gather_kernel(parts, riders, *refs):
+def gather_kernel(parts, hops, *refs):
+    riders = len(hops)
     srcs, riding = refs[:parts], refs[parts : parts + riders]
     outs, landed = refs[parts + riders : 2 * parts + riders], refs[2 * parts + riders :][:riders]
     own_sem, send, recv, ride_send, ride_recv = refs[2 * parts + 2 * riders :]
@@ -102,7 +103,7 @@
     greet(dp, ctx, (1, 2, 4), (1, 2, 3))
 
     def ride(i):
-        return remote(riding[i], landed[i], ride_send.at[i], ride_recv.at[i], dp, ctx ^ 1)
+        return remote(riding[i], landed[i], ride_send.at[i], ride_recv.at[i], dp, ctx ^ hops[i])
 
     def line(p, s):
         return remote(
@@ -167,10 +168,10 @@
         ride(i).wait()
 
 
-def gather_all(shards, riding, cid):
+def gather_all(shards, riding, hops, cid):
     parts, riders = len(shards), len(riding)
     outs = pl.pallas_call(
-        functools.partial(gather_kernel, parts, riders),
+        functools.partial(gather_kernel, parts, hops),
         in_specs=[ANY] * (parts + riders),
         out_specs=[ANY] * (parts + riders),
         out_shape=[jax.ShapeDtypeStruct((8, 4) + s.shape, s.dtype) for s in shards]
@@ -189,76 +190,94 @@
     return full + list(outs[parts:])
 
 
-def sum_kernel(parts, hops, *refs):
-    riders = len(hops)
-    ins, riding = refs[:parts], refs[parts : parts + riders]
-    refs = refs[parts + riders :]
-    outs, landed = refs[:parts], refs[parts : parts + riders]
-    refs = refs[parts + riders :]
-    keep, got, plane1, plane2, lines = (refs[i * parts : (i + 1) * parts] for i in range(5))
+SUM_PARTS = ((0, 0, 768), (0, 768, 768), (1, 0, 768), (1, 768, 768), (2, 0, 1024))
+
+
+def sum_kernel(hops, *refs):
+    riders, parts = len(hops), len(SUM_PARTS) + 1
+    lefts, rights, ready, riding = refs[:3], refs[3:6], refs[6], refs[7 : 7 + riders]
+    refs = refs[7 + riders :]
+    outs, landed = refs[:4], refs[4 : 4 + riders]
+    refs = refs[4 + riders :]
+    terms, got, plane1, plane2, lines = (refs[i * parts : (i + 1) * parts] for i in range(5))
     load, send, recv, ride_send, ride_recv = refs[5 * parts :]
     dp, ctx = lax.axis_index("dp"), lax.axis_index("ctx")
+    chip = dp // 2
+    core = dp - 2 * chip
+    halves = (pl.ds(0, 2), pl.ds(2, 2))
+    rows = lefts[0].shape[1]
 
     def ride(i):
         return remote(riding[i], landed[i], ride_send.at[i], ride_recv.at[i], dp, ctx ^ hops[i])
 
-    chip = dp // 2
-    core = dp - 2 * chip
-
-    halves = (pl.ds(0, 2), pl.ds(2, 2))
-
-    def fetch(p, k):
-        return pltpu.make_async_copy(
-            ins[p].at[2 * (chip ^ k) + core], keep[p].at[k], load.at[p, k]
-        )
+    def kept(k):
+        return 2 * (chip ^ k) + core
+
+    fetch = pltpu.make_async_copy(ready, terms[-1], load)
+
+    def multiply(p):
+        which, start, width = SUM_PARTS[p]
+        step = 2 * 4 * terms[p].shape[2]
+
+        def tile(t, carry):
+            cols = pl.ds(pl.multiple_of(t * step, step), step)
+            product = mdot(lefts[which][:, cols], rights[which][:, start : start + width], TN)
+            terms[p][pl.ds(2 * t, 2)] = product.astype(bf16).reshape(2, *terms[p].shape[1:])
+            return carry
+
+        lax.fori_loop(0, rows // step, tile, 0)
 
     def across(p, k):
         return remote(
-            ins[p].at[2 * (chip ^ k) + (1 - core)], got[p].at[k],
+            terms[p].at[2 * (chip ^ k) + (1 - core)], got[p].at[k],
             send.at[p, k], recv.at[p, k], dp ^ 1, ctx,
         )
 
     def first(p, w, i):
         k = (1 << w) if i == 0 else 3
         return remote(
-            keep[p].at[k, halves[w]], plane1[p].at[i, halves[w]],
+            terms[p].at[kept(k), halves[w]], plane1[p].at[i, halves[w]],
             send.at[p, 4 + 2 * w + i], recv.at[p, 4 + 2 * w + i], dp ^ (2 << w), ctx,
         )
 
     def second(p, w):
-        k = 1 << (1 - w)
         return remote(
-            keep[p].at[k, halves[w]], plane2[p].at[halves[w]],
+            terms[p].at[kept(1 << (1 - w)), halves[w]], plane2[p].at[halves[w]],
             send.at[p, 8 + w], recv.at[p, 8 + w], dp ^ (2 << (1 - w)), ctx,
         )
 
     def line(p, s):
         return remote(
-            keep[p].at[0, ctx ^ s], lines[p].at[s - 1],
+            terms[p].at[kept(0), ctx ^ s], lines[p].at[s - 1],
             send.at[p, 9 + s], recv.at[p, 9 + s], dp, ctx ^ s,
         )
 
-    for p in range(parts):
-        for k in (3, 1, 2, 0):
-            fetch(p, k).start()
+    def add(target, term):
+        target[...] = (target[...].astype(f32) + term[...].astype(f32)).astype(bf16)
+
+    fetch.start()
     greet(dp, ctx, (1, 2, 4), (1, 2, 3))
-    for p in range(parts):
+    for i in range(riders):
+        ride(i).start()
+
+    def begin(p):
+        if p < parts - 1:
+            multiply(p)
+        else:
+            fetch.wait()
         for k in (3, 1, 2, 0):
             across(p, k).start()
-    for i in range(riders):
-        ride(i).start()
-
-    def add(target, term):
-        target[...] = (target[...].astype(f32) + term[...].astype(f32)).astype(bf16)
-
-    for step in range(parts + 3):
+
+    begin(0)
+    for step in range(parts + 2):
+        if step + 1 < parts:
+            begin(step + 1)
         if step < parts:
             p = step
             for k in (3, 1, 2, 0):
-                fetch(p, k).wait()
                 across(p, k).wait_recv()
                 for c in range(4):
-                    add(keep[p].at[k, c], got[p].at[k, c])
+                    add(terms[p].at[kept(k), c], got[p].at[k, c])
                 if k == 3:
                     for w in (0, 1):
                         first(p, w, 1).start()
@@ -268,30 +287,32 @@
             p = step - 1
             for w in (0, 1):
                 first(p, w, 1).wait_recv()
-                other = 1 << (1 - w)
                 for c in (2 * w, 2 * w + 1):
-                    add(keep[p].at[other, c], plane1[p].at[1, c])
+                    add(terms[p].at[kept(1 << (1 - w)), c], plane1[p].at[1, c])
                 second(p, w).start()
             for w in (0, 1):
                 first(p, w, 0).wait_recv()
                 for c in (2 * w, 2 * w + 1):
-                    add(keep[p].at[0, c], plane1[p].at[0, c])
+                    add(terms[p].at[kept(0), c], plane1[p].at[0, c])
         if 0 <= step - 2 < parts:
             p = step - 2
             for w in (0, 1):
                 second(p, w).wait_recv()
                 for c in (2 * w, 2 * w + 1):
-                    add(keep[p].at[0, c], plane2[p].at[c])
+                    add(terms[p].at[kept(0), c], plane2[p].at[c])
             for s in (3, 2, 1):
                 line(p, s).start()
-        if 0 <= step - 3 < parts:
-            p = step - 3
-            for s in (1, 2, 3):
-                line(p, s).wait_recv()
-            total = keep[p][0, ctx].astype(f32)
-            for s in (1, 2, 3):
-                total = total + lines[p][s - 1].astype(f32)
-            outs[p][...] = total
+    for p in range(parts):
+        for s in (1, 2, 3):
+            line(p, s).wait_recv()
+        total = terms[p][kept(0), ctx].astype(f32)
+        for s in (1, 2, 3):
+            total = total + lines[p][s - 1].astype(f32)
+        if p < parts - 1:
+            which, start, width = SUM_PARTS[p]
+            outs[which][:, start : start + width] = total
+        else:
+            outs[3][...] = total
     for p in range(parts):
         for k in range(4):
             across(p, k).wait_send()
@@ -305,33 +326,37 @@
         ride(i).wait()
 
 
-def sum_all(terms, riding, hops, cid):
-    parts, riders = len(terms), len(riding)
-    blocks = [t.reshape(8, 4, t.shape[0] // 32, t.shape[1]) for t in terms]
-    shapes = [b.shape[2:] for b in blocks]
-
-    def per(lead):
-        return [pltpu.VMEM(lead + s, bf16) for s in shapes]
+def sum_all(lefts, rights, ready, riding, hops, cid):
+    parts, riders = len(SUM_PARTS) + 1, len(riding)
+    rows = lefts[0].shape[1]
+    share = rows // 32
+    blocks = ready.reshape(8, 4, share, ready.shape[1])
+    widths = [width for _, _, width in SUM_PARTS] + [ready.shape[1]]
+    vmem = pl.BlockSpec(memory_space=pltpu.VMEM)
+
+    def per(*lead):
+        return [pltpu.VMEM(lead + (share, width), bf16) for width in widths]
 
     return pl.pallas_call(
-        functools.partial(sum_kernel, parts, hops),
-        in_specs=[ANY] * (parts + riders),
-        out_specs=[pl.BlockSpec(memory_space=pltpu.VMEM)] * parts + [ANY] * riders,
-        out_shape=[jax.ShapeDtypeStruct(s, f32) for s in shapes]
+        functools.partial(sum_kernel, hops),
+        in_specs=[vmem] * 6 + [ANY] * (1 + riders),
+        out_specs=[vmem] * 4 + [ANY] * riders,
+        out_shape=[jax.ShapeDtypeStruct((share, r.shape[1]), f32) for r in rights]
+        + [jax.ShapeDtypeStruct((share, ready.shape[1]), f32)]
         + [jax.ShapeDtypeStruct(r.shape, r.dtype) for r in riding],
-        scratch_shapes=per((4, 4)) + per((4, 4)) + per((2, 4)) + per((4,)) + per((3,))
+        scratch_shapes=per(8, 4) + per(4, 4) + per(2, 4) + per(4) + per(3)
         + [
-            pltpu.SemaphoreType.DMA((parts, 4)),
+            pltpu.SemaphoreType.DMA,
             pltpu.SemaphoreType.DMA((parts, 13)),
             pltpu.SemaphoreType.DMA((parts, 13)),
             pltpu.SemaphoreType.DMA((riders,)),
             pltpu.SemaphoreType.DMA((riders,)),
         ],
         compiler_params=pltpu.CompilerParams(
-            collective_id=cid, has_side_effects=True, vmem_limit_bytes=48 * 2**20
+            collective_id=cid, has_side_effects=True, vmem_limit_bytes=56 * 2**20
         ),
         name="sum_all",
-    )(*blocks, *riding)
+    )(*lefts, *rights, blocks, *riding)
 
 
 def causal_mask(rows, limit, key_axis):
@@ -339,46 +364,6 @@
     key = lax.broadcasted_iota(jnp.int32, shape, key_axis)
     row = lax.broadcasted_iota(jnp.int32, shape, 1 - key_axis)
     return jnp.where((key <= row) & (key < limit), 0.0, NEG_BIG).astype(f32)
-
-
-def attn_fwd_kernel(blocks, where_ref, q_ref, *refs):
-    kv_refs, (o_ref, log_ref, mask, acc) = refs[:blocks], refs[blocks:]
-    rows = q_ref.shape[0]
-    mine, limit = where_ref[0], where_ref[1]
-
-    @pl.when(pl.program_id(0) == 0)
-    def _():
-        mask[...] = causal_mask(rows, limit, 1)
-
-    def head(kv_ref, pair, diagonal):
-        keys = kv_ref[0][:, pair * HD : (pair + 1) * HD]
-        values = kv_ref[1][:, pair * HD : (pair + 1) * HD]
-        extended = jnp.concatenate([values, jnp.ones_like(values)], -1)
-        for g in range(GROUP):
-            h = pair * GROUP + g
-            scores = mdot(q_ref[:, h * HD : (h + 1) * HD], keys, NT)
-            if diagonal:
-                scores = scores + mask[...]
-            term = mdot(jnp.exp(scores).astype(bf16), extended)
-            acc[h] = term if diagonal else acc[h] + term
-
-    for pair in range(2):
-        head(kv_refs[0], pair, True)
-    for back in range(1, blocks):
-
-        @pl.when(mine >= back)
-        def _():
-            for pair in range(2):
-                head(kv_refs[back], pair, False)
-
-    lane = lax.broadcasted_iota(jnp.int32, (rows, 2 * HD), 1)
-    logs = jnp.zeros((rows, 2 * HD), f32)
-    for h in range(2 * GROUP):
-        full = acc[h]
-        total = full[:, HD : HD + 1]
-        o_ref[:, h * HD : (h + 1) * HD] = (full[:, :HD] / total).astype(bf16)
-        logs = jnp.where(lane == h, jnp.log(total), logs)
-    log_ref[0] = jnp.transpose(logs)[:8]
 
 
 def split_dot(values, weights, dims):
@@ -412,6 +397,225 @@
     scaled = grad_upper * gain
     grad_lower = factor * (scaled - unit_rows * head_means(scaled * unit_rows))
     return grad_lower, jnp.sum(grad_upper * unit_rows, axis=0, keepdims=True)
+
+
+def norm_rotate(raw, cosine, signed_sine, gain):
+    values = raw * lax.rsqrt(head_means(raw * raw) + EPSILON) * gain
+    return values * cosine + half_swap(values) * signed_sine
+
+
+def attn_fwd_kernel(*refs):
+    length_ref, normed, w_kv, cosine, sine, gains, tokens, gain_mid = refs[:8]
+    query_hbm, out_hbm, rows_hbm, two_hbm = refs[8:12]
+    q_ref, o_ref, log_ref, q_raw, k_raw, hidden, mid = refs[12:19]
+    kv_hbm, three_hbm = refs[19:23], refs[23]
+    w_query, w_out, kv, acc, mask, load, store, send, recv = refs[24:]
+    rows, width = normed.shape
+    half = KVH * HD
+    dp, mine = lax.axis_index("dp"), lax.axis_index("ctx")
+    middle = (mine == 1) | (mine == 2)
+
+    loads = [
+        pltpu.make_async_copy(query_hbm, w_query, load.at[0]),
+        pltpu.make_async_copy(out_hbm, w_out, load.at[1]),
+    ]
+
+    def lift(k):
+        return remote(kv.at[0], kv.at[k], send.at[k - 1], recv.at[k - 1], dp, mine + k)
+
+    lift_on = remote(kv.at[2], kv.at[3], send.at[2], recv.at[2], dp, mine + 1)
+    rows_three = remote(rows_hbm, three_hbm, send.at[3], recv.at[3], dp, mine ^ 3)
+    rows_on = remote(two_hbm, three_hbm, send.at[4], recv.at[3], dp, mine ^ 1)
+
+    def keep(k):
+        return pltpu.make_async_copy(kv.at[k], kv_hbm[k], store.at[k])
+
+    for copy in loads:
+        copy.start()
+    greet(dp, mine, (), (1, 2, 3))
+
+    for i in range(2):
+        cols = slice(4 * i * HD, (4 * i + 4) * HD)
+        raw = mdot(normed[...], w_kv[:, cols])
+        k_raw[:, cols] = raw
+        for j in range(2):
+            part = slice(2 * j * HD, (2 * j + 2) * HD)
+            turned = norm_rotate(raw[:, part], cosine[...], sine[...], gains[1:2, :])
+            kv[0, 0, :, (4 * i + 2 * j) * HD : (4 * i + 2 * j + 2) * HD] = turned.astype(bf16)
+        value = mdot(normed[...], w_kv[:, half + 4 * i * HD : half + (4 * i + 4) * HD])
+        kv[0, 1, :, cols] = value.astype(bf16)
+
+    @pl.when(mine <= 2)
+    def _():
+        lift(1).start()
+
+    @pl.when(mine <= 1)
+    def _():
+        lift(2).start()
+
+    @pl.when(mine == 1)
+    def _():
+        rows_on.start()
+
+    @pl.when(mine == 2)
+    def _():
+        rows_three.start()
+
+    keep(0).start()
+    mask[...] = causal_mask(rows, length_ref[0] - mine * rows, 1)
+    loads[0].wait()
+
+    def make_query(i, carry):
+        cols = pl.ds(pl.multiple_of(i * 2 * GROUP * HD, 2 * GROUP * HD), 2 * GROUP * HD)
+        raw = mdot(normed[...], w_query[:, cols])
+        q_raw[:, cols] = raw
+        turned = [
+            norm_rotate(
+                raw[:, 2 * j * HD : (2 * j + 2) * HD], cosine[...], sine[...], gains[0:1, :]
+            )
+            for j in range(GROUP)
+        ]
+        low = jnp.concatenate(turned, 1).astype(bf16)
+        q_ref[:, cols] = (low.astype(f32) * (HD**-0.5)).astype(bf16)
+        return carry
+
+    lax.fori_loop(0, PAIRS, make_query, 0)
+
+    def attend(k):
+        def pairs(i, carry):
+            two = pl.ds(pl.multiple_of(i * 2 * HD, 2 * HD), 2 * HD)
+            cols = pl.ds(pl.multiple_of(i * 2 * GROUP * HD, 2 * GROUP * HD), 2 * GROUP * HD)
+            both_keys, both_values, queries = kv[k, 0, :, two], kv[k, 1, :, two], q_ref[:, cols]
+            for pair in range(2):
+                keys = both_keys[:, pair * HD : (pair + 1) * HD]
+                values = both_values[:, pair * HD : (pair + 1) * HD]
+                extended = jnp.concatenate([values, jnp.ones_like(values)], -1)
+                for g in range(GROUP):
+                    h = pair * GROUP + g
+                    scores = mdot(queries[:, h * HD : (h + 1) * HD], keys, NT)
+                    if k == 0:
+                        scores = scores + mask[...]
+                    term = mdot(jnp.exp(scores).astype(bf16), extended)
+                    place = 2 * GROUP * i + h
+                    acc[place] = term if k == 0 else acc[place] + term
+            return carry
+
+        lax.fori_loop(0, PAIRS, pairs, 0)
+
+    attend(0)
+    for k in (1, 2, 3):
+
+        @pl.when(mine >= k)
+        def _():
+            (lift_on if k == 3 else lift(k)).wait_recv()
+            if k == 2:
+
+                @pl.when(mine == 2)
+                def _():
+                    lift_on.start()
+                    rows_on.start()
+
+            keep(k).start()
+            attend(k)
+
+        if k == 1:
+
+            @pl.when(mine <= 1)
+            def _():
+                lift(1).wait_send()
+                lift(2).wait_send()
+
+            @pl.when(mine == 1)
+            def _():
+                rows_three.start()
+
+    lane = lax.broadcasted_iota(jnp.int32, (rows, 2 * HD), 1)
+
+    def finish(i, carry):
+        cols = pl.ds(pl.multiple_of(i * 2 * GROUP * HD, 2 * GROUP * HD), 2 * GROUP * HD)
+        logs = jnp.zeros((rows, 2 * HD), f32)
+        heads = []
+        for h in range(2 * GROUP):
+            full = acc[2 * GROUP * i + h]
+            total = full[:, HD : HD + 1]
+            heads.append(full[:, :HD] / total)
+            logs = jnp.where(lane == h, jnp.log(total), logs)
+        o_ref[:, cols] = jnp.concatenate(heads, 1).astype(bf16)
+        log_ref[i] = jnp.transpose(logs)[:8]
+        return carry
+
+    lax.fori_loop(0, PAIRS, finish, 0)
+
+    loads[1].wait()
+    tile = 256
+
+    def project(t, carry):
+        cols = pl.ds(pl.multiple_of(t * tile, tile), tile)
+        hidden[:, cols] = tokens[:, cols].astype(f32) + mdot(o_ref[...], w_out[cols, :], NT)
+        return carry
+
+    lax.fori_loop(0, width // tile, project, 0)
+    value = hidden[...]
+    factor = lax.rsqrt(jnp.mean(value * value, axis=-1, keepdims=True) + EPSILON)
+    mid[...] = (value * factor * gain_mid[...]).astype(bf16)
+
+    rows_three.wait_recv()
+
+    @pl.when(middle)
+    def _():
+        rows_three.wait_send()
+        rows_on.wait_send()
+
+    @pl.when(mine == 2)
+    def _():
+        lift(1).wait_send()
+        lift_on.wait_send()
+
+    keep(0).wait()
+    for k in (1, 2, 3):
+
+        @pl.when(mine >= k)
+        def _():
+            keep(k).wait()
+
+
+def attn_forward(length, normed, full_kv, tables, gains, tokens, gain_mid, weights, ups, cid):
+    rows, width = normed.shape
+    vmem = pl.BlockSpec(memory_space=pltpu.VMEM)
+    keys = jax.ShapeDtypeStruct((2, rows, KVH * HD), bf16)
+    rows_like = jax.ShapeDtypeStruct((rows, width), bf16)
+    heads = jax.ShapeDtypeStruct((rows, H * HD), bf16)
+    return pl.pallas_call(
+        attn_fwd_kernel,
+        in_specs=[pl.BlockSpec(memory_space=pltpu.SMEM)] + [vmem] * 7 + [ANY] * 4,
+        out_specs=[vmem] * 7 + [ANY] * 5,
+        out_shape=[
+            heads,
+            heads,
+            jax.ShapeDtypeStruct((PAIRS, 8, rows), f32),
+            jax.ShapeDtypeStruct((rows, H * HD), f32),
+            jax.ShapeDtypeStruct((rows, KVH * HD), f32),
+            jax.ShapeDtypeStruct((rows, width), f32),
+            rows_like,
+        ]
+        + [keys] * 4
+        + [rows_like],
+        scratch_shapes=[
+            pltpu.VMEM((width, H * HD), bf16),
+            pltpu.VMEM((width, H * HD), bf16),
+            pltpu.VMEM((4, 2, rows, KVH * HD), bf16),
+            pltpu.VMEM((H, rows, 2 * HD), f32),
+            pltpu.VMEM((rows, rows), f32),
+            pltpu.SemaphoreType.DMA((2,)),
+            pltpu.SemaphoreType.DMA((4,)),
+            pltpu.SemaphoreType.DMA((5,)),
+            pltpu.SemaphoreType.DMA((4,)),
+        ],
+        compiler_params=pltpu.CompilerParams(
+            collective_id=cid, has_side_effects=True, vmem_limit_bytes=56 * 2**20
+        ),
+        name="attn_forward",
+    )(length, normed, full_kv, *tables, gains, tokens, gain_mid, *weights, *ups)
 
 
 def attn_bwd_kernel(blocks, length_ref, q_ref, *refs):
@@ -556,29 +760,6 @@
 
 def log_spec(rows):
     return pl.BlockSpec((1, 8, rows), lambda i, *_: (i, 0, 0))
-
-
-def attn_forward(where, query, kv_blocks):
-    rows, blocks = query.shape[0], len(kv_blocks)
-    return pl.pallas_call(
-        functools.partial(attn_fwd_kernel, blocks),
-        grid_spec=pltpu.PrefetchScalarGridSpec(
-            num_scalar_prefetch=1,
-            grid=(PAIRS,),
-            in_specs=[head_spec(rows)] + [kv_spec(rows)] * blocks,
-            out_specs=[head_spec(rows), log_spec(rows)],
-            scratch_shapes=[
-                pltpu.VMEM((rows, rows), f32),
-                pltpu.VMEM((2 * GROUP, rows, 2 * HD), f32),
-            ],
-        ),
-        out_shape=[
-            jax.ShapeDtypeStruct((rows, H * HD), bf16),
-            jax.ShapeDtypeStruct((PAIRS, 8, rows), f32),
-        ],
-        compiler_params=pltpu.CompilerParams(vmem_limit_bytes=48 * 2**20),
-        name="attn_forward",
-    )(where, query, *kv_blocks)
 
 
 def whole_spec(*shape):
@@ -866,15 +1047,16 @@
     def swap(block, r):
         return move(block, [(i, i ^ r) for i in range(ctx)])
 
-    def gather(blocks, riding, cid):
+    def gather(blocks, riding, hops, cid):
         if small:
-            return gather_all(blocks, riding, cid)
+            return gather_all(blocks, riding, hops, cid)
         full = [lax.all_gather(b, every, axis=0, tiled=True) for b in blocks]
-        return full + [swap(b, 1) for b in riding]
-
-    def collect(terms, riding, hops, cid):
+        return full + [swap(b, r) for b, r in zip(riding, hops)]
+
+    def collect(lefts, rights, ready, riding, hops, cid):
         if small:
-            return sum_all(terms, riding, hops, cid)
+            return sum_all(lefts, rights, ready, riding, hops, cid)
+        terms = [mdot(a, b, TN).astype(bf16) for a, b in zip(lefts, rights)] + [ready]
         return [
             lax.psum_scatter(t, every, scatter_dimension=0, tiled=True).astype(f32) for t in terms
         ] + [swap(block, r) for block, r in zip(riding, hops)]
@@ -884,48 +1066,45 @@
     valid_rows = (positions < length).astype(f32)[:, None]
     upstream = grad_out.astype(f32) * valid_rows
     upstream_low = upstream.astype(bf16)
-    full_kv, full_query, full_out_t, ups_near = gather(
-        [jnp.concatenate([w_key, w_value, extra], 1), w_query, w_out.T], [upstream_low], 1
+    full_kv, full_query, full_out_t, ups_near, ups_two = gather(
+        [jnp.concatenate([w_key, w_value, extra], 1), w_query, w_out.T],
+        [upstream_low, upstream_low],
+        (1, 2),
+        1,
     )
     kv_width = 2 * KVH * HD
     full_extra = full_kv[:, kv_width:].astype(f32)
     full_gain_in, full_gain_mid = full_extra[:, 0], full_extra[:, 1]
     full_qk = full_extra[:, 2].reshape(world, share)[:, :qk_share].reshape(-1)
-    full_gate, full_up, full_down_t = (
-        lax.all_gather(after(w, full_kv), "dp", axis=0, tiled=True)
-        for w in (w_gate, w_up, w_down.T)
-    )
-    full_kv = full_kv[:, :kv_width]
+    full_gate = lax.all_gather(w_gate, "dp", axis=0, tiled=True)
+    full_up = lax.all_gather(after(w_up, full_kv, full_gate), "dp", axis=0, tiled=True)
+    full_down_t = lax.all_gather(after(w_down.T, full_kv, full_gate), "dp", axis=0, tiled=True)
+    wide_kv, full_kv = full_kv, full_kv[:, :kv_width]
 
     inputs = tokens.astype(f32)
 
     normed_f, factor_in = rms_scale(inputs, full_gain_in)
     normed = normed_f.astype(bf16)
-    kv_raw = mdot(normed, full_kv)
-    key_raw = kv_raw[:, : KVH * HD].reshape(rows, KVH, HD)
-    value_low = kv_raw[:, KVH * HD :].astype(bf16)
-    gain_query = full_qk[:HD]
-    gain_key = full_qk[HD:]
-    key_normed, factor_key = rms_scale(key_raw, gain_key)
-    key_low = rotate(key_normed, cosine_table, sine_table).astype(bf16).reshape(rows, KVH * HD)
-    kv_own = jnp.stack([key_low, value_low])
-    kv_blocks = lift(kv_own)
-    far_low = after(upstream_low, kv_blocks)
-    ups_two = swap(far_low, 2)
-    ups_middle = move(far_low, [(1, 2), (2, 1)])
-    ups_ends = move(ups_two, [(2, 3), (1, 0)])
-    ups_three = jnp.where((mine == 1) | (mine == 2), ups_middle, ups_ends)
-    ups = [upstream_low, ups_near, ups_two, ups_three]
-    query_flat = mdot(normed, full_query)
-    query_raw = query_flat.reshape(rows, H, HD)
-    query_normed, factor_query = rms_scale(query_raw, gain_query)
-    query_low = rotate(query_normed, cosine_table, sine_table).astype(bf16)
-    query_low = (query_low * (HD**-0.5)).astype(bf16).reshape(rows, H * HD)
-
-    mixed_low, logs = attn_forward(where, query_low, kv_blocks)
-    hidden = inputs + mdot(mixed_low, full_out_t, NT)
-    normed_mid_f, factor_mid = rms_scale(hidden, full_gain_mid)
-    normed_mid = normed_mid_f.astype(bf16)
+    flat_cosine = jnp.concatenate([cosine_table[:, 0], cosine_table[:, 0]], 1)
+    flat_sine = jnp.concatenate([sine_table[:, 0], sine_table[:, 0]], 1)
+    turn_sign = jnp.where(jnp.arange(2 * HD) % HD < HD // 2, -1.0, 1.0).astype(f32)
+    tables = (flat_cosine, flat_sine * turn_sign)
+    pair_gains = jnp.concatenate([full_qk.reshape(2, HD), full_qk.reshape(2, HD)], 1)
+    query_low, mixed_low, logs, query_flat, key_flat, hidden, normed_mid, *landed = attn_forward(
+        seq_lens,
+        normed,
+        wide_kv,
+        tables,
+        pair_gains,
+        tokens,
+        full_gain_mid[None],
+        (full_query, full_out_t),
+        (upstream_low, ups_two),
+        3,
+    )
+    kv_blocks = landed[:4]
+    ups = [upstream_low, ups_near, ups_two] + landed[4:]
+    factor_mid = rms_scale(hidden, full_gain_mid)[1]
 
     grad_mid_term, down_parts, grad_ffn = feed_forward(
         normed_mid, ups, full_gate, full_up, full_down_t, lax.axis_size("dp"), 2
@@ -937,11 +1116,7 @@
     grad_hidden = upstream + grad_hidden_norm
     grad_branch = grad_hidden.astype(bf16)
     grad_mixed = mdot(grad_branch, full_out_t).astype(bf16)
-    grad_wout_t = mdot(grad_branch, mixed_low, TN).astype(bf16)
-
-    flat_cosine = jnp.concatenate([cosine_table[:, 0], cosine_table[:, 0]], 1)
-    flat_sine = jnp.concatenate([sine_table[:, 0], sine_table[:, 0]], 1)
-    turn_sign = jnp.where(jnp.arange(2 * HD) % HD < HD // 2, -1.0, 1.0).astype(f32)
+
     grad_query_low, grad_kv_low, gain_rows = attn_backward(
         seq_lens,
         query_low,
@@ -950,18 +1125,16 @@
         mixed_low,
         logs,
         query_flat,
-        kv_raw[:, : KVH * HD],
-        (flat_cosine, flat_sine * turn_sign),
-        jnp.concatenate([full_qk.reshape(2, HD), full_qk.reshape(2, HD)], 1),
-        3,
+        key_flat,
+        tables,
+        pair_gains,
+        5,
     )
     later = after(down_parts, grad_query_low)
     for_far, for_two, for_near = (later[mine ^ r] for r in (3, 2, 1))
     passed = move(for_far, [(0, 1), (3, 2)])
     down_terms = [later[mine], move(for_far, [(1, 2), (2, 1)])]
     for_two = (for_two.astype(f32) + passed.astype(f32)).astype(bf16)
-    grad_wquery = mdot(normed, grad_query_low, TN).astype(bf16)
-    grad_wkv = mdot(normed, grad_kv_low, TN).astype(bf16)
     grad_normed = mdot(grad_query_low, full_query, NT) + mdot(grad_kv_low, full_kv, NT)
     grad_input_norm, gain_terms_in = norm_back(grad_normed, inputs, factor_in, full_gain_in)
     grad_tokens = grad_hidden + grad_input_norm
@@ -972,7 +1145,9 @@
     )
     grad_extra = jnp.pad(grad_extra, ((0, 0), (0, 125))).astype(bf16)
     grad_wout, sum_query, sum_kv, sum_extra, *landed = collect(
-        [grad_wout_t, grad_wquery, grad_wkv, grad_extra],
+        (grad_branch, normed, normed),
+        (mixed_low, grad_query_low, grad_kv_low),
+        grad_extra,
         [for_two, for_near],
         (2, 1),
         4,

time: 673 us -> 642 us (0.954)
  Pallas kernels: 422 us -> 522 us
  starting transfers between devices: 42 us -> 4.43 us
  waiting for transfers between devices: 69.7 us -> 35.4 us
  matrix products: 38.7 us -> 8.55 us
  local copies, waits for them, and re-layouts: 38 us -> 19.2 us
  other arithmetic: 38 us -> 28.7 us
    pallas_call x3, Pallas kernels: 172 us -> 238 us  [the longest x1 93.8 us: sum_all(): pl.pallas_call(functools.partial(sum_kernel, hops), in_specs=[vmem] * 6 +...]
    ppermute x8 -> x2, waiting for transfers between devices: 68.3 us -> 6.89 us  [move(): return lax.ppermute(block, 'ctx', pairs)]
    ppermute x8 -> x2, starting transfers between devices: 41.8 us -> 4.27 us  [move(): return lax.ppermute(block, 'ctx', pairs)]
    dot_general x9 -> x3, matrix products: 38.7 us -> 8.55 us  [mdot(): return lax.dot_general(a, b, dims, preferred_element_type=f32)]
    all_gather x3, waiting for transfers between devices: 0.01 us -> 27.1 us  [the longest x1 27.1 us: shards(): lax.all_gather(after(w_down.T, full_kv, full_gate), 'dp', axis=0, tiled=T...]
    pallas_call x1, Pallas kernels: 177 us -> 202 us  [feed_forward(): pl.pallas_call(functools.partial(feed_forward_kernel, dp_blocks), in_spec...]
    mul x16 -> x0, local copies, waits for them, and re-layouts: 15.3 us -> none  [the longest x6 9.34 us: rotate(): return values * cosine_table + turned * sine_table]
    pallas_call x1, Pallas kernels: 73.5 us -> 81.9 us  [attn_backward(): pl.pallas_call(functools.partial(attn_bwd_kernel, blocks), grid=(PAIRS,),...]
  transfers between devices with their start and end apart: 12 -> 6, of which waited for: 4 -> 2; matrix products, arithmetic and copies ran while one was open for 14% -> 7% of each run, Pallas kernels for 26% -> 51%
where the time goes in v4:
time: 642 us; the launch traced here: 633 us
  Pallas kernels  522 us (81%)
  waiting for transfers between devices  35.4 us (6%)
  other arithmetic  28.7 us (4%)
  local copies, waits for them, and re-layouts  19.2 us (3%)
  between operations  15.1 us (2%)
  matrix products  8.55 us (1%)
    pallas_call x1, Pallas kernels, feed_forward(): pl.pallas_call(functools.partial(feed_forward_kernel, dp_blocks), in_spec...  202 us
    pallas_call x1, Pallas kernels, sum_all(): pl.pallas_call(functools.partial(sum_kernel, hops), in_specs=[vmem] * 6 +...  93.8 us
    pallas_call x1, Pallas kernels, gather_all(): pl.pallas_call(functools.partial(gather_kernel, parts, hops), in_specs=[A...  92.5 us
    pallas_call x1, Pallas kernels, attn_backward(): pl.pallas_call(functools.partial(attn_bwd_kernel, blocks), grid=(PAIRS,),...  81.9 us
    pallas_call x1, Pallas kernels, attn_forward(): pl.pallas_call(attn_fwd_kernel, in_specs=[pl.BlockSpec(memory_space=pltpu...  51.4 us
    all_gather x1, waiting for transfers between devices, shards(): lax.all_gather(after(w_down.T, full_kv, full_gate), 'dp', axis=0, tiled=T...  27.1 us
  transfers between devices with their start and end apart: 6, of which 2 were waited for; matrix products, arithmetic and copies ran while one was open for 7% of the time, Pallas kernels for 51%

profile of v4, /device:TPU:0, one launch (start us, length us, event | category | flops | bytes accessed | tf_op | source)
XLA Modules:
  0.0 632.9 jit_solution(12979055934133857894)
XLA Ops:
  10.1 1.5 fusion.19.refs_0_
  11.5 2.5 fusion.17.refs_3_.refs_4_.refs_10_
  14.1 92.5 %gather_all.1 = (bf16[8,4,48,1152]{3,2,1,0:T(8,128)(2,1)}, bf16[8,4,48,1536]{3,2,1,0:T(8,128)(2,1)}, bf16[8,4,48,1536]{3,2,1,0:T(8,128)(2,1)}, bf16[384,1536]{1,0:T(8,128)(2,1)}, bf16[384,1536]{1,0:T(8,128)(2,1)}) custom-call(bf16[48,1152]{1,0:T(8,128)(2,1)} %fusion.19.refs_0_, bf16[48,1536]{1,0:T(8,128)(2,1)} %refs_1_.1, bf16[48,1536]{1,0:T(8,128)(2,1)} %bitcast.46, ...), custom_call_target="tpu_custom_call" | custom-call | tf_op jit(solution)/shard_map/gather_all/pallas_call | solution.py:173
  107.4 1.0 slice_convert_fusion.2
  108.5 1.1 slice_reduce_fusion
  111.3 0.8 multiply_sine_fusion
  112.1 1.1 pad_maximum_fusion
  113.2 1.3 fusion.9.refs_1_.refs_2_
  114.6 51.4 %attn_forward.1 = (bf16[384,1536]{1,0:T(8,128)(2,1)}, bf16[384,1536]{1,0:T(8,128)(2,1)}, f32[4,8,384]{2,1,0:T(8,128)}, f32[384,1536]{1,0:T(8,128)}, f32[384,512]...) custom-call(s32[1]{0:T(128)} %copy.38.refs_0_.length_ref, ...), custom_call_target="tpu_custom_call" | custom-call | tf_op jit(solution)/shard_map/attn_forward/pallas_call | solution.py:588
  166.1 27.1 %all-gather.8.cloned.1.call-done.refs_3_ = bf16[1536,1728]{1,0:T(8,128)(2,1)} async-done(((bf16[192,1728]{1,0:T(8,128)(2,1)}), bf16[1536,1728]{1,0:T(8,128)(2,1)}) %all-gather.8.cloned.1.call-update) | async-done | bytes 5308432 | tf_op jit(solution)/shard_map/all_gather | solution.py:1081
  193.2 201.9 %feed_forward.1 = (f32[384,1536]{1,0:T(8,128)}, bf16[4,384,1536]{2,1,0:T(8,128)(2,1)}, bf16[8,3,192,1728]{3,2,1,0:T(8,128)(2,1)}) custom-call(bf16[384,1536]{1,0:T(8,128)(2,1)} %get-tuple-element.54.refs_0_, bf16[1536,1728]{1,0:T(8,128)(2,1)} %all-gather.4.cloned.1.call-done.refs_1_, bf16[1536,1728]{1,0:T(8,128)(2,1)} %all-gather.6.cloned.1.call-done.refs_2_, ...), custom_call_target="tpu_custom_call" | custom-call | tf_op jit(solution)/shard_map/feed_forward/pallas_call | solution.py:980
  395.2 1.6 copy-done
  397.5 1.2 multiply_reduce_fusion
  398.7 2.2 fusion.23
  400.9 3.0 convolution_convert_fusion.refs_4_
  404.0 81.9 %attn_backward.1 = (bf16[384,1536]{1,0:T(8,128)(2,1)}, bf16[384,1024]{1,0:T(8,128)(2,1)}, f32[2,128]{1,0:T(2,128)}) custom-call(s32[1]{0:T(128)} %copy.38.refs_0_.length_ref, bf16[384,1536]{1,0:T(8,128)(2,1)} %get-tuple-element.61.q_ref, bf16[2,384,512]{2,1,0:T(8,128)(2,1)} %get-tuple-element.62.refs_0_, bf16[2,384,512]{2,1,0:T(8,128)(2,1)} %get-tuple-element.63.refs_1_, ...), custom_call_target="tpu_custom_call" | custom-call | flops 120000004096 | tf_op jit(solution)/shard_map/attn_backward/pallas_call | solution.py:772
  485.9 4.0 dynamic-slice_bitcast_fusion
  489.9 2.6 collective-permute-start.1
  492.5 1.7 collective-permute-start
  494.2 2.0 fusion.25
  496.2 3.5 fusion.11
  503.9 4.5 fusion.14
  508.7 0.8 pad.21.clone
  509.5 6.9 %collective-permute-done.1 = bf16[384,1536]{1,0:T(8,128)(2,1)} collective-permute-done((bf16[384,1536]{1,0:T(8,128)(2,1)}, bf16[384,1536]{1,0:T(8,128)(2,1)}, u32[]{:S(2)}, u32[]{:S(2)}) %collective-permute-start.1) | collective-permute-done | bytes 1179680 | tf_op jit(solution)/shard_map/ppermute | solution.py:1037
  516.4 2.9 fusion.16.refs_7_
  519.4 93.8 %sum_all.1 = (f32[48,1536]{1,0:T(8,128)}, f32[48,1536]{1,0:T(8,128)}, f32[48,1024]{1,0:T(8,128)}, f32[48,128]{1,0:T(8,128)}, bf16[384,1536]{1,0:T(8,128)(2,1)}, /*index=5*/bf16[384,1536]{1,0:T(8,128)(2,1)}) custom-call(bf16[384,1536]{1,0:T(8,128)(2,1)} %copy-done.4, bf16[384,1536]{1,0:T(8,128)(2,1)} %fusion.9.refs_1_.refs_2_, ...), custom_call_target="tpu_custom_call" | custom-call | tf_op jit(solution)/shard_map/sum_all/pallas_call | solution.py:340
  613.2 1.4 slice_reduce_fusion.5
  614.6 1.5 slice_reduce_fusion.3
  616.1 1.6 fusion.24
  617.7 3.7 convert_bitcast_fusion
  621.5 3.1 add_convert_fusion
  624.6 0.7 copy.39
  (89 shorter events, 10.7 us)
Async XLA Ops:
  7.2 99.4 %all-gather.4.cloned.1.call-start = ((), (), s32[]{:S(2)}) async-start(), calls=%async_computation.1 | async-start | bytes 6193152 | tf_op jit(solution)/shard_map/all_gather | solution.py:1079
  7.9 158.1 %all-gather.6.cloned.1.call-start = ((), (), s32[]{:S(2)}) async-start(), calls=%async_computation.2 | async-start | bytes 6193152 | tf_op jit(solution)/shard_map/all_gather | solution.py:1080
  106.6 4.4 copy-start.1
  106.6 86.5 %all-gather.8.cloned.1.call-start = ((), (), s32[]{:S(2)}) async-start(), calls=%async_computation.3 | async-start | bytes 6193152 | tf_op jit(solution)/shard_map/all_gather | solution.py:1081
  107.4 510.3 %reduce-scatter.2.cloned.1.call-start = ((), (), s32[]{:S(2)}) async-start(), calls=%async_computation.4 | async-start | bytes 18579456 | tf_op jit(solution)/shard_map/reduce_scatter | solution.py:1112
  109.6 5.0 copy-start.14
  111.3 54.7 %copy-start.18 = (f32[384]{0:T(512)}, f32[384]{0:T(512)S(1)}, u32[]{:S(2)}) copy-start(f32[384]{0:T(512)S(1)} %add_rsqrt_fusion.1) | copy-start | bytes 4612
  395.1 1.7 copy-start
  395.2 2.3 copy-start.3
  396.8 1.9 copy-start.5
  397.5 3.4 slice-start.2
  398.7 2.2 slice-start.3
  400.9 3.0 copy-start.4
  400.9 93.2 %slice-start = ((s8[4718592]{0:T(1024)(128)(4,1)}), s8[4194304]{0:T(1024)(128)(4,1)S(1)}, s32[]{:S(2)}) async-start(s8[4718592]{0:T(1024)(128)(4,1)} %bitcast.33), calls=%async_computation.5 | async-start | bytes 8388608
  404.0 90.2 %slice-start.1 = ((s8[4718592]{0:T(1024)(128)(4,1)}), s8[524288]{0:T(1024)(128)(4,1)S(1)}, s32[]{:S(2)}) async-start(s8[4718592]{0:T(1024)(128)(4,1)} %bitcast.33), calls=%async_computation.6 | async-start | bytes 1048576
  485.9 8.3 %copy-start.8 = (bf16[384,1536]{1,0:T(8,128)(2,1)S(1)}, bf16[384,1536]{1,0:T(8,128)(2,1)}, u32[]{:S(2)}) copy-start(bf16[384,1536]{1,0:T(8,128)(2,1)} %get-tuple-element.71.refs_4_) | copy-start | bytes 3538948
  489.9 6.3 %copy-start.2 = (bf16[384,1536]{1,0:T(8,128)(2,1)S(1)}, bf16[384,1536]{1,0:T(8,128)(2,1)}, u32[]{:S(2)}) copy-start(bf16[384,1536]{1,0:T(8,128)(2,1)} %refs_6_.1) | copy-start | bytes 3538948
  489.9 6.3 %copy-start.7 = (bf16[8,4,48,1152]{3,2,1,0:T(8,128)(2,1)S(1)}, bf16[8,4,48,1152]{3,2,1,0:T(8,128)(2,1)}, u32[]{:S(2)}) copy-start(bf16[8,4,48,1152]{3,2,1,0:T(8,128)(2,1)} %get-tuple-element.49) | copy-start | bytes 10616836
  489.9 6.4 %copy-start.11 = (bf16[384,1024]{1,0:T(8,128)(2,1)S(1)}, bf16[384,1024]{1,0:T(8,128)(2,1)}, u32[]{:S(2)}) copy-start(bf16[384,1024]{1,0:T(8,128)(2,1)} %get-tuple-element.73.refs_5_) | copy-start | bytes 2359300
  489.9 6.4 %copy-start.15 = (f32[1536]{0:T(1024)S(1)}, f32[1536]{0:T(1024)}, u32[]{:S(2)}) copy-start(f32[1536]{0:T(1024)} %copy-done.14) | copy-start | bytes 18436
  489.9 6.4 %copy-start.19 = (f32[384]{0:T(512)S(1)}, f32[384]{0:T(512)}, u32[]{:S(2)}) copy-start(f32[384]{0:T(512)} %copy-done.18) | copy-start | bytes 4612
  489.9 26.5 %collective-permute-start.1 = (bf16[384,1536]{1,0:T(8,128)(2,1)}, bf16[384,1536]{1,0:T(8,128)(2,1)}, u32[]{:S(2)}, u32[]{:S(2)}) collective-permute-start(bf16[384,1536]{1,0:T(8,128)(2,1)} %get-tuple-element.98), channel_id=1, source_target_pairs={{0,1},{3,2},{4,5},{7,6},{8,9},{11,10},{12,13},{15,14},{16,17},{19,... | collective-permute-start | bytes 3538952 | tf_op jit(solution)/shard_map/ppermute | solution.py:1037
  492.5 125.3 %collective-permute-start = (bf16[384,1536]{1,0:T(8,128)(2,1)}, bf16[384,1536]{1,0:T(8,128)(2,1)}, u32[]{:S(2)}, u32[]{:S(2)}) collective-permute-start(bf16[384,1536]{1,0:T(8,128)(2,1)} %get-tuple-element.98), channel_id=1, source_target_pairs={{1,2},{2,1},{5,6},{6,5},{9,10},{10,9},{13,14},{14,13},{17,18},{18,... | collective-permute-start | bytes 3538952 | tf_op jit(solution)/shard_map/ppermute | solution.py:1037
  496.2 3.5 copy-start.20
  503.9 4.5 copy-start.16
  503.9 4.5 copy-start.17
  617.7 3.8 copy-start.6
  617.7 3.8 copy-start.9
  617.7 3.8 copy-start.10
  621.5 3.1 copy-start.13
  621.5 3.8 copy-start.12
Sparse Core Ops, SparseCore 0:
  9.9 59.7 all-gather.3
  106.8 42.2 all-gather.5
  150.9 42.2 all-gather.7
  395.3 118.4 reduce-scatter.1

commit v5 on v4

--- a/solution.py
+++ b/solution.py
@@ -193,27 +193,50 @@
 SUM_PARTS = ((0, 0, 768), (0, 768, 768), (1, 0, 768), (1, 768, 768), (2, 0, 1024))
 
 
-def sum_kernel(hops, *refs):
-    riders, parts = len(hops), len(SUM_PARTS) + 1
-    lefts, rights, ready, riding = refs[:3], refs[3:6], refs[6], refs[7 : 7 + riders]
-    refs = refs[7 + riders :]
-    outs, landed = refs[:4], refs[4 : 4 + riders]
-    refs = refs[4 + riders :]
+def sum_kernel(*refs):
+    parts = len(SUM_PARTS) + 1
+    lefts, rights = refs[:3], refs[3:6]
+    w_query, w_kv, tokens, gain_in, grad_hidden, gain_rows = refs[6:12]
+    home, outs, grad_tokens = refs[12], refs[13:17], refs[17]
+    near_hbm, two_hbm, met_hbm = refs[18:21]
+    refs = refs[21:]
     terms, got, plane1, plane2, lines = (refs[i * parts : (i + 1) * parts] for i in range(5))
-    load, send, recv, ride_send, ride_recv = refs[5 * parts :]
+    for_two, passed, load, send, recv, home_send, home_recv = refs[5 * parts :]
     dp, ctx = lax.axis_index("dp"), lax.axis_index("ctx")
+    middle = (ctx == 1) | (ctx == 2)
     chip = dp // 2
     core = dp - 2 * chip
     halves = (pl.ds(0, 2), pl.ds(2, 2))
     rows = lefts[0].shape[1]
 
-    def ride(i):
-        return remote(riding[i], landed[i], ride_send.at[i], ride_recv.at[i], dp, ctx ^ hops[i])
+    near = remote(home.at[ctx ^ 1], near_hbm, home_send.at[0], home_recv.at[0], dp, ctx ^ 1)
+    far = home.at[ctx ^ 3]
+    meet = remote(far, met_hbm, home_send.at[1], home_recv.at[1], dp, ctx ^ 3)
+    hand = remote(far, passed, home_send.at[1], home_recv.at[2], dp, ctx ^ 1)
+    fetch = pltpu.make_async_copy(home.at[ctx ^ 2], for_two, load)
+    two = remote(for_two, two_hbm, home_send.at[2], home_recv.at[3], dp, ctx ^ 2)
 
     def kept(k):
         return 2 * (chip ^ k) + core
 
-    fetch = pltpu.make_async_copy(ready, terms[-1], load)
+    def first_norm():
+        def tile(t, carry):
+            cols = pl.ds(pl.multiple_of(t * 256, 256), 256)
+            term = mdot(rights[1][...], w_query[cols, :], NT)
+            grad_tokens[:, cols] = term + mdot(rights[2][...], w_kv[cols, : 2 * KVH * HD], NT)
+            return carry
+
+        lax.fori_loop(0, rows // 256, tile, 0)
+        values, grad_upper = tokens[...].astype(f32), grad_tokens[...]
+        factor = lax.rsqrt(jnp.mean(values * values, axis=-1, keepdims=True) + EPSILON)
+        grad_lower, gain_terms = norm_back(grad_upper, values, factor, gain_in[...])
+        grad_tokens[...] = grad_hidden[...] + grad_lower
+        gain_row = jnp.sum(gain_terms, axis=0, keepdims=True)
+        which = lax.broadcasted_iota(jnp.int32, (128, rows), 0)
+        stacked = jnp.where(which == 0, gain_row, 0.0)
+        stacked = jnp.where(which == 1, gain_rows[0:1, :], stacked)
+        stacked = jnp.where(which == 2, gain_rows[1:2, :], stacked)
+        terms[-1][...] = jnp.transpose(stacked).astype(bf16).reshape(terms[-1].shape)
 
     def multiply(p):
         which, start, width = SUM_PARTS[p]
@@ -257,14 +280,20 @@
 
     fetch.start()
     greet(dp, ctx, (1, 2, 4), (1, 2, 3))
-    for i in range(riders):
-        ride(i).start()
+
+    @pl.when(middle)
+    def _():
+        meet.start()
+
+    @pl.when(jnp.logical_not(middle))
+    def _():
+        hand.start()
+
+    near.start()
 
     def begin(p):
         if p < parts - 1:
             multiply(p)
-        else:
-            fetch.wait()
         for k in (3, 1, 2, 0):
             across(p, k).start()
 
@@ -272,6 +301,16 @@
     for step in range(parts + 2):
         if step + 1 < parts:
             begin(step + 1)
+        if step == 1:
+            first_norm()
+            fetch.wait()
+
+            @pl.when(middle)
+            def _():
+                hand.wait_recv()
+                add(for_two, passed)
+
+            two.start()
         if step < parts:
             p = step
             for k in (3, 1, 2, 0):
@@ -322,41 +361,51 @@
             second(p, w).wait_send()
         for s in (1, 2, 3):
             line(p, s).wait_send()
-    for i in range(riders):
-        ride(i).wait()
-
-
-def sum_all(lefts, rights, ready, riding, hops, cid):
-    parts, riders = len(SUM_PARTS) + 1, len(riding)
+    near.wait()
+    two.wait()
+
+    @pl.when(middle)
+    def _():
+        meet.wait()
+
+    @pl.when(jnp.logical_not(middle))
+    def _():
+        hand.wait_send()
+
+
+def sum_all(lefts, rights, norm_in, home, cid):
+    parts = len(SUM_PARTS) + 1
     rows = lefts[0].shape[1]
     share = rows // 32
-    blocks = ready.reshape(8, 4, share, ready.shape[1])
-    widths = [width for _, _, width in SUM_PARTS] + [ready.shape[1]]
+    widths = [width for _, _, width in SUM_PARTS] + [128]
     vmem = pl.BlockSpec(memory_space=pltpu.VMEM)
 
     def per(*lead):
         return [pltpu.VMEM(lead + (share, width), bf16) for width in widths]
 
     return pl.pallas_call(
-        functools.partial(sum_kernel, hops),
-        in_specs=[vmem] * 6 + [ANY] * (1 + riders),
-        out_specs=[vmem] * 4 + [ANY] * riders,
+        sum_kernel,
+        in_specs=[vmem] * 12 + [ANY],
+        out_specs=[vmem] * 5 + [ANY] * 3,
         out_shape=[jax.ShapeDtypeStruct((share, r.shape[1]), f32) for r in rights]
-        + [jax.ShapeDtypeStruct((share, ready.shape[1]), f32)]
-        + [jax.ShapeDtypeStruct(r.shape, r.dtype) for r in riding],
+        + [jax.ShapeDtypeStruct((share, 128), f32)]
+        + [jax.ShapeDtypeStruct(lefts[0].shape, f32)]
+        + [jax.ShapeDtypeStruct(home.shape[1:], bf16)] * 3,
         scratch_shapes=per(8, 4) + per(4, 4) + per(2, 4) + per(4) + per(3)
         + [
+            pltpu.VMEM(home.shape[1:], bf16),
+            pltpu.VMEM(home.shape[1:], bf16),
             pltpu.SemaphoreType.DMA,
             pltpu.SemaphoreType.DMA((parts, 13)),
             pltpu.SemaphoreType.DMA((parts, 13)),
-            pltpu.SemaphoreType.DMA((riders,)),
-            pltpu.SemaphoreType.DMA((riders,)),
+            pltpu.SemaphoreType.DMA((3,)),
+            pltpu.SemaphoreType.DMA((4,)),
         ],
         compiler_params=pltpu.CompilerParams(
-            collective_id=cid, has_side_effects=True, vmem_limit_bytes=56 * 2**20
+            collective_id=cid, has_side_effects=True, vmem_limit_bytes=60 * 2**20
         ),
         name="sum_all",
-    )(*lefts, *rights, blocks, *riding)
+    )(*lefts, *rights, *norm_in, home)
 
 
 def causal_mask(rows, limit, key_axis):
@@ -1053,13 +1102,25 @@
         full = [lax.all_gather(b, every, axis=0, tiled=True) for b in blocks]
         return full + [swap(b, r) for b, r in zip(riding, hops)]
 
-    def collect(lefts, rights, ready, riding, hops, cid):
+    def collect(lefts, rights, norm_in, home, cid):
         if small:
-            return sum_all(lefts, rights, ready, riding, hops, cid)
-        terms = [mdot(a, b, TN).astype(bf16) for a, b in zip(lefts, rights)] + [ready]
-        return [
+            return sum_all(lefts, rights, norm_in, home, cid)
+        query_weight, kv_weight, _, gain_vec, grad_above, gain_rows = norm_in
+        upper = mdot(rights[1], query_weight, NT)
+        upper += mdot(rights[2], kv_weight[:, : 2 * KVH * HD], NT)
+        factor = rms_scale(inputs, gain_vec)[1]
+        lower, gain_terms = norm_back(upper, inputs, factor, gain_vec)
+        columns = jnp.concatenate([jnp.sum(gain_terms, axis=0, keepdims=True), gain_rows], 0).T
+        columns = jnp.pad(columns, ((0, 0), (0, 125))).astype(bf16)
+        terms = [mdot(a, b, TN).astype(bf16) for a, b in zip(lefts, rights)] + [columns]
+        sums = [
             lax.psum_scatter(t, every, scatter_dimension=0, tiled=True).astype(f32) for t in terms
-        ] + [swap(block, r) for block, r in zip(riding, hops)]
+        ]
+        far = home[mine ^ 3]
+        passed = move(far, [(0, 1), (3, 2)])
+        two = (home[mine ^ 2].astype(f32) + passed.astype(f32)).astype(bf16)
+        landed = [swap(home[mine ^ 1], 1), swap(two, 2), move(far, [(1, 2), (2, 1)])]
+        return sums + [grad_above + lower] + landed
 
     extra = jnp.stack([gain_in, gain_mid, jnp.pad(qk_gains, (0, share - qk_share))], 1)
     extra = jnp.pad(extra, ((0, 0), (0, 125)))
@@ -1130,29 +1191,18 @@
         pair_gains,
         5,
     )
-    later = after(down_parts, grad_query_low)
-    for_far, for_two, for_near = (later[mine ^ r] for r in (3, 2, 1))
-    passed = move(for_far, [(0, 1), (3, 2)])
-    down_terms = [later[mine], move(for_far, [(1, 2), (2, 1)])]
-    for_two = (for_two.astype(f32) + passed.astype(f32)).astype(bf16)
-    grad_normed = mdot(grad_query_low, full_query, NT) + mdot(grad_kv_low, full_kv, NT)
-    grad_input_norm, gain_terms_in = norm_back(grad_normed, inputs, factor_in, full_gain_in)
-    grad_tokens = grad_hidden + grad_input_norm
     grad_qk = (gain_rows[:, :HD] + gain_rows[:, HD:]).reshape(-1)
-    qk_column = jnp.pad(grad_qk.reshape(world, qk_share), ((0, 0), (0, share - qk_share)))
-    grad_extra = jnp.stack(
-        [jnp.sum(gain_terms_in, axis=0), jnp.sum(gain_terms_mid, axis=0), qk_column.reshape(-1)], 1
-    )
-    grad_extra = jnp.pad(grad_extra, ((0, 0), (0, 125))).astype(bf16)
-    grad_wout, sum_query, sum_kv, sum_extra, *landed = collect(
+    qk_row = jnp.pad(grad_qk.reshape(world, qk_share), ((0, 0), (0, share - qk_share)))
+    other_gains = jnp.stack([jnp.sum(gain_terms_mid, axis=0), qk_row.reshape(-1)])
+    grad_wout, sum_query, sum_kv, sum_extra, grad_tokens, *down_terms = collect(
         (grad_branch, normed, normed),
         (mixed_low, grad_query_low, grad_kv_low),
-        grad_extra,
-        [for_two, for_near],
-        (2, 1),
+        (full_query, wide_kv, tokens, full_gain_in[None], grad_hidden, other_gains),
+        down_parts,
         4,
     )
-    down_terms += landed
+    inner = (mine == 1) | (mine == 2)
+    down_terms = [down_parts[mine], *down_terms[:2], jnp.where(inner, down_terms[2], 0)]
     grad_ffn, down_terms = after((grad_ffn, down_terms), sum_kv)
     output = (hidden + sum(t.astype(f32) for t in down_terms)).astype(bf16)
     grad_wgate, grad_wup, grad_wdown = (

time: 642 us -> 637 us (level)
  Pallas kernels: 522 us -> 552 us
  other arithmetic: 28.7 us -> 21.1 us
  waiting for transfers between devices: 35.4 us -> 28.5 us
    pallas_call x1, Pallas kernels: 93.8 us -> 124 us  [sum_all(): pl.pallas_call(sum_kernel, in_specs=[vmem] * 12 + [ANY], out_specs=[vmem]...]
    ppermute x2 -> x0, waiting for transfers between devices: 6.89 us -> none  [move(): return lax.ppermute(block, 'ctx', pairs)]
  transfers between devices with their start and end apart: 6 -> 4, of which waited for: 2 -> 1; matrix products, arithmetic and copies ran while one was open for 7% -> 4% of each run, Pallas kernels for 51% -> 55%
where the time goes in v5:
time: 637 us; the launch traced here: 634 us
  Pallas kernels  552 us (87%)
  waiting for transfers between devices  28.5 us (4%)
  other arithmetic  21.1 us (3%)
  between operations  14.8 us (2%)
  local copies, waits for them, and re-layouts  13.9 us (2%)
    pallas_call x1, Pallas kernels, feed_forward(): pl.pallas_call(functools.partial(feed_forward_kernel, dp_blocks), in_spec...  202 us
    pallas_call x1, Pallas kernels, sum_all(): pl.pallas_call(sum_kernel, in_specs=[vmem] * 12 + [ANY], out_specs=[vmem]...  124 us
    pallas_call x1, Pallas kernels, gather_all(): pl.pallas_call(functools.partial(gather_kernel, parts, hops), in_specs=[A...  92.5 us
    pallas_call x1, Pallas kernels, attn_backward(): pl.pallas_call(functools.partial(attn_bwd_kernel, blocks), grid=(PAIRS,),...  81.9 us
    pallas_call x1, Pallas kernels, attn_forward(): pl.pallas_call(attn_fwd_kernel, in_specs=[pl.BlockSpec(memory_space=pltpu...  51.5 us
    all_gather x1, waiting for transfers between devices, shards(): lax.all_gather(after(w_down.T, full_kv, full_gate), 'dp', axis=0, tiled=T...  27.1 us
  transfers between devices with their start and end apart: 4, of which 1 were waited for; matrix products, arithmetic and copies ran while one was open for 4% of the time, Pallas kernels for 55%

profile of v5, /device:TPU:0, one launch (start us, length us, event | category | flops | bytes accessed | tf_op | source)
XLA Modules:
  0.0 633.7 jit_solution(10348479561115777108)
XLA Ops:
  7.2 0.7 all-gather.4.cloned.1.call-update
  8.6 0.7 pad_bitcast_fusion
  9.3 0.7 pad_maximum_fusion.2
  10.1 1.5 fusion.5.refs_0_
  11.5 2.5 fusion.3.refs_3_.refs_4_.refs_10_
  14.1 92.5 %gather_all.1 = (bf16[8,4,48,1152]{3,2,1,0:T(8,128)(2,1)}, bf16[8,4,48,1536]{3,2,1,0:T(8,128)(2,1)}, bf16[8,4,48,1536]{3,2,1,0:T(8,128)(2,1)}, bf16[384,1536]{1,0:T(8,128)(2,1)}, bf16[384,1536]{1,0:T(8,128)(2,1)}) custom-call(bf16[48,1152]{1,0:T(8,128)(2,1)} %fusion.5.refs_0_, bf16[48,1536]{1,0:T(8,128)(2,1)} %refs_1_.1, bf16[48,1536]{1,0:T(8,128)(2,1)} %bitcast.32, ...), custom_call_target="tpu_custom_call" | custom-call | tf_op jit(solution)/shard_map/gather_all/pallas_call | solution.py:173
  106.7 0.7 all-gather.8.cloned.1.call-update
  107.4 1.0 slice_convert_fusion.2
  108.5 1.1 slice_reduce_fusion
  111.3 0.8 multiply_sine_fusion
  112.1 1.1 pad_maximum_fusion
  113.2 1.4 fusion.2.refs_1_.refs_2_
  114.6 51.5 %attn_forward.1 = (bf16[384,1536]{1,0:T(8,128)(2,1)}, bf16[384,1536]{1,0:T(8,128)(2,1)}, f32[4,8,384]{2,1,0:T(8,128)}, f32[384,1536]{1,0:T(8,128)}, f32[384,512]...) custom-call(s32[1]{0:T(128)} %copy.35.refs_0_.length_ref, ...), custom_call_target="tpu_custom_call" | custom-call | tf_op jit(solution)/shard_map/attn_forward/pallas_call | solution.py:637
  166.1 27.1 %all-gather.8.cloned.1.call-done.refs_3_ = bf16[1536,1728]{1,0:T(8,128)(2,1)} async-done(((bf16[192,1728]{1,0:T(8,128)(2,1)}), bf16[1536,1728]{1,0:T(8,128)(2,1)}) %all-gather.8.cloned.1.call-update) | async-done | bytes 5308432 | tf_op jit(solution)/shard_map/all_gather | solution.py:1142
  193.2 201.9 %feed_forward.1 = (f32[384,1536]{1,0:T(8,128)}, bf16[4,384,1536]{2,1,0:T(8,128)(2,1)}, bf16[8,3,192,1728]{3,2,1,0:T(8,128)(2,1)}) custom-call(bf16[384,1536]{1,0:T(8,128)(2,1)} %get-tuple-element.55.refs_0_, bf16[1536,1728]{1,0:T(8,128)(2,1)} %all-gather.4.cloned.1.call-done.refs_1_, bf16[1536,1728]{1,0:T(8,128)(2,1)} %all-gather.6.cloned.1.call-done.refs_2_, ...), custom_call_target="tpu_custom_call" | custom-call | tf_op jit(solution)/shard_map/feed_forward/pallas_call | solution.py:1029
  395.7 1.0 copy-done
  397.6 0.7 multiply_reduce_fusion
  398.3 2.2 fusion.9
  400.6 3.0 convolution_convert_fusion.refs_4_
  403.6 81.9 %attn_backward.1 = (bf16[384,1536]{1,0:T(8,128)(2,1)}, bf16[384,1024]{1,0:T(8,128)(2,1)}, f32[2,128]{1,0:T(2,128)}) custom-call(s32[1]{0:T(128)} %copy.35.refs_0_.length_ref, bf16[384,1536]{1,0:T(8,128)(2,1)} %get-tuple-element.64.q_ref, bf16[2,384,512]{2,1,0:T(8,128)(2,1)} %get-tuple-element.65.refs_0_, bf16[2,384,512]{2,1,0:T(8,128)(2,1)} %get-tuple-element.66.refs_1_, ...), custom_call_target="tpu_custom_call" | custom-call | flops 120000004096 | tf_op jit(solution)/shard_map/attn_backward/pallas_call | solution.py:821
  485.5 0.8 slice_add_fusion
  487.1 124.4 %sum_all.1 = (f32[48,1536]{1,0:T(8,128)}, f32[48,1536]{1,0:T(8,128)}, f32[48,1024]{1,0:T(8,128)}, f32[48,128]{1,0:T(8,128)}, f32[384,1536]{1,0:T(8,128)}, /*inde...) custom-call(bf16[384,1536]{1,0:T(8,128)(2,1)} %copy-done.5, ...), custom_call_target="tpu_custom_call" | custom-call | tf_op jit(solution)/shard_map/sum_all/pallas_call | solution.py:386
  611.5 1.5 slice_reduce_fusion.5
  612.9 1.5 slice_reduce_fusion.3
  614.4 1.6 fusion.10
  616.1 1.3 dynamic-slice_bitcast_fusion
  617.4 1.1 broadcast_select_fusion
  618.5 3.7 convert_bitcast_fusion
  622.3 1.8 add_convert_fusion
  624.1 1.4 copy.36
  625.5 0.7 copy.37
  626.2 0.7 copy.38
  (57 shorter events, 4.4 us)
Async XLA Ops:
  7.2 99.4 %all-gather.4.cloned.1.call-start = ((), (), s32[]{:S(2)}) async-start(), calls=%async_computation.1 | async-start | bytes 6193152 | tf_op jit(solution)/shard_map/all_gather | solution.py:1140
  7.9 158.2 %all-gather.6.cloned.1.call-start = ((), (), s32[]{:S(2)}) async-start(), calls=%async_computation.2 | async-start | bytes 6193152 | tf_op jit(solution)/shard_map/all_gather | solution.py:1141
  106.6 4.4 copy-start.1
  106.6 86.5 %all-gather.8.cloned.1.call-start = ((), (), s32[]{:S(2)}) async-start(), calls=%async_computation.3 | async-start | bytes 6193152 | tf_op jit(solution)/shard_map/all_gather | solution.py:1142
  107.4 511.2 %reduce-scatter.2.cloned.1.call-start = ((), (), s32[]{:S(2)}) async-start(), calls=%async_computation.4 | async-start | bytes 18579456 | tf_op jit(solution)/shard_map/reduce_scatter | solution.py:1173
  395.1 1.7 copy-start
  395.7 1.9 copy-start.2
  396.8 1.5 copy-start.4
  397.6 2.9 slice-start
  398.3 2.2 slice-start.1
  400.5 3.0 copy-start.5
  611.5 6.0 copy-start.7
  618.5 3.8 copy-start.3
  618.5 3.8 copy-start.8
  618.5 3.8 copy-start.9
  622.3 1.8 copy-start.6
  624.1 1.4 copy-start.11
  624.1 2.1 copy-start.10
Sparse Core Ops, SparseCore 0:
  9.9 59.7 all-gather.3
  106.8 42.2 all-gather.5
  150.9 42.2 all-gather.7
  395.3 128.5 reduce-scatter.1
